TPU v7x, 32 devices: a whole 2x2x4 slice. The times are simulated.
32 devices in a mesh: wide: 8 (over z, x), narrow: 4 (over y, core).
Axes of the slice: x: 2, y: 2, z: 4, core: 2. Of those that a mesh axis runs over, the one named last changes fastest.
Arguments:
- dosage: bfloat16 [32768, 4096], P(('wide', 'narrow')), may hold values from 0 to 2
- keep_rows: int32 [28672], P(('wide', 'narrow')), may hold values from 0 to 1023, as said below
- allele_counts: int32 [4096], replicated, may hold values from 19660 to 45874, as said below
- projection: bfloat16 [4096, 128], replicated, may hold values from -0.09375 to 0.09375
Outputs:
- scores: float32 [28672, 128], P(('wide', 'narrow'))
- loadings: float32 [4096, 128], P('narrow')
Inputs may be any that keep to these rules, and one draw needn't show every extreme that they name: `keep_rows`: each block of 896 entries holds distinct local row numbers of one device's 1024 samples, ascending. `allele_counts`: totals over all 32768 genotyped samples, before outlier removal.
All inputs are finite; a program needn't handle non-finite values.
Results may differ from a plain program's by a relative error of at most 0.0075.
The roundings to bfloat16 on the way count: a program that leaves them out, or rounds other values in their place, can miss the bound.
Values sent between devices are 32-bit elements; how exact they have to be, the bound alone decides.
No kernel may reach another device: no remote copies, remote signals or barrier semaphores. Data moves between devices by JAX's collectives and lax.ppermute only.
A program may use at most 64 MiB of HBM per device.

v0:
```python
import math

import jax
import jax.numpy as jnp
from jax import lax
from jax.sharding import PartitionSpec as P

ITERS = 2


def transposed_product(left_side, right_side):
    return lax.dot_general(
        left_side, right_side, (((0,), (0,)), ((), ())), preferred_element_type=jnp.float32
    )


def invert_factor(gram_matrix):
    lower_factor = jnp.linalg.cholesky(gram_matrix)
    unit_matrix = jnp.eye(gram_matrix.shape[0], dtype=jnp.float32)
    return jax.scipy.linalg.solve_triangular(lower_factor, unit_matrix, lower=True)


def on_device(dosage, keep_rows, allele_counts, projection):
    groups = lax.axis_size("wide") * lax.axis_size("narrow")
    samples_total = dosage.shape[0] * groups
    kept_total = keep_rows.shape[0] * groups
    snp_count = dosage.shape[1]
    narrow_size = lax.axis_size("narrow")
    share_rows = snp_count // narrow_size
    position = lax.axis_index("narrow")
    frequency = allele_counts.astype(jnp.float32) / (2.0 * samples_total)
    center = 2.0 * frequency
    spread = jnp.sqrt(2.0 * frequency * (1.0 - frequency))
    chosen = jnp.take(dosage, keep_rows, axis=0)
    standard = ((chosen.astype(jnp.float32) - center) / spread).astype(jnp.bfloat16)
    projected = jnp.dot(standard, projection, preferred_element_type=jnp.float32).astype(
        jnp.bfloat16
    )
    inverse = None
    loadings = None
    for iteration in range(ITERS):
        last_turn = iteration + 1 == ITERS
        gram_matrix = None
        gram_matrix = lax.psum(transposed_product(projected, projected), ("wide", "narrow"))
        totals = lax.psum(transposed_product(standard, projected), ("wide", "narrow"))
        inverse = invert_factor(gram_matrix)
        loadings_all = jnp.dot(totals, inverse.T, precision=lax.Precision.HIGHEST)
        if last_turn:
            loadings = lax.dynamic_slice_in_dim(loadings_all, position * share_rows, share_rows, 0)
        else:
            projected = jnp.dot(
                standard, loadings_all.astype(jnp.bfloat16), preferred_element_type=jnp.float32
            ).astype(jnp.bfloat16)
    scores = jnp.dot(
        projected.astype(jnp.float32), inverse.T, precision=lax.Precision.HIGHEST
    ) * math.sqrt(kept_total)
    return (scores, loadings)


def solution(mesh):
    in_specs = (P(("wide", "narrow"), None), P(("wide", "narrow")), P(), P())
    out_specs = (P(("wide", "narrow"), None), P("narrow", None))
    return jax.shard_map(
        on_device, mesh=mesh, in_specs=in_specs, out_specs=out_specs, check_vma=False
    )
```

profile of v0, /device:TPU:0, one launch (start us, length us, event | category | flops | bytes accessed | tf_op | source)
XLA Modules:
  0.0 389.7 jit_solution(3513980681995114010)
XLA Ops:
  7.2 0.8 compare_select_fusion
  8.7 0.7 convert_multiply_fusion
  9.4 19.5 %gather_fusion = bf16[896,4096]{1,0:T(8,128)(2,1)} fusion(bf16[1024,4096]{1,0:T(8,128)(2,1)} %param.7, s32[1024]{0:T(1024)S(1)} %pad_clamp_fusion), kind=kCustom, calls=%fused_computation | custom fusion | bytes 14683648 | tf_op jit(solution)/shard_map/jit(_take)/gather | solution.py:34
  28.9 6.6 %divide_convert_fusion = bf16[896,4096]{1,0:T(8,128)(2,1)S(1)} fusion(f32[4096]{0:T(1024)S(1)} %get-tuple-element.9, f32[4096]{0:T(1024)S(1)} %get-tuple-element.8, bf16[896,4096]{1,0:T(8,128)(2,1)} %gather_fusion, pred[896]{0:T(1024)(128)(4,1)S(1)} %compare_and_fusion), kind=kLoop, calls=%fused_computation.1 | loop fusion | flops 18350080 | bytes 14713728 | tf_op jit(solution)/shard_map/convert_element_type | solution.py:35
  35.5 2.1 convolution_convert_fusion.2
  37.6 3.5 fusion.10
  41.1 0.9 fusion.11
  42.3 137.4 %all-reduce.7.cloned.1.call-done = (f32[4096,128]{1,0:T(8,128)}, f32[128,128]{0,1:T(8,128)}) async-done(((f32[4096,128]{1,0:T(8,128)}, f32[128,128]{0,1:T(8,128)}), (f32[4096,128]{1,0:T(8,128)}, f32[128,128]{0,1:T(8,128)})) %all-reduce.7.cloned.1.call-update) | async-done | bytes 2162704 | tf_op jit(solution)/shard_map/psum | solution.py:45
  179.7 0.9 copy.7
  180.6 0.9 fusion.9
  181.5 11.7 %cholesky.44 = f32[128,128]{1,0:T(8,128)S(1)} custom-call(f32[128,128]{1,0:T(8,128)S(1)} %fusion.9), custom_call_target="Cholesky" | custom-call | tf_op jit(solution)/shard_map/jit(cholesky)/cholesky | solution.py:18
  194.6 9.8 %custom-call.6 = f32[1,128,128]{1,2,0:T(8,128)S(1)} custom-call(f32[1,128,128]{2,1,0:T(8,128)S(1)} %fusion.4), custom_call_target="InvertDiagBlocksLowerTriangular" | custom-call | tf_op jit(solution)/shard_map/jit(_solve_triangular)/triangular_solve | solution.py:20
  204.7 3.5 convolution_convert_fusion
  208.2 5.3 %convolution_convert_fusion.1 = bf16[896,128]{1,0:T(8,128)(2,1)S(1)} fusion(bf16[896,4096]{1,0:T(8,128)(2,1)} %copy-done.1, bf16[4096,128]{1,0:T(8,128)(2,1)S(1)} %convolution_convert_fusion), kind=kOutput, calls=%fused_computation.4 | convolution fusion | flops 939638784 | bytes 8617984 | tf_op jit(solution)/shard_map/dot_general | solution.py:51
  213.6 3.5 fusion.13
  217.1 0.9 fusion.12
  218.0 134.2 %all-reduce.5.cloned.1.call-done = (f32[128,128]{0,1:T(8,128)}, f32[4096,128]{1,0:T(8,128)}) async-done(((f32[128,128]{0,1:T(8,128)}, f32[4096,128]{1,0:T(8,128)}), (f32[128,128]{0,1:T(8,128)}, f32[4096,128]{1,0:T(8,128)})) %all-reduce.5.cloned.1.call-update) | async-done | bytes 2162704 | tf_op jit(solution)/shard_map/psum | solution.py:44
  352.2 1.1 copy.9
  353.4 0.9 fusion.7
  354.2 11.7 %cholesky.55 = f32[128,128]{1,0:T(8,128)S(1)} custom-call(f32[128,128]{1,0:T(8,128)S(1)} %fusion.7), custom_call_target="Cholesky" | custom-call | tf_op jit(solution)/shard_map/jit(cholesky)/cholesky | solution.py:18
  367.3 9.8 %custom-call.7 = f32[1,128,128]{1,2,0:T(8,128)S(1)} custom-call(f32[1,128,128]{2,1,0:T(8,128)S(1)} %fusion.5), custom_call_target="InvertDiagBlocksLowerTriangular" | custom-call | tf_op jit(solution)/shard_map/jit(_solve_triangular)/triangular_solve | solution.py:20
  377.4 1.1 convolution_multiply_fusion
  378.5 3.5 fusion.14
  382.0 0.8 constant_dynamic-slice_fusion
  (23 shorter events, 4.3 us)
Async XLA Ops:
  7.2 28.3 %copy-start = (bf16[4096,128]{1,0:T(8,128)(2,1)S(1)}, bf16[4096,128]{1,0:T(8,128)(2,1)}, u32[]{:S(2)}) copy-start(bf16[4096,128]{1,0:T(8,128)(2,1)} %param.10) | copy-start | bytes 3145732
  7.2 172.5 %all-reduce.7.cloned.1.call-start = ((), (), s32[]{:S(2)}) async-start(), calls=%async_computation.1 | async-start | bytes 4325376 | tf_op jit(solution)/shard_map/psum | solution.py:45
  35.5 5.6 %copy-start.1 = (bf16[896,4096]{1,0:T(8,128)(2,1)}, bf16[896,4096]{1,0:T(8,128)(2,1)S(1)}, u32[]{:S(2)}) copy-start(bf16[896,4096]{1,0:T(8,128)(2,1)S(1)} %divide_convert_fusion) | copy-start | bytes 22020100
  42.0 310.2 %all-reduce.5.cloned.1.call-start = ((), (), s32[]{:S(2)}) async-start(), calls=%async_computation | async-start | bytes 4325376 | tf_op jit(solution)/shard_map/psum | solution.py:44
  204.7 8.9 %slice-start = ((s8[7340032]{0:T(1024)(128)(4,1)}), s8[4194304]{0:T(1024)(128)(4,1)S(1)}, s32[]{:S(2)}) async-start(s8[7340032]{0:T(1024)(128)(4,1)} %bitcast.36), calls=%async_computation.2 | async-start | bytes 8388608
  208.2 5.3 %slice-start.1 = ((s8[7340032]{0:T(1024)(128)(4,1)}), s8[3145728]{0:T(1024)(128)(4,1)S(1)}, s32[]{:S(2)}) async-start(s8[7340032]{0:T(1024)(128)(4,1)} %bitcast.36), calls=%async_computation.3 | async-start | bytes 6291456
Sparse Core Ops, SparseCore 0:
  42.1 137.5 all-reduce.6
  218.1 134.0 all-reduce.4
where the time goes:
time: 390 us
  waiting for transfers between devices  272 us (70%)
  other arithmetic  56.2 us (14%)
  matrix products  24.9 us (6%)
  local copies, waits for them, and re-layouts  22.4 us (6%)
  between operations  14.2 us (4%)
    psum x1, waiting for transfers between devices, on_device(): lax.psum(transposed_product(standard, projected), ('wide', 'narrow'))  137 us
    psum x1, waiting for transfers between devices, on_device(): lax.psum(transposed_product(projected, projected), ('wide', 'narrow'))  134 us
    another operation x6, other arithmetic, invert_factor(): lower_factor = jnp.linalg.cholesky(gram_matrix)  24.8 us
    another operation x4, other arithmetic, invert_factor(): jax.scipy.linalg.solve_triangular(lower_factor, unit_matrix, lower=True)  20.9 us
    gather x1, local copies, waits for them, and re-layouts, on_device(): chosen = jnp.take(dosage, keep_rows, axis=0)  19.5 us
    dot_general x4, matrix products, transposed_product(): lax.dot_general(left_side, right_side, (((0,), (0,)), ((), ())), preferre...  8.83 us
  transfers between devices with their start and end apart: 2, of which 2 were waited for; matrix products, arithmetic and copies ran while one was open for 0% of the time, Pallas kernels for 0%

commit v1 on v0

v1 whole, which is shorter than its diff:
```python
import functools
import math

import jax
import jax.numpy as jnp
from jax import lax
from jax.experimental import pallas as pl
from jax.experimental.pallas import tpu as pltpu
from jax.sharding import PartitionSpec as P

AXES = ("wide", "narrow")
TILE = 128
BLOCKS = 32
ROWS = 256
VMEM = 48 * 1024 * 1024


def split(value):
    high = value.astype(jnp.bfloat16)
    low = (value - high.astype(jnp.float32)).astype(jnp.bfloat16)
    return high, low


def product(left, right_high, right_low):
    high, low = split(left)
    dims = (((1,), (1,)), ((), ()))
    dot = functools.partial(lax.dot_general, dimension_numbers=dims, preferred_element_type=jnp.float32)
    return dot(high, right_high) + (dot(high, right_low) + dot(low, right_high))


def relative(position, core):
    first = (position >> 3) & 1
    second = (position >> 2) & 1
    core_bit = (position >> 4) & 1
    target = core ^ core_bit
    bit_x = jnp.where(target == 0, first, second)
    bit_y = jnp.where(target == 0, second, first)
    return core_bit | (bit_y << 1) | (bit_x << 2) | ((position & 3) << 3)


def block_order(device):
    position = lax.iota(jnp.int32, BLOCKS)
    owner = device ^ relative(position, device & 1)
    return (owner & 3) * 8 + ((owner >> 2) & 7)


def exchange(value, mask_of):
    count = lax.axis_size(AXES)
    return lax.ppermute(value, AXES, [(d, d ^ mask_of(d)) for d in range(count)])


def core_mask(d):
    return 1


def first_mask(d):
    return 2 if d & 1 else 4


def second_mask(d):
    return 4 if d & 1 else 2


def standard_kernel(samples_total, order, dosage, keep, counts, projection, standard, projected, turned, gram, kept, table, basis):
    step = pl.program_id(0)

    @pl.when(step == 0)
    def _():
        frequency = counts[...].astype(jnp.float32) / (2.0 * samples_total)
        table[0] = 2.0 * frequency
        table[1] = 1.0 / jnp.sqrt(2.0 * frequency * (1.0 - frequency))
        for p in range(BLOCKS):
            start = pl.multiple_of(order[p] * TILE, TILE)
            basis[p * TILE : (p + 1) * TILE, :] = projection[pl.ds(start, TILE), :]
        gram[...] = jnp.zeros_like(gram)

    rows = lax.broadcasted_iota(jnp.int32, (ROWS, TILE), 0) + step * ROWS
    found = jnp.zeros((ROWS, TILE), jnp.float32)
    for j in range(keep.shape[0]):
        found = jnp.where(rows == keep[j : j + 1, :], 1.0, found)
    found = jnp.broadcast_to(jnp.max(found, axis=1, keepdims=True), (ROWS, TILE))
    kept[...] = found
    for p in range(BLOCKS):
        block = order[p]
        center = table[0, pl.ds(block, 1), :]
        scale = table[1, pl.ds(block, 1), :]
        value = dosage[:, pl.ds(pl.multiple_of(block * TILE, TILE), TILE)].astype(jnp.float32)
        standard[:, p * TILE : (p + 1) * TILE] = ((value - center) * scale).astype(jnp.bfloat16)
    value = jnp.dot(standard[...], basis[...], preferred_element_type=jnp.float32)
    value = jnp.where(found > 0.0, value, 0.0)
    low = value.astype(jnp.bfloat16)
    low_turned = value.T.astype(jnp.bfloat16)
    projected[...] = low
    turned[...] = low_turned
    gram[...] += jnp.dot(low_turned, low, preferred_element_type=jnp.float32)


def standardize(samples_total, order, dosage, keep, counts, projection):
    samples, snps = dosage.shape
    steps = samples // ROWS
    return pl.pallas_call(
        functools.partial(standard_kernel, samples_total),
        grid_spec=pltpu.PrefetchScalarGridSpec(
            num_scalar_prefetch=1,
            grid=(steps,),
            in_specs=[
                pl.BlockSpec((ROWS, snps), lambda i, order: (i, 0)),
                pl.BlockSpec(keep.shape, lambda i, order: (0, 0)),
                pl.BlockSpec(counts.shape, lambda i, order: (0, 0)),
                pl.BlockSpec(projection.shape, lambda i, order: (0, 0)),
            ],
            out_specs=[
                pl.BlockSpec((ROWS, snps), lambda i, order: (i, 0)),
                pl.BlockSpec((ROWS, TILE), lambda i, order: (i, 0)),
                pl.BlockSpec((TILE, ROWS), lambda i, order: (0, i)),
                pl.BlockSpec((TILE, TILE), lambda i, order: (0, 0)),
                pl.BlockSpec((ROWS, TILE), lambda i, order: (i, 0)),
            ],
            scratch_shapes=[
                pltpu.VMEM((2,) + counts.shape, jnp.float32),
                pltpu.VMEM(projection.shape, jnp.bfloat16),
            ],
        ),
        out_shape=[
            jax.ShapeDtypeStruct((samples, snps), jnp.bfloat16),
            jax.ShapeDtypeStruct((samples, TILE), jnp.bfloat16),
            jax.ShapeDtypeStruct((TILE, samples), jnp.bfloat16),
            jax.ShapeDtypeStruct((TILE, TILE), jnp.float32),
            jax.ShapeDtypeStruct((samples, TILE), jnp.float32),
        ],
        compiler_params=pltpu.CompilerParams(vmem_limit_bytes=VMEM),
        cost_estimate=pl.CostEstimate(flops=2 * samples * snps * TILE, bytes_accessed=4 * samples * snps, transcendentals=0),
        name="standardize",
    )(order, dosage, keep, counts, projection)


WIDTH = 512


def totals_kernel(turned, standard, out):
    out[...] = jnp.dot(turned[...], standard[...], preferred_element_type=jnp.float32).T


def totals(turned, standard, low, high):
    samples = standard.shape[0]
    base = low * TILE // WIDTH
    count = (high - low) * TILE
    return pl.pallas_call(
        totals_kernel,
        grid=(count // WIDTH,),
        in_specs=[
            pl.BlockSpec((TILE, samples), lambda i: (0, 0)),
            pl.BlockSpec((samples, WIDTH), lambda i: (0, base + i)),
        ],
        out_specs=pl.BlockSpec((WIDTH, TILE), lambda i: (i, 0)),
        out_shape=jax.ShapeDtypeStruct((count, TILE), jnp.float32),
        compiler_params=pltpu.CompilerParams(vmem_limit_bytes=VMEM),
        cost_estimate=pl.CostEstimate(flops=2 * samples * count * TILE, bytes_accessed=2 * samples * count, transcendentals=0),
        name="totals",
    )(turned, standard)


def project_kernel(pieces, *refs):
    parts = refs[:pieces]
    inverse, standard, kept, projected, turned, gram, basis = refs[pieces:]

    @pl.when(pl.program_id(0) == 0)
    def _():
        high, low = split(inverse[...])
        start = 0
        for part in parts:
            size = part.shape[0]
            basis[start : start + size, :] = product(part[...], high, low).astype(jnp.bfloat16)
            start += size
        gram[...] = jnp.zeros_like(gram)

    value = jnp.dot(standard[...], basis[...], preferred_element_type=jnp.float32)
    value = jnp.where(kept[...] > 0.0, value, 0.0)
    low = value.astype(jnp.bfloat16)
    low_turned = value.T.astype(jnp.bfloat16)
    projected[...] = low
    turned[...] = low_turned
    gram[...] += jnp.dot(low_turned, low, preferred_element_type=jnp.float32)


def project(parts, inverse, standard, kept):
    samples, snps = standard.shape
    return pl.pallas_call(
        functools.partial(project_kernel, len(parts)),
        grid=(samples // ROWS,),
        in_specs=[pl.BlockSpec(part.shape, lambda i: (0, 0)) for part in parts]
        + [
            pl.BlockSpec((TILE, TILE), lambda i: (0, 0)),
            pl.BlockSpec((ROWS, snps), lambda i: (i, 0)),
            pl.BlockSpec((ROWS, TILE), lambda i: (i, 0)),
        ],
        out_specs=[
            pl.BlockSpec((ROWS, TILE), lambda i: (i, 0)),
            pl.BlockSpec((TILE, ROWS), lambda i: (0, i)),
            pl.BlockSpec((TILE, TILE), lambda i: (0, 0)),
        ],
        out_shape=[
            jax.ShapeDtypeStruct((samples, TILE), jnp.bfloat16),
            jax.ShapeDtypeStruct((TILE, samples), jnp.bfloat16),
            jax.ShapeDtypeStruct((TILE, TILE), jnp.float32),
        ],
        scratch_shapes=[pltpu.VMEM((snps, TILE), jnp.bfloat16)],
        compiler_params=pltpu.CompilerParams(vmem_limit_bytes=VMEM),
        cost_estimate=pl.CostEstimate(flops=2 * samples * snps * TILE, bytes_accessed=2 * samples * snps, transcendentals=0),
        name="project",
    )(*parts, inverse, standard, kept)


PANEL = 16


def inverse_kernel(gram, out, left, right):
    left[...] = gram[...]
    lanes = lax.broadcasted_iota(jnp.int32, (TILE, TILE), 1)
    subs = lax.broadcasted_iota(jnp.int32, (TILE, TILE), 0)
    right[...] = jnp.where(lanes == subs, 1.0, 0.0)
    panel_rows = lax.broadcasted_iota(jnp.int32, (PANEL, TILE), 0)
    for start in range(0, TILE, PANEL):
        stop = start + PANEL
        upper = left[start:stop, :]
        done = right[start:stop, :]
        columns = [
            jnp.broadcast_to(upper[:, start + j : start + j + 1], (PANEL, TILE)) for j in range(PANEL)
        ]
        for k in range(PANEL):
            pivot = columns[k][k : k + 1, :]
            root = lax.rsqrt(pivot)
            below = jnp.where(panel_rows > k, columns[k] * (root * root), 0.0)
            for j in range(k + 1, PANEL):
                columns[j] = columns[j] - below * columns[j][k : k + 1, :]
            factor = jnp.where(panel_rows == k, root, 1.0)
            upper = upper * factor - below * upper[k : k + 1, :]
            done = done * factor - below * done[k : k + 1, :]
        out[start:stop, :] = done
        if stop < TILE:
            both = lax.dot_general(
                upper[:, stop:] if False else upper,
                jnp.concatenate([upper, done], axis=1),
                (((0,), (0,)), ((), ())),
                precision=lax.Precision.HIGHEST,
                preferred_element_type=jnp.float32,
            )
            left[stop:, :] -= both[stop:, :TILE]
            right[stop:, :] -= both[stop:, TILE:]


def invert_factor(gram):
    return pl.pallas_call(
        inverse_kernel,
        out_shape=jax.ShapeDtypeStruct((TILE, TILE), jnp.float32),
        scratch_shapes=[pltpu.VMEM((TILE, TILE), jnp.float32), pltpu.VMEM((TILE, TILE), jnp.float32)],
        compiler_params=pltpu.CompilerParams(vmem_limit_bytes=VMEM),
        cost_estimate=pl.CostEstimate(flops=20_000_000, bytes_accessed=16_000_000, transcendentals=0),
        name="invert_factor",
    )(gram)


def scores_kernel(scale, keep, projected, inverse, scores):
    high, low = split(inverse[...])
    samples = projected.shape[0]
    lanes = lax.broadcasted_iota(jnp.int32, (TILE, samples), 1).astype(jnp.float32)
    for j in range(keep.shape[0]):
        row = jnp.broadcast_to(keep[j : j + 1, :].astype(jnp.float32), (TILE, TILE)).T
        pick = jnp.where(lanes == jnp.tile(row, (1, samples // TILE)), 1.0, 0.0).astype(jnp.bfloat16)
        chosen = jnp.dot(pick, projected[...], preferred_element_type=jnp.float32).astype(jnp.bfloat16)
        dims = (((1,), (1,)), ((), ()))
        value = lax.dot_general(chosen, high, dims, preferred_element_type=jnp.float32)
        value = value + lax.dot_general(chosen, low, dims, preferred_element_type=jnp.float32)
        scores[j * TILE : (j + 1) * TILE, :] = value * scale


def score(scale, keep, projected, inverse):
    return pl.pallas_call(
        functools.partial(scores_kernel, scale),
        out_shape=jax.ShapeDtypeStruct((keep.shape[0] * TILE, TILE), jnp.float32),
        compiler_params=pltpu.CompilerParams(vmem_limit_bytes=VMEM),
        cost_estimate=pl.CostEstimate(flops=1_000_000_000, bytes_accessed=1_000_000, transcendentals=0),
        name="score",
    )(keep, projected, inverse)


def loadings_kernel(pieces, order, *refs):
    parts = refs[:pieces]
    inverse, loadings = refs[pieces:]
    high, low = split(inverse[...])
    position = 0
    for part in parts:
        for row in range(0, part.shape[0], TILE):
            start = pl.multiple_of(order[position] * TILE, TILE)
            loadings[pl.ds(start, TILE), :] = product(part[row : row + TILE, :], high, low)
            position += 1


def load(order, parts, inverse):
    count = sum(part.shape[0] for part in parts)
    return pl.pallas_call(
        functools.partial(loadings_kernel, len(parts)),
        in_specs=[pl.BlockSpec(memory_space=pltpu.SMEM)] + [pl.BlockSpec(memory_space=pltpu.VMEM)] * (len(parts) + 1),
        out_shape=jax.ShapeDtypeStruct((count, TILE), jnp.float32),
        compiler_params=pltpu.CompilerParams(vmem_limit_bytes=VMEM),
        cost_estimate=pl.CostEstimate(flops=100_000_000, bytes_accessed=1_000_000, transcendentals=0),
        name="load",
    )(order, *parts, inverse)


def scatter_sum(turned, standard, gram):
    half = BLOCKS // 2 * TILE
    sent = totals(turned, standard, BLOCKS // 2, BLOCKS)
    got = exchange(sent, core_mask)
    got_gram = exchange(gram, core_mask)
    own = totals(turned, standard, 0, BLOCKS // 2)
    for mask in (first_mask, second_mask):
        half //= 2
        gram = gram + got_gram
        send = own[half:] + got[half:]
        own = own[:half] + got[:half]
        both = exchange(jnp.concatenate([send, gram], axis=0), mask)
        got, got_gram = both[:half], both[half:]
    gram = gram + got_gram
    own = own + got
    packets = []
    for q in range(1, 4):
        packet = jnp.concatenate([own[q * TILE : (q + 1) * TILE], gram], axis=0)
        packets.append(exchange(packet, lambda d, q=q: q << 3))
    total = jnp.concatenate([own[:TILE], gram], axis=0)
    total = (total + packets[0]) + (packets[1] + packets[2])
    bit = BLOCKS
    while bit < lax.axis_size(AXES):
        total = total + exchange(total, lambda d, bit=bit: bit)
        bit *= 2
    return total[:TILE], total[TILE:]


def along_z(own):
    return [own] + [exchange(own, lambda d, q=q: q << 3) for q in range(1, 4)]


def on_device(dosage, keep_rows, allele_counts, projection):
    groups = lax.axis_size(AXES)
    samples_total = dosage.shape[0] * groups
    kept_total = keep_rows.shape[0] * groups
    device = lax.axis_index("wide") * lax.axis_size("narrow") + lax.axis_index("narrow")
    order = block_order(device)
    keep = keep_rows.reshape(-1, TILE)
    counts = allele_counts.reshape(-1, TILE)
    standard, _, turned, gram, kept = standardize(samples_total, order, dosage, keep, counts, projection)
    own, gram = scatter_sum(turned, standard, gram)
    inverse = invert_factor(gram)
    near = jnp.concatenate(along_z(own), axis=0)
    plane = [near, exchange(near, second_mask)]
    plane = plane + [exchange(part, first_mask) for part in plane]
    parts = plane + [exchange(part, core_mask) for part in plane]
    projected, turned, gram = project(parts, inverse, standard, kept)
    own, gram = scatter_sum(turned, standard, gram)
    inverse = invert_factor(gram)
    near = jnp.concatenate(along_z(own), axis=0)
    parts = [near, exchange(near, lambda d: 4)]
    scores = score(math.sqrt(kept_total), keep, projected, inverse)
    position = lax.iota(jnp.int32, 8)
    place = (lax.axis_index("wide") & 7) ^ (((position & 3) << 1) | (position >> 2))
    loadings = load(place, parts, inverse)
    return (scores, loadings)


def solution(mesh):
    in_specs = (P(AXES, None), P(AXES), P(), P())
    out_specs = (P(AXES, None), P("narrow", None))
    return jax.shard_map(
        on_device, mesh=mesh, in_specs=in_specs, out_specs=out_specs, check_vma=False
    )
```

time: 390 us -> 149 us (0.38)
  waiting for transfers between devices: 272 us -> 62.5 us
  other arithmetic: 56.2 us -> 0.75 us
  Pallas kernels: 0 us -> 47.1 us
  starting transfers between devices: 0.26 us -> 34.4 us
  matrix products: 24.9 us -> 0 us
  local copies, waits for them, and re-layouts: 22.4 us -> 2.67 us
  between operations: 14.2 us -> 0.96 us
    psum x2 -> x0, waiting for transfers between devices: 272 us -> none  [the longest x1 137 us: on_device(): lax.psum(transposed_product(standard, projected), ('wide', 'narrow'))]
    ppermute x0 -> x28, waiting for transfers between devices: none -> 62.5 us  [exchange(): lax.ppermute(value, AXES, [(d, d ^ mask_of(d)) for d in range(count)])]
    pallas_call x0 -> x10, Pallas kernels: none -> 47.1 us  [the longest x4 15.4 us: totals(): pl.pallas_call(totals_kernel, grid=(count // WIDTH,), in_specs=[pl.BlockS...]
    another operation x10 -> x0, other arithmetic: 45.7 us -> none  [the longest x6 24.8 us: invert_factor(): lower_factor = jnp.linalg.cholesky(gram_matrix)]
    ppermute x0 -> x28, starting transfers between devices: none -> 34.4 us  [exchange(): lax.ppermute(value, AXES, [(d, d ^ mask_of(d)) for d in range(count)])]
    dot_general x9 -> x0, matrix products: 24.3 us -> none  [the longest x4 8.83 us: transposed_product(): lax.dot_general(left_side, right_side, (((0,), (0,)), ((), ())), preferre...]
    gather x1 -> x0, local copies, waits for them, and re-layouts: 19.5 us -> none  [on_device(): chosen = jnp.take(dosage, keep_rows, axis=0)]
    convert_element_type x1 -> x0, other arithmetic: 6.56 us -> none  [on_device(): ((chosen.astype(jnp.float32) - center) / spread).astype(jnp.bfloat16)]
  transfers between devices with their start and end apart: 2 -> 28, of which waited for: 2 -> 16; matrix products, arithmetic and copies ran while one was open for 0% -> 0% of each run, Pallas kernels for 0% -> 13%
where the time goes in v1:
time: 149 us; the launch traced here: 148 us
  waiting for transfers between devices  62.5 us (42%)
  Pallas kernels  47.1 us (32%)
  starting transfers between devices  34.4 us (23%)
  local copies, waits for them, and re-layouts  2.67 us (2%)
    ppermute x28, waiting for transfers between devices, exchange(): lax.ppermute(value, AXES, [(d, d ^ mask_of(d)) for d in range(count)])  62.5 us
    ppermute x28, starting transfers between devices, exchange(): lax.ppermute(value, AXES, [(d, d ^ mask_of(d)) for d in range(count)])  34.4 us
    pallas_call x4, Pallas kernels, totals(): pl.pallas_call(totals_kernel, grid=(count // WIDTH,), in_specs=[pl.BlockS...  15.4 us
    pallas_call x1, Pallas kernels, standardize(): pl.pallas_call(functools.partial(standard_kernel, samples_total), grid_sp...  10.3 us
    pallas_call x2, Pallas kernels, invert_factor(): pl.pallas_call(inverse_kernel, out_shape=jax.ShapeDtypeStruct((TILE, TILE...  9.79 us
    pallas_call x1, Pallas kernels, project(): pl.pallas_call(functools.partial(project_kernel, len(parts)), grid=(sampl...  7.15 us
  transfers between devices with their start and end apart: 28, of which 16 were waited for; matrix products, arithmetic and copies ran while one was open for 0% of the time, Pallas kernels for 13%

profile of v1, /device:TPU:0, one launch (start us, length us, event | category | flops | bytes accessed | tf_op | source)
XLA Modules:
  0.0 148.3 jit_solution(10807353097141738583)
XLA Ops:
  3.3 10.3 %standardize.1 = (bf16[1024,4096]{1,0:T(8,128)(2,1)}, bf16[1024,128]{1,0:T(8,128)(2,1)}, bf16[128,1024]{1,0:T(8,128)(2,1)S(1)}, f32[128,128]{1,0:T(8,128)S(1)}, f32[1024,128]{1,0:T(8,128)S(1)}) custom-call(s32[32]{0:T(128)S(1)} %and_add_fusion.order, bf16[1024,4096]{1,0:T(8,128)(2,1)} %dosage.1, s32[7,128]{1,0:T(8,128)S(1)} %bitcast.3, ...), custom_call_target="tpu_custom_call" | custom-call | flops 1073741824 | bytes 16777216 | tf_op jit(solution)/shard_map/standardize/pallas_call | solution.py:101
  13.6 3.8 %totals.5 = f32[2048,128]{1,0:T(8,128)S(1)} custom-call(bf16[128,1024]{1,0:T(8,128)(2,1)S(1)} %get-tuple-element.9.turned, bf16[1024,4096]{1,0:T(8,128)(2,1)} %get-tuple-element.10.standard.refs_9_), custom_call_target="tpu_custom_call" | custom-call | flops 536870912 | bytes 4194304 | tf_op jit(solution)/shard_map/totals/pallas_call | solution.py:148
  18.0 3.8 %totals.4 = f32[2048,128]{1,0:T(8,128)S(1)} custom-call(bf16[128,1024]{1,0:T(8,128)(2,1)S(1)} %get-tuple-element.9.turned, bf16[1024,4096]{1,0:T(8,128)(2,1)} %get-tuple-element.10.standard.refs_9_), custom_call_target="tpu_custom_call" | custom-call | flops 536870912 | bytes 4194304 | tf_op jit(solution)/shard_map/totals/pallas_call | solution.py:148
  22.0 3.0 %collective-permute-start.2 = (f32[1152,128]{1,0:T(8,128)S(1)}, f32[1152,128]{1,0:T(8,128)S(1)}, u32[]{:S(2)}, u32[]{:S(2)}) collective-permute-start(f32[1152,128]{1,0:T(8,128)S(1)} %pad_maximum_fusion), channel_id=1, source_target_pairs={{0,4},{1,3},{2,6},{3,1},{4,0},{5,7},{6,2},{7,5},{8,12},{9,11},{10,... | collective-permute-start | bytes 1769480 | tf_op jit(solution)/shard_map/ppermute | solution.py:49
  25.0 7.9 %collective-permute-done.2 = f32[1152,128]{1,0:T(8,128)S(1)} collective-permute-done((f32[1152,128]{1,0:T(8,128)S(1)}, f32[1152,128]{1,0:T(8,128)S(1)}, u32[]{:S(2)}, u32[]{:S(2)}) %collective-permute-start.2) | collective-permute-done | bytes 589856 | tf_op jit(solution)/shard_map/ppermute | solution.py:49
  33.0 2.1 %collective-permute-start.3 = (f32[640,128]{1,0:T(8,128)S(1)}, f32[640,128]{1,0:T(8,128)S(1)}, u32[]{:S(2)}, u32[]{:S(2)}) collective-permute-start(f32[640,128]{1,0:T(8,128)S(1)} %pad_maximum_fusion.2), channel_id=1, source_target_pairs={{0,2},{1,5},{2,0},{3,7},{4,6},{5,1},{6,4},{7,3},{8,10},{9,13},{10,... | collective-permute-start | bytes 983048 | tf_op jit(solution)/shard_map/ppermute | solution.py:49
  35.1 5.1 %collective-permute-done.3 = f32[640,128]{1,0:T(8,128)S(1)} collective-permute-done((f32[640,128]{1,0:T(8,128)S(1)}, f32[640,128]{1,0:T(8,128)S(1)}, u32[]{:S(2)}, u32[]{:S(2)}) %collective-permute-start.3) | collective-permute-done | bytes 327712 | tf_op jit(solution)/shard_map/ppermute | solution.py:49
  40.2 2.1 %collective-permute-start.4 = (f32[256,128]{1,0:T(8,128)S(1)}, f32[256,128]{1,0:T(8,128)S(1)}, u32[]{:S(2)}, u32[]{:S(2)}) collective-permute-start(f32[256,128]{1,0:T(8,128)S(1)} %get-tuple-element.36), channel_id=1, source_target_pairs={{0,8},{1,9},{2,10},{3,11},{4,12},{5,13},{6,14},{7,15},{8,0},{9,1},... | collective-permute-start | bytes 393224 | tf_op jit(solution)/shard_map/ppermute | solution.py:49
  42.4 2.6 %collective-permute-start.5 = (f32[256,128]{1,0:T(8,128)S(1)}, f32[256,128]{1,0:T(8,128)S(1)}, u32[]{:S(2)}, u32[]{:S(2)}) collective-permute-start(f32[256,128]{1,0:T(8,128)S(1)} %get-tuple-element.37), channel_id=1, source_target_pairs={{0,16},{1,17},{2,18},{3,19},{4,20},{5,21},{6,22},{7,23},{8,24},{9,... | collective-permute-start | bytes 393224 | tf_op jit(solution)/shard_map/ppermute | solution.py:49
  46.7 7.2 %collective-permute-done.5 = f32[256,128]{1,0:T(8,128)S(1)} collective-permute-done((f32[256,128]{1,0:T(8,128)S(1)}, f32[256,128]{1,0:T(8,128)S(1)}, u32[]{:S(2)}, u32[]{:S(2)}) %collective-permute-start.5) | collective-permute-done | bytes 131104 | tf_op jit(solution)/shard_map/ppermute | solution.py:49
  53.9 2.5 %collective-permute-start.9 = (f32[128,128]{1,0:T(8,128)S(1)}, f32[128,128]{1,0:T(8,128)S(1)}, u32[]{:S(2)}, u32[]{:S(2)}) collective-permute-start(f32[128,128]{1,0:T(8,128)S(1)} %get-tuple-element.31), channel_id=1, source_target_pairs={{0,24},{1,25},{2,26},{3,27},{4,28},{5,29},{6,30},{7,31},{8,16},{9,... | collective-permute-start | bytes 196616 | tf_op jit(solution)/shard_map/ppermute | solution.py:49
  65.4 6.0 %collective-permute-done.10.refs_1_ = f32[512,128]{1,0:T(8,128)S(1)} collective-permute-done((f32[512,128]{1,0:T(8,128)S(1)}, f32[512,128]{1,0:T(8,128)S(1)}, u32[]{:S(2)}, u32[]{:S(2)}) %collective-permute-start.10) | collective-permute-done | bytes 262176 | tf_op jit(solution)/shard_map/ppermute | solution.py:49
  73.5 4.3 %collective-permute-done.12.refs_3_ = f32[512,128]{1,0:T(8,128)S(1)} collective-permute-done((f32[512,128]{1,0:T(8,128)S(1)}, f32[512,128]{1,0:T(8,128)S(1)}, u32[]{:S(2)}, u32[]{:S(2)}) %collective-permute-start.12) | collective-permute-done | bytes 262176 | tf_op jit(solution)/shard_map/ppermute | solution.py:49
  77.8 4.9 %invert_factor.2.refs_8_ = f32[128,128]{1,0:T(8,128)S(1)} custom-call(f32[128,128]{1,0:T(8,128)S(1)} %get-tuple-element.30.gram), custom_call_target="tpu_custom_call" | custom-call | flops 20000000 | bytes 16000000 | tf_op jit(solution)/shard_map/invert_factor/pallas_call | solution.py:253
  82.8 7.2 %project.1 = (bf16[1024,128]{1,0:T(8,128)(2,1)S(1)}, bf16[128,1024]{1,0:T(8,128)(2,1)S(1)}, f32[128,128]{1,0:T(8,128)S(1)}) custom-call(f32[512,128]{1,0:T(8,128)S(1)} %pad_maximum_fusion.4.refs_0_, f32[512,128]{1,0:T(8,128)S(1)} %collective-permute-done.10.refs_1_, f32[512,128]{1,0:T(8,128)S(1)} %collective-permute-done.11.refs_2_, ...), custom_call_target="tpu_custom_call" | custom-call | flops 1073741824 | bytes 8388608 | tf_op jit(solution)/shard_map/project/pallas_call | solution.py:188
  89.9 3.8 %totals.7 = f32[2048,128]{1,0:T(8,128)S(1)} custom-call(bf16[128,1024]{1,0:T(8,128)(2,1)S(1)} %get-tuple-element.14.turned, bf16[1024,4096]{1,0:T(8,128)(2,1)} %get-tuple-element.10.standard.refs_9_), custom_call_target="tpu_custom_call" | custom-call | flops 536870912 | bytes 4194304 | tf_op jit(solution)/shard_map/totals/pallas_call | solution.py:148
  94.4 4.0 %totals.6 = f32[2048,128]{1,0:T(8,128)S(1)} custom-call(bf16[128,1024]{1,0:T(8,128)(2,1)S(1)} %get-tuple-element.14.turned, bf16[1024,4096]{1,0:T(8,128)(2,1)} %get-tuple-element.10.standard.refs_9_), custom_call_target="tpu_custom_call" | custom-call | flops 536870912 | bytes 4194304 | tf_op jit(solution)/shard_map/totals/pallas_call | solution.py:148
  100.2 8.3 %collective-permute-done.19 = f32[1152,128]{1,0:T(8,128)S(1)} collective-permute-done((f32[1152,128]{1,0:T(8,128)S(1)}, f32[1152,128]{1,0:T(8,128)S(1)}, u32[]{:S(2)}, u32[]{:S(2)}) %collective-permute-start.19) | collective-permute-done | bytes 589856 | tf_op jit(solution)/shard_map/ppermute | solution.py:49
  110.2 5.5 %collective-permute-done.20 = f32[640,128]{1,0:T(8,128)S(1)} collective-permute-done((f32[640,128]{1,0:T(8,128)S(1)}, f32[640,128]{1,0:T(8,128)S(1)}, u32[]{:S(2)}, u32[]{:S(2)}) %collective-permute-start.20) | collective-permute-done | bytes 327712 | tf_op jit(solution)/shard_map/ppermute | solution.py:49
  121.7 7.0 %collective-permute-done.22 = f32[256,128]{1,0:T(8,128)S(1)} collective-permute-done((f32[256,128]{1,0:T(8,128)S(1)}, f32[256,128]{1,0:T(8,128)S(1)}, u32[]{:S(2)}, u32[]{:S(2)}) %collective-permute-start.22) | collective-permute-done | bytes 131104 | tf_op jit(solution)/shard_map/ppermute | solution.py:49
  128.7 2.2 %collective-permute-start.26 = (f32[128,128]{1,0:T(8,128)S(1)}, f32[128,128]{1,0:T(8,128)S(1)}, u32[]{:S(2)}, u32[]{:S(2)}) collective-permute-start(f32[128,128]{1,0:T(8,128)S(1)} %get-tuple-element.28), channel_id=1, source_target_pairs={{0,24},{1,25},{2,26},{3,27},{4,28},{5,29},{6,30},{7,31},{8,16},{9,... | collective-permute-start | bytes 196616 | tf_op jit(solution)/shard_map/ppermute | solution.py:49
  133.2 2.3 %collective-permute-done.26 = f32[128,128]{1,0:T(8,128)S(1)} collective-permute-done((f32[128,128]{1,0:T(8,128)S(1)}, f32[128,128]{1,0:T(8,128)S(1)}, u32[]{:S(2)}, u32[]{:S(2)}) %collective-permute-start.26) | collective-permute-done | bytes 65568 | tf_op jit(solution)/shard_map/ppermute | solution.py:49
  139.0 4.9 %invert_factor.3.inverse.refs_2_ = f32[128,128]{1,0:T(8,128)S(1)} custom-call(f32[128,128]{1,0:T(8,128)S(1)} %get-tuple-element.29.gram), custom_call_target="tpu_custom_call" | custom-call | flops 20000000 | bytes 16000000 | tf_op jit(solution)/shard_map/invert_factor/pallas_call | solution.py:253
  143.9 2.4 %score.1 = f32[896,128]{1,0:T(8,128)} custom-call(s32[7,128]{1,0:T(8,128)S(1)} %bitcast.4, bf16[1024,128]{1,0:T(8,128)(2,1)S(1)} %get-tuple-element.13.projected, f32[128,128]{1,0:T(8,128)S(1)} %invert_factor.3.inverse.refs_2_), custom_call_target="tpu_custom_call" | custom-call | flops 1000000000 | bytes 1000000 | tf_op jit(solution)/shard_map/score/pallas_call | solution.py:278
  (77 shorter events, 34.0 us)
Async XLA Ops:
  17.4 4.4 %collective-permute-start = (f32[2048,128]{1,0:T(8,128)S(1)}, f32[2048,128]{1,0:T(8,128)S(1)}, u32[]{:S(2)}, u32[]{:S(2)}) collective-permute-start(f32[2048,128]{1,0:T(8,128)S(1)} %totals.5), channel_id=1, source_target_pairs={{0,1},{1,0},{2,3},{3,2},{4,5},{5,4},{6,7},{7,6},{8,9},{9,8},{10,11... | collective-permute-start | bytes 3145736 | tf_op jit(solution)/shard_map/ppermute | solution.py:49
  22.0 10.9 %collective-permute-start.2 = (f32[1152,128]{1,0:T(8,128)S(1)}, f32[1152,128]{1,0:T(8,128)S(1)}, u32[]{:S(2)}, u32[]{:S(2)}) collective-permute-start(f32[1152,128]{1,0:T(8,128)S(1)} %pad_maximum_fusion), channel_id=1, source_target_pairs={{0,4},{1,3},{2,6},{3,1},{4,0},{5,7},{6,2},{7,5},{8,12},{9,11},{10,... | collective-permute-start | bytes 1769480 | tf_op jit(solution)/shard_map/ppermute | solution.py:49
  33.0 7.1 %collective-permute-start.3 = (f32[640,128]{1,0:T(8,128)S(1)}, f32[640,128]{1,0:T(8,128)S(1)}, u32[]{:S(2)}, u32[]{:S(2)}) collective-permute-start(f32[640,128]{1,0:T(8,128)S(1)} %pad_maximum_fusion.2), channel_id=1, source_target_pairs={{0,2},{1,5},{2,0},{3,7},{4,6},{5,1},{6,4},{7,3},{8,10},{9,13},{10,... | collective-permute-start | bytes 983048 | tf_op jit(solution)/shard_map/ppermute | solution.py:49
  40.2 6.4 %collective-permute-start.4 = (f32[256,128]{1,0:T(8,128)S(1)}, f32[256,128]{1,0:T(8,128)S(1)}, u32[]{:S(2)}, u32[]{:S(2)}) collective-permute-start(f32[256,128]{1,0:T(8,128)S(1)} %get-tuple-element.36), channel_id=1, source_target_pairs={{0,8},{1,9},{2,10},{3,11},{4,12},{5,13},{6,14},{7,15},{8,0},{9,1},... | collective-permute-start | bytes 393224 | tf_op jit(solution)/shard_map/ppermute | solution.py:49
  42.4 11.5 %collective-permute-start.5 = (f32[256,128]{1,0:T(8,128)S(1)}, f32[256,128]{1,0:T(8,128)S(1)}, u32[]{:S(2)}, u32[]{:S(2)}) collective-permute-start(f32[256,128]{1,0:T(8,128)S(1)} %get-tuple-element.37), channel_id=1, source_target_pairs={{0,16},{1,17},{2,18},{3,19},{4,20},{5,21},{6,22},{7,23},{8,24},{9,... | collective-permute-start | bytes 393224 | tf_op jit(solution)/shard_map/ppermute | solution.py:49
  45.0 8.8 %collective-permute-start.6 = (f32[256,128]{1,0:T(8,128)S(1)}, f32[256,128]{1,0:T(8,128)S(1)}, u32[]{:S(2)}, u32[]{:S(2)}) collective-permute-start(f32[256,128]{1,0:T(8,128)S(1)} %get-tuple-element.35), channel_id=1, source_target_pairs={{0,24},{1,25},{2,26},{3,27},{4,28},{5,29},{6,30},{7,31},{8,16},{9,... | collective-permute-start | bytes 393224 | tf_op jit(solution)/shard_map/ppermute | solution.py:49
  53.9 6.4 %collective-permute-start.9 = (f32[128,128]{1,0:T(8,128)S(1)}, f32[128,128]{1,0:T(8,128)S(1)}, u32[]{:S(2)}, u32[]{:S(2)}) collective-permute-start(f32[128,128]{1,0:T(8,128)S(1)} %get-tuple-element.31), channel_id=1, source_target_pairs={{0,24},{1,25},{2,26},{3,27},{4,28},{5,29},{6,30},{7,31},{8,16},{9,... | collective-permute-start | bytes 196616 | tf_op jit(solution)/shard_map/ppermute | solution.py:49
  56.4 5.2 %collective-permute-start.8 = (f32[128,128]{1,0:T(8,128)S(1)}, f32[128,128]{1,0:T(8,128)S(1)}, u32[]{:S(2)}, u32[]{:S(2)}) collective-permute-start(f32[128,128]{1,0:T(8,128)S(1)} %get-tuple-element.31), channel_id=1, source_target_pairs={{0,16},{1,17},{2,18},{3,19},{4,20},{5,21},{6,22},{7,23},{8,24},{9,... | collective-permute-start | bytes 196616 | tf_op jit(solution)/shard_map/ppermute | solution.py:49
  62.4 9.1 %collective-permute-start.10 = (f32[512,128]{1,0:T(8,128)S(1)}, f32[512,128]{1,0:T(8,128)S(1)}, u32[]{:S(2)}, u32[]{:S(2)}) collective-permute-start(f32[512,128]{1,0:T(8,128)S(1)} %pad_maximum_fusion.4.refs_0_), channel_id=1, source_target_pairs={{0,2},{1,5},{2,0},{3,7},{4,6},{5,1},{6,4},{7,3},{8,10},{9,13},{10,... | collective-permute-start | bytes 786440 | tf_op jit(solution)/shard_map/ppermute | solution.py:49
  63.9 9.6 %collective-permute-start.11 = (f32[512,128]{1,0:T(8,128)S(1)}, f32[512,128]{1,0:T(8,128)S(1)}, u32[]{:S(2)}, u32[]{:S(2)}) collective-permute-start(f32[512,128]{1,0:T(8,128)S(1)} %pad_maximum_fusion.4.refs_0_), channel_id=1, source_target_pairs={{0,4},{1,3},{2,6},{3,1},{4,0},{5,7},{6,2},{7,5},{8,12},{9,11},{10,... | collective-permute-start | bytes 786440 | tf_op jit(solution)/shard_map/ppermute | solution.py:49
  71.5 6.4 %collective-permute-start.12 = (f32[512,128]{1,0:T(8,128)S(1)}, f32[512,128]{1,0:T(8,128)S(1)}, u32[]{:S(2)}, u32[]{:S(2)}) collective-permute-start(f32[512,128]{1,0:T(8,128)S(1)} %collective-permute-done.10.refs_1_), channel_id=1, source_target_pairs={{0,4},{1,3},{2,6},{3,1},{4,0},{5,7},{6,2},{7,5},{8,12},{9,11},{10,... | collective-permute-start | bytes 786440 | tf_op jit(solution)/shard_map/ppermute | solution.py:49
  73.0 9.7 %collective-permute-start.13 = (f32[512,128]{1,0:T(8,128)S(1)}, f32[512,128]{1,0:T(8,128)S(1)}, u32[]{:S(2)}, u32[]{:S(2)}) collective-permute-start(f32[512,128]{1,0:T(8,128)S(1)} %pad_maximum_fusion.4.refs_0_), channel_id=1, source_target_pairs={{0,1},{1,0},{2,3},{3,2},{4,5},{5,4},{6,7},{7,6},{8,9},{9,8},{10,11... | collective-permute-start | bytes 786440 | tf_op jit(solution)/shard_map/ppermute | solution.py:49
  73.0 9.8 %collective-permute-start.14 = (f32[512,128]{1,0:T(8,128)S(1)}, f32[512,128]{1,0:T(8,128)S(1)}, u32[]{:S(2)}, u32[]{:S(2)}) collective-permute-start(f32[512,128]{1,0:T(8,128)S(1)} %collective-permute-done.10.refs_1_), channel_id=1, source_target_pairs={{0,1},{1,0},{2,3},{3,2},{4,5},{5,4},{6,7},{7,6},{8,9},{9,8},{10,11... | collective-permute-start | bytes 786440 | tf_op jit(solution)/shard_map/ppermute | solution.py:49
  73.5 9.3 %collective-permute-start.15 = (f32[512,128]{1,0:T(8,128)S(1)}, f32[512,128]{1,0:T(8,128)S(1)}, u32[]{:S(2)}, u32[]{:S(2)}) collective-permute-start(f32[512,128]{1,0:T(8,128)S(1)} %collective-permute-done.11.refs_2_), channel_id=1, source_target_pairs={{0,1},{1,0},{2,3},{3,2},{4,5},{5,4},{6,7},{7,6},{8,9},{9,8},{10,11... | collective-permute-start | bytes 786440 | tf_op jit(solution)/shard_map/ppermute | solution.py:49
  77.8 4.9 %collective-permute-start.16 = (f32[512,128]{1,0:T(8,128)S(1)}, f32[512,128]{1,0:T(8,128)S(1)}, u32[]{:S(2)}, u32[]{:S(2)}) collective-permute-start(f32[512,128]{1,0:T(8,128)S(1)} %collective-permute-done.12.refs_3_), channel_id=1, source_target_pairs={{0,1},{1,0},{2,3},{3,2},{4,5},{5,4},{6,7},{7,6},{8,9},{9,8},{10,11... | collective-permute-start | bytes 786440 | tf_op jit(solution)/shard_map/ppermute | solution.py:49
  93.8 4.7 %collective-permute-start.17 = (f32[2048,128]{1,0:T(8,128)S(1)}, f32[2048,128]{1,0:T(8,128)S(1)}, u32[]{:S(2)}, u32[]{:S(2)}) collective-permute-start(f32[2048,128]{1,0:T(8,128)S(1)} %totals.7), channel_id=1, source_target_pairs={{0,1},{1,0},{2,3},{3,2},{4,5},{5,4},{6,7},{7,6},{8,9},{9,8},{10,11... | collective-permute-start | bytes 3145736 | tf_op jit(solution)/shard_map/ppermute | solution.py:49
  98.6 9.9 %collective-permute-start.19 = (f32[1152,128]{1,0:T(8,128)S(1)}, f32[1152,128]{1,0:T(8,128)S(1)}, u32[]{:S(2)}, u32[]{:S(2)}) collective-permute-start(f32[1152,128]{1,0:T(8,128)S(1)} %pad_maximum_fusion.1), channel_id=1, source_target_pairs={{0,4},{1,3},{2,6},{3,1},{4,0},{5,7},{6,2},{7,5},{8,12},{9,11},{10,... | collective-permute-start | bytes 1769480 | tf_op jit(solution)/shard_map/ppermute | solution.py:49
  108.7 7.1 %collective-permute-start.20 = (f32[640,128]{1,0:T(8,128)S(1)}, f32[640,128]{1,0:T(8,128)S(1)}, u32[]{:S(2)}, u32[]{:S(2)}) collective-permute-start(f32[640,128]{1,0:T(8,128)S(1)} %pad_maximum_fusion.3), channel_id=1, source_target_pairs={{0,2},{1,5},{2,0},{3,7},{4,6},{5,1},{6,4},{7,3},{8,10},{9,13},{10,... | collective-permute-start | bytes 983048 | tf_op jit(solution)/shard_map/ppermute | solution.py:49
  115.9 5.7 %collective-permute-start.21 = (f32[256,128]{1,0:T(8,128)S(1)}, f32[256,128]{1,0:T(8,128)S(1)}, u32[]{:S(2)}, u32[]{:S(2)}) collective-permute-start(f32[256,128]{1,0:T(8,128)S(1)} %get-tuple-element.33), channel_id=1, source_target_pairs={{0,8},{1,9},{2,10},{3,11},{4,12},{5,13},{6,14},{7,15},{8,0},{9,1},... | collective-permute-start | bytes 393224 | tf_op jit(solution)/shard_map/ppermute | solution.py:49
  117.0 11.6 %collective-permute-start.22 = (f32[256,128]{1,0:T(8,128)S(1)}, f32[256,128]{1,0:T(8,128)S(1)}, u32[]{:S(2)}, u32[]{:S(2)}) collective-permute-start(f32[256,128]{1,0:T(8,128)S(1)} %get-tuple-element.34), channel_id=1, source_target_pairs={{0,16},{1,17},{2,18},{3,19},{4,20},{5,21},{6,22},{7,23},{8,24},{9,... | collective-permute-start | bytes 393224 | tf_op jit(solution)/shard_map/ppermute | solution.py:49
  119.0 9.7 %collective-permute-start.23 = (f32[256,128]{1,0:T(8,128)S(1)}, f32[256,128]{1,0:T(8,128)S(1)}, u32[]{:S(2)}, u32[]{:S(2)}) collective-permute-start(f32[256,128]{1,0:T(8,128)S(1)} %get-tuple-element.32), channel_id=1, source_target_pairs={{0,24},{1,25},{2,26},{3,27},{4,28},{5,29},{6,30},{7,31},{8,16},{9,... | collective-permute-start | bytes 393224 | tf_op jit(solution)/shard_map/ppermute | solution.py:49
  128.7 6.8 %collective-permute-start.26 = (f32[128,128]{1,0:T(8,128)S(1)}, f32[128,128]{1,0:T(8,128)S(1)}, u32[]{:S(2)}, u32[]{:S(2)}) collective-permute-start(f32[128,128]{1,0:T(8,128)S(1)} %get-tuple-element.28), channel_id=1, source_target_pairs={{0,24},{1,25},{2,26},{3,27},{4,28},{5,29},{6,30},{7,31},{8,16},{9,... | collective-permute-start | bytes 196616 | tf_op jit(solution)/shard_map/ppermute | solution.py:49
  131.0 5.7 %collective-permute-start.25 = (f32[128,128]{1,0:T(8,128)S(1)}, f32[128,128]{1,0:T(8,128)S(1)}, u32[]{:S(2)}, u32[]{:S(2)}) collective-permute-start(f32[128,128]{1,0:T(8,128)S(1)} %get-tuple-element.28), channel_id=1, source_target_pairs={{0,16},{1,17},{2,18},{3,19},{4,20},{5,21},{6,22},{7,23},{8,24},{9,... | collective-permute-start | bytes 196616 | tf_op jit(solution)/shard_map/ppermute | solution.py:49
  137.4 8.9 %collective-permute-start.27 = (f32[512,128]{1,0:T(8,128)S(1)}, f32[512,128]{1,0:T(8,128)S(1)}, u32[]{:S(2)}, u32[]{:S(2)}) collective-permute-start(f32[512,128]{1,0:T(8,128)S(1)} %pad_maximum_fusion.5.refs_0_), channel_id=1, source_target_pairs={{0,4},{1,5},{2,6},{3,7},{4,0},{5,1},{6,2},{7,3},{8,12},{9,13},{10,... | collective-permute-start | bytes 786440 | tf_op jit(solution)/shard_map/ppermute | solution.py:49
  (8 other events, 68.8 us)

commit v2 on v1

v2 whole, which is shorter than its diff:
```python
import functools
import math

import jax
import jax.numpy as jnp
from jax import lax
from jax.experimental import pallas as pl
from jax.experimental.pallas import tpu as pltpu
from jax.sharding import PartitionSpec as P

AXES = ("wide", "narrow")
TILE = 128
BLOCKS = 32
ROWS = 256
VMEM = 28 * 1024 * 1024
SMALL = 16 * 1024 * 1024
GROUPS = 8


def split(value):
    high = value.astype(jnp.bfloat16)
    low = (value - high.astype(jnp.float32)).astype(jnp.bfloat16)
    return high, low


def product(left, right_high, right_low):
    high, low = split(left)
    dims = (((1,), (1,)), ((), ()))
    dot = functools.partial(lax.dot_general, dimension_numbers=dims, preferred_element_type=jnp.float32)
    return dot(high, right_high) + (dot(high, right_low) + dot(low, right_high))


def relative(position, core):
    first = (position >> 3) & 1
    second = (position >> 2) & 1
    core_bit = (position >> 4) & 1
    target = core ^ core_bit
    bit_x = jnp.where(target == 0, first, second)
    bit_y = jnp.where(target == 0, second, first)
    return core_bit | (bit_y << 1) | (bit_x << 2) | ((position & 3) << 3)


def block_order(device):
    position = lax.iota(jnp.int32, BLOCKS)
    owner = device ^ relative(position, device & 1)
    return (owner & 3) * 8 + ((owner >> 2) & 7)


def exchange(value, mask_of):
    count = lax.axis_size(AXES)
    return lax.ppermute(value, AXES, [(d, d ^ mask_of(d)) for d in range(count)])


def core_mask(d):
    return 1


def first_mask(d):
    return 2 if d & 1 else 4


def second_mask(d):
    return 4 if d & 1 else 2


def group_order(device):
    place = lax.iota(jnp.int32, GROUPS)
    return (((place >> 2) ^ (device & 1)) << 2) | ((place & 3) ^ ((device >> 3) & 3))


def standard_kernel(samples_total, order, dosage, keep, counts, projection, standard, projected, turned, gram, kept, rows_in, sketch_in, keep_in, counts_in, table, basis, whole, sems):
    samples = dosage.shape[0]
    steps = samples // ROWS
    small = [
        pltpu.make_async_copy(source, target, sems.at[i])
        for i, (source, target) in enumerate(((counts, counts_in), (keep, keep_in), (projection, sketch_in)))
    ]
    slabs = [slice(i * ROWS, (i + 1) * ROWS) for i in range(steps)]
    large = [
        pltpu.make_async_copy(dosage.at[slab, :], rows_in.at[slab, :], sems.at[3 + i]) for i, slab in enumerate(slabs)
    ]
    small[0].start()
    small[1].start()
    large[0].start()
    small[2].start()
    for copy in large[1:]:
        copy.start()
    small[0].wait()
    small[1].wait()
    frequency = counts_in[...].astype(jnp.float32) / (2.0 * samples_total)
    table[0] = 2.0 * frequency
    table[1] = 1.0 / jnp.sqrt(2.0 * frequency * (1.0 - frequency))
    for i in range(samples // TILE):
        rows = lax.broadcasted_iota(jnp.int32, (TILE, TILE), 0) + i * TILE
        found = jnp.zeros((TILE, TILE), jnp.float32)
        for j in range(keep.shape[0]):
            found = jnp.where(rows == keep_in[j : j + 1, :], 1.0, found)
        kept[i * TILE : (i + 1) * TILE, :] = jnp.broadcast_to(jnp.max(found, axis=1, keepdims=True), (TILE, TILE))
    for i, slab in enumerate(slabs):
        large[i].wait()
        if i == 0:
            small[2].wait()
            for p in range(BLOCKS):
                start = pl.multiple_of(order[p] * TILE, TILE)
                basis[p * TILE : (p + 1) * TILE, :] = sketch_in[pl.ds(start, TILE), :]
        for p in range(BLOCKS):
            block = order[p]
            center = table[0, pl.ds(block, 1), :]
            scale = table[1, pl.ds(block, 1), :]
            value = rows_in[slab, pl.ds(pl.multiple_of(block * TILE, TILE), TILE)].astype(jnp.float32)
            standard[slab, p * TILE : (p + 1) * TILE] = ((value - center) * scale).astype(jnp.bfloat16)
    project_rows(standard, basis, kept, projected, turned, whole)
    height = TILE // GROUPS
    for place in range(GROUPS):
        start = pl.multiple_of(order[BLOCKS + place] * height, height)
        gram[place * height : (place + 1) * height, :] = whole[pl.ds(start, height), :]


def project_rows(standard, basis, kept, projected, turned, gram):
    value = jnp.dot(standard[...], basis[...], preferred_element_type=jnp.float32)
    value = jnp.where(kept[...] > 0.0, value, 0.0)
    low = value.astype(jnp.bfloat16)
    low_turned = value.T.astype(jnp.bfloat16)
    projected[...] = low
    turned[...] = low_turned
    gram[...] = jnp.dot(low_turned, low, preferred_element_type=jnp.float32)


ON_CHIP = pl.BlockSpec(memory_space=pltpu.VMEM)
SCALARS = pl.BlockSpec(memory_space=pltpu.SMEM)
FAR = pl.BlockSpec(memory_space=pltpu.HBM)


def standardize(samples_total, order, *arrays):
    dosage, keep, counts, projection = [pltpu.with_memory_space_constraint(x, pltpu.HBM) for x in arrays]
    samples, snps = arrays[0].shape
    return pl.pallas_call(
        functools.partial(standard_kernel, samples_total),
        in_specs=[SCALARS, FAR, FAR, FAR, FAR],
        out_specs=[ON_CHIP] * 5,
        out_shape=[
            jax.ShapeDtypeStruct((samples, snps), jnp.bfloat16),
            jax.ShapeDtypeStruct((samples, TILE), jnp.bfloat16),
            jax.ShapeDtypeStruct((TILE, samples), jnp.bfloat16),
            jax.ShapeDtypeStruct((TILE, TILE), jnp.float32),
            jax.ShapeDtypeStruct((samples, TILE), jnp.float32),
        ],
        scratch_shapes=[
            pltpu.VMEM((samples, snps), jnp.bfloat16),
            pltpu.VMEM(arrays[3].shape, jnp.bfloat16),
            pltpu.VMEM(arrays[1].shape, jnp.int32),
            pltpu.VMEM(arrays[2].shape, jnp.int32),
            pltpu.VMEM((2,) + arrays[2].shape, jnp.float32),
            pltpu.VMEM(arrays[3].shape, jnp.bfloat16),
            pltpu.VMEM((TILE, TILE), jnp.float32),
            pltpu.SemaphoreType.DMA((3 + samples // ROWS,)),
        ],
        compiler_params=pltpu.CompilerParams(vmem_limit_bytes=VMEM),
        cost_estimate=pl.CostEstimate(flops=2 * samples * snps * TILE, bytes_accessed=4 * samples * snps, transcendentals=0),
        name="standardize",
    )(order, dosage, keep, counts, projection)


WIDTH = 512


def totals_kernel(low, high, turned, standard, *refs):
    out = refs[-1]
    base = low * TILE
    for start in range(base, high * TILE, WIDTH):
        value = jnp.dot(turned[...], standard[:, start : start + WIDTH], preferred_element_type=jnp.float32)
        out[start - base : start - base + WIDTH, :] = value.T
    if len(refs) == 2:
        tail = refs[0].shape[0] // 2
        out[(high - low) * TILE :, :] = refs[0][tail:, :]


def totals(turned, standard, low, high, *gram):
    samples = standard.shape[0]
    count = (high - low) * TILE
    tail = TILE // 2 if gram else 0
    return pl.pallas_call(
        functools.partial(totals_kernel, low, high),
        in_specs=[ON_CHIP] * (2 + len(gram)),
        out_specs=ON_CHIP,
        out_shape=jax.ShapeDtypeStruct((count + tail, TILE), jnp.float32),
        compiler_params=pltpu.CompilerParams(vmem_limit_bytes=SMALL),
        cost_estimate=pl.CostEstimate(flops=2 * samples * count * TILE, bytes_accessed=2 * samples * count, transcendentals=0),
        name="totals",
    )(turned, standard, *gram)


def combine_kernel(plan, count, *refs):
    for out, pieces in zip(refs[count:], plan):
        row = 0
        for rows, terms in pieces:
            values = [refs[index][start : start + rows, :] for index, start in terms]
            while len(values) > 1:
                values = [sum(values[i + 1 : i + 2], values[i]) for i in range(0, len(values), 2)]
            out[row : row + rows, :] = values[0]
            row += rows


def combine(arrays, plan):
    shapes = [jax.ShapeDtypeStruct((sum(rows for rows, _ in pieces), TILE), jnp.float32) for pieces in plan]
    size = sum(shape.shape[0] for shape in shapes) * TILE
    return pl.pallas_call(
        functools.partial(combine_kernel, plan, len(arrays)),
        in_specs=[ON_CHIP] * len(arrays),
        out_specs=[ON_CHIP] * len(plan),
        out_shape=shapes,
        compiler_params=pltpu.CompilerParams(vmem_limit_bytes=SMALL),
        cost_estimate=pl.CostEstimate(flops=2 * size, bytes_accessed=12 * size, transcendentals=0),
        name="combine",
    )(*arrays)


def project_kernel(pieces, *refs):
    parts = refs[:pieces]
    inverse, order, standard, kept, projected, turned, gram, basis, whole = refs[pieces:]
    high, low = split(inverse[...])
    start = 0
    for part in parts:
        size = part.shape[0]
        basis[start : start + size, :] = product(part[...], high, low).astype(jnp.bfloat16)
        start += size
    project_rows(standard, basis, kept, projected, turned, whole)
    height = TILE // GROUPS
    for place in range(GROUPS):
        start = pl.multiple_of(order[BLOCKS + place] * height, height)
        gram[place * height : (place + 1) * height, :] = whole[pl.ds(start, height), :]


def project(parts, inverse, order, standard, kept):
    samples, snps = standard.shape
    return pl.pallas_call(
        functools.partial(project_kernel, len(parts)),
        in_specs=[ON_CHIP] * (len(parts) + 1) + [SCALARS, ON_CHIP, ON_CHIP],
        out_specs=[ON_CHIP] * 3,
        out_shape=[
            jax.ShapeDtypeStruct((samples, TILE), jnp.bfloat16),
            jax.ShapeDtypeStruct((TILE, samples), jnp.bfloat16),
            jax.ShapeDtypeStruct((TILE, TILE), jnp.float32),
        ],
        scratch_shapes=[pltpu.VMEM((snps, TILE), jnp.bfloat16), pltpu.VMEM((TILE, TILE), jnp.float32)],
        compiler_params=pltpu.CompilerParams(vmem_limit_bytes=SMALL),
        cost_estimate=pl.CostEstimate(flops=2 * samples * snps * TILE, bytes_accessed=2 * samples * snps, transcendentals=0),
        name="project",
    )(*parts, inverse, order, standard, kept)


PANEL = 16


def inverse_kernel(own, other, order, out, left, right):
    height = TILE // GROUPS
    for half, source in enumerate((own, other)):
        for row in range(GROUPS // 2):
            start = pl.multiple_of(order[BLOCKS + half * (GROUPS // 2) + row] * height, height)
            left[pl.ds(start, height), :] = source[row * height : (row + 1) * height, :]
    lanes = lax.broadcasted_iota(jnp.int32, (TILE, TILE), 1)
    subs = lax.broadcasted_iota(jnp.int32, (TILE, TILE), 0)
    right[...] = jnp.where(lanes == subs, 1.0, 0.0)
    panel_rows = lax.broadcasted_iota(jnp.int32, (PANEL, TILE), 0)
    for start in range(0, TILE, PANEL):
        stop = start + PANEL
        upper = left[start:stop, :]
        done = right[start:stop, :]
        columns = [
            jnp.broadcast_to(upper[:, start + j : start + j + 1], (PANEL, TILE)) for j in range(PANEL)
        ]
        for k in range(PANEL):
            pivot = columns[k][k : k + 1, :]
            root = lax.rsqrt(pivot)
            below = jnp.where(panel_rows > k, columns[k] * (root * root), 0.0)
            for j in range(k + 1, PANEL):
                columns[j] = columns[j] - below * columns[j][k : k + 1, :]
            factor = jnp.where(panel_rows == k, root, 1.0)
            upper = upper * factor - below * upper[k : k + 1, :]
            done = done * factor - below * done[k : k + 1, :]
        out[start:stop, :] = done
        if stop < TILE:
            both = lax.dot_general(
                upper,
                jnp.concatenate([upper, done], axis=1),
                (((0,), (0,)), ((), ())),
                precision=lax.Precision.HIGHEST,
                preferred_element_type=jnp.float32,
            )
            left[stop:, :] -= both[stop:, :TILE]
            right[stop:, :] -= both[stop:, TILE:]


def invert_factor(own, other, order):
    return pl.pallas_call(
        inverse_kernel,
        in_specs=[ON_CHIP, ON_CHIP, SCALARS],
        out_specs=ON_CHIP,
        out_shape=jax.ShapeDtypeStruct((TILE, TILE), jnp.float32),
        scratch_shapes=[pltpu.VMEM((TILE, TILE), jnp.float32), pltpu.VMEM((TILE, TILE), jnp.float32)],
        compiler_params=pltpu.CompilerParams(vmem_limit_bytes=SMALL),
        cost_estimate=pl.CostEstimate(flops=2_000_000_000, bytes_accessed=16_000_000, transcendentals=0),
        name="invert_factor",
    )(own, other, order)


def pick_kernel(keep, projected, chosen):
    samples = projected.shape[0]
    lanes = lax.broadcasted_iota(jnp.int32, (TILE, samples), 1).astype(jnp.float32)
    for j in range(keep.shape[0]):
        row = jnp.broadcast_to(keep[j : j + 1, :].astype(jnp.float32), (TILE, TILE)).T
        pick = jnp.where(lanes == jnp.tile(row, (1, samples // TILE)), 1.0, 0.0).astype(jnp.bfloat16)
        value = jnp.dot(pick, projected[...], preferred_element_type=jnp.float32)
        chosen[j * TILE : (j + 1) * TILE, :] = value.astype(jnp.bfloat16)


def pick_rows(keep, projected):
    return pl.pallas_call(
        pick_kernel,
        in_specs=[ON_CHIP, ON_CHIP],
        out_specs=ON_CHIP,
        out_shape=jax.ShapeDtypeStruct((keep.shape[0] * TILE, TILE), jnp.bfloat16),
        compiler_params=pltpu.CompilerParams(vmem_limit_bytes=SMALL),
        cost_estimate=pl.CostEstimate(flops=500_000_000, bytes_accessed=4_000_000, transcendentals=0),
        name="pick_rows",
    )(keep, projected)


def scores_kernel(scale, chosen, inverse, scores):
    high, low = split(inverse[...])
    dims = (((1,), (1,)), ((), ()))
    value = lax.dot_general(chosen[...], high, dims, preferred_element_type=jnp.float32)
    value = value + lax.dot_general(chosen[...], low, dims, preferred_element_type=jnp.float32)
    scores[...] = value * scale


def score(scale, chosen, inverse):
    return pl.pallas_call(
        functools.partial(scores_kernel, scale),
        out_shape=jax.ShapeDtypeStruct(chosen.shape, jnp.float32),
        compiler_params=pltpu.CompilerParams(vmem_limit_bytes=SMALL),
        cost_estimate=pl.CostEstimate(flops=500_000_000, bytes_accessed=4_000_000, transcendentals=0),
        name="score",
    )(chosen, inverse)


def loadings_kernel(pieces, order, *refs):
    parts = refs[:pieces]
    inverse, loadings = refs[pieces:]
    high, low = split(inverse[...])
    position = 0
    for part in parts:
        for row in range(0, part.shape[0], TILE):
            start = pl.multiple_of(order[position] * TILE, TILE)
            loadings[pl.ds(start, TILE), :] = product(part[row : row + TILE, :], high, low)
            position += 1


def load(order, parts, inverse):
    count = sum(part.shape[0] for part in parts)
    return pl.pallas_call(
        functools.partial(loadings_kernel, len(parts)),
        in_specs=[pl.BlockSpec(memory_space=pltpu.SMEM)] + [pl.BlockSpec(memory_space=pltpu.VMEM)] * (len(parts) + 1),
        out_shape=jax.ShapeDtypeStruct((count, TILE), jnp.float32),
        compiler_params=pltpu.CompilerParams(vmem_limit_bytes=VMEM),
        cost_estimate=pl.CostEstimate(flops=100_000_000, bytes_accessed=1_000_000, transcendentals=0),
        name="load",
    )(order, *parts, inverse)


def span(rows, *terms):
    return (rows, terms)


def scatter_sum(turned, standard, gram):
    four = 4 * TILE
    eight = 8 * TILE
    slot = TILE // GROUPS
    half = TILE // 2
    far = exchange(totals(turned, standard, 24, 32, gram), core_mask)
    close = exchange(totals(turned, standard, 16, 24), core_mask)
    own = totals(turned, standard, 0, 16)
    (send,) = combine(
        [own, far, gram],
        [[span(four, (0, eight + four), (1, four)), span(half, (2, 0), (1, eight))]],
    )
    first = exchange(send, first_mask)
    (send_rest,) = combine([own, far], [[span(four, (0, eight), (1, 0))]])
    rest = exchange(send_rest, first_mask)
    (send_next,) = combine(
        [own, close, first, send],
        [[span(four, (0, four), (1, four), (2, 0)), span(half, (3, four), (2, four))]],
    )
    second = exchange(send_next, second_mask)
    packets = combine(
        [own, close, rest, second, send_next],
        [
            [
                span(TILE, (0, q * TILE), (1, q * TILE), (2, q * TILE), (3, q * TILE)),
                span(slot, (4, four + q * slot), (3, four + q * slot)),
            ]
            for q in range(4)
        ],
    )
    return packets


def along_z(value):
    return [exchange(value, lambda d, q=q: q << 3) for q in range(1, 4)]


def finish_sum(packets):
    size = TILE + TILE // GROUPS
    arrived = [exchange(packets[q], lambda d, q=q: q << 3) for q in range(1, 4)]
    (total,) = combine([packets[0]] + arrived, [[span(size, *((q, 0) for q in range(4)))]])
    bit = BLOCKS
    while bit < lax.axis_size(AXES):
        total = total + exchange(total, lambda d, bit=bit: bit)
        bit *= 2
    return total


def gather_near(total):
    arrived = [total] + along_z(total)
    slot = TILE // GROUPS
    return combine(
        arrived,
        [[span(TILE, (q, 0)) for q in range(4)], [span(slot, (q, TILE)) for q in range(4)]],
    )


def on_device(dosage, keep_rows, allele_counts, projection):
    groups = lax.axis_size(AXES)
    samples_total = dosage.shape[0] * groups
    kept_total = keep_rows.shape[0] * groups
    device = lax.axis_index("wide") * lax.axis_size("narrow") + lax.axis_index("narrow")
    order = jnp.concatenate([block_order(device), group_order(device)])
    keep = keep_rows.reshape(-1, TILE)
    counts = allele_counts.reshape(-1, TILE)
    standard, _, turned, gram, kept = standardize(samples_total, order, dosage, keep, counts, projection)
    total = finish_sum(scatter_sum(turned, standard, gram))
    near, own_gram = gather_near(total)
    across = exchange(near, second_mask)
    along = exchange(near, first_mask)
    inverse = invert_factor(own_gram, exchange(own_gram, core_mask), order)
    across, inverse = lax.optimization_barrier((across, inverse))
    plane = [near, across, along, exchange(across, first_mask)]
    parts = plane + [exchange(part, core_mask) for part in plane]
    projected, turned, gram = project(parts, inverse, order, standard, kept)
    packets = scatter_sum(turned, standard, gram)
    total = finish_sum(packets)
    chosen = pick_rows(keep, projected)
    total, chosen = lax.optimization_barrier((total, chosen))
    near, own_gram = gather_near(total)
    parts = [near, exchange(near, lambda d: 4)]
    inverse = invert_factor(own_gram, exchange(own_gram, core_mask), order)
    scores = score(math.sqrt(kept_total), chosen, inverse)
    position = lax.iota(jnp.int32, 8)
    place = (lax.axis_index("wide") & 7) ^ (((position & 3) << 1) | (position >> 2))
    loadings = load(place, parts, inverse)
    return (scores, loadings)


def solution(mesh):
    in_specs = (P(AXES, None), P(AXES), P(), P())
    out_specs = (P(AXES, None), P("narrow", None))
    return jax.shard_map(
        on_device, mesh=mesh, in_specs=in_specs, out_specs=out_specs, check_vma=False
    )
```

time: 149 us -> 115 us (0.77)
  Pallas kernels: 47.1 us -> 31 us
  waiting for transfers between devices: 62.5 us -> 46.8 us
  local copies, waits for them, and re-layouts: 2.67 us -> 0.01 us
    ppermute x28 -> x32, waiting for transfers between devices: 62.5 us -> 46.8 us  [exchange(): lax.ppermute(value, AXES, [(d, d ^ mask_of(d)) for d in range(count)])]
    pallas_call x8 -> x23, Pallas kernels: 42.7 us -> 28 us  [the longest x2 10.9 us: invert_factor(): pl.pallas_call(inverse_kernel, in_specs=[ON_CHIP, ON_CHIP, SCALARS], out_...]
    unnamed x8 -> x2, local copies, waits for them, and re-layouts: 2.63 us -> 0.01 us
    ppermute x28 -> x32, starting transfers between devices: 34.4 us -> 35.8 us  [exchange(): lax.ppermute(value, AXES, [(d, d ^ mask_of(d)) for d in range(count)])]
  transfers between devices with their start and end apart: 28 -> 32, of which waited for: 16 -> 18; matrix products, arithmetic and copies ran while one was open for 0% -> 0% of each run, Pallas kernels for 13% -> 14%
where the time goes in v2:
time: 115 us
  waiting for transfers between devices  46.8 us (41%)
  starting transfers between devices  35.8 us (31%)
  Pallas kernels  31 us (27%)
    ppermute x32, waiting for transfers between devices, exchange(): lax.ppermute(value, AXES, [(d, d ^ mask_of(d)) for d in range(count)])  46.8 us
    ppermute x32, starting transfers between devices, exchange(): lax.ppermute(value, AXES, [(d, d ^ mask_of(d)) for d in range(count)])  35.8 us
    pallas_call x2, Pallas kernels, invert_factor(): pl.pallas_call(inverse_kernel, in_specs=[ON_CHIP, ON_CHIP, SCALARS], out_...  10.9 us
    pallas_call x1, Pallas kernels, standardize(): pl.pallas_call(functools.partial(standard_kernel, samples_total), in_spec...  7.92 us
    pallas_call x1, Pallas kernels, project(): pl.pallas_call(functools.partial(project_kernel, len(parts)), in_specs=[O...  4.16 us
    pallas_call x6, Pallas kernels, totals(): pl.pallas_call(functools.partial(totals_kernel, low, high), in_specs=[ON_...  3.86 us
  transfers between devices with their start and end apart: 32, of which 18 were waited for; matrix products, arithmetic and copies ran while one was open for 0% of the time, Pallas kernels for 14%

profile of v2, /device:TPU:0, one launch (start us, length us, event | category | flops | bytes accessed | tf_op | source)
XLA Modules:
  0.0 114.6 jit_solution(2993380465023249826)
XLA Ops:
  0.7 7.9 %standardize.1 = (bf16[1024,4096]{1,0:T(8,128)(2,1)S(1)}, bf16[1024,128]{1,0:T(8,128)(2,1)}, bf16[128,1024]{1,0:T(8,128)(2,1)S(1)}, f32[128,128]{1,0:T(8,128)S(1)}, f32[1024,128]{1,0:T(8,128)S(1)}) custom-call(s32[40]{0:T(128)S(1)} %pad_add_fusion.order.refs_9_, bf16[1024,4096]{1,0:T(8,128)(2,1)} %dosage.1, s32[7,128]{1,0:T(8,128)} %bitcast.2, ...), custom_call_target="tpu_custom_call" | custom-call | flops 1073741824 | bytes 16777216 | tf_op jit(solution)/shard_map/standardize/pallas_call | solution.py:137
  11.4 2.9 %collective-permute-start.3 = (f32[576,128]{1,0:T(8,128)S(1)}, f32[576,128]{1,0:T(8,128)S(1)}, u32[]{:S(2)}, u32[]{:S(2)}) collective-permute-start(f32[576,128]{1,0:T(8,128)S(1)} %combine.13.refs_3_), channel_id=1, source_target_pairs={{0,4},{1,3},{2,6},{3,1},{4,0},{5,7},{6,2},{7,5},{8,12},{9,11},{10,... | collective-permute-start | bytes 884744 | tf_op jit(solution)/shard_map/ppermute | solution.py:51
  14.3 4.7 %collective-permute-done.3.refs_2_ = f32[576,128]{1,0:T(8,128)S(1)} collective-permute-done((f32[576,128]{1,0:T(8,128)S(1)}, f32[576,128]{1,0:T(8,128)S(1)}, u32[]{:S(2)}, u32[]{:S(2)}) %collective-permute-start.3) | collective-permute-done | bytes 294944 | tf_op jit(solution)/shard_map/ppermute | solution.py:51
  19.1 2.1 %collective-permute-start.4 = (f32[576,128]{1,0:T(8,128)S(1)}, f32[576,128]{1,0:T(8,128)S(1)}, u32[]{:S(2)}, u32[]{:S(2)}) collective-permute-start(f32[576,128]{1,0:T(8,128)S(1)} %combine.14.refs_4_), channel_id=1, source_target_pairs={{0,2},{1,5},{2,0},{3,7},{4,6},{5,1},{6,4},{7,3},{8,10},{9,13},{10,... | collective-permute-start | bytes 884744 | tf_op jit(solution)/shard_map/ppermute | solution.py:51
  22.8 4.9 %collective-permute-done.2.refs_2_ = f32[512,128]{1,0:T(8,128)S(1)} collective-permute-done((f32[512,128]{1,0:T(8,128)S(1)}, f32[512,128]{1,0:T(8,128)S(1)}, u32[]{:S(2)}, u32[]{:S(2)}) %collective-permute-start.2) | collective-permute-done | bytes 262176 | tf_op jit(solution)/shard_map/ppermute | solution.py:51
  30.5 2.6 %collective-permute-start.6 = (f32[144,128]{1,0:T(8,128)S(1)}, f32[144,128]{1,0:T(8,128)S(1)}, u32[]{:S(2)}, u32[]{:S(2)}) collective-permute-start(f32[144,128]{1,0:T(8,128)S(1)} %get-tuple-element.30), channel_id=1, source_target_pairs={{0,16},{1,17},{2,18},{3,19},{4,20},{5,21},{6,22},{7,23},{8,24},{9,... | collective-permute-start | bytes 221192 | tf_op jit(solution)/shard_map/ppermute | solution.py:51
  33.2 4.7 %collective-permute-done.6.refs_2_ = f32[144,128]{1,0:T(8,128)S(1)} collective-permute-done((f32[144,128]{1,0:T(8,128)S(1)}, f32[144,128]{1,0:T(8,128)S(1)}, u32[]{:S(2)}, u32[]{:S(2)}) %collective-permute-start.6) | collective-permute-done | bytes 73760 | tf_op jit(solution)/shard_map/ppermute | solution.py:51
  39.4 1.9 %collective-permute-start.10 = (f32[144,128]{1,0:T(8,128)S(1)}, f32[144,128]{1,0:T(8,128)S(1)}, u32[]{:S(2)}, u32[]{:S(2)}) collective-permute-start(f32[144,128]{1,0:T(8,128)S(1)} %combine.16.refs_0_), channel_id=1, source_target_pairs={{0,24},{1,25},{2,26},{3,27},{4,28},{5,29},{6,30},{7,31},{8,16},{9,... | collective-permute-start | bytes 221192 | tf_op jit(solution)/shard_map/ppermute | solution.py:51
  41.6 2.3 %collective-permute-start.8 = (f32[144,128]{1,0:T(8,128)S(1)}, f32[144,128]{1,0:T(8,128)S(1)}, u32[]{:S(2)}, u32[]{:S(2)}) collective-permute-start(f32[144,128]{1,0:T(8,128)S(1)} %combine.16.refs_0_), channel_id=1, source_target_pairs={{0,8},{1,9},{2,10},{3,11},{4,12},{5,13},{6,14},{7,15},{8,0},{9,1},... | collective-permute-start | bytes 221192 | tf_op jit(solution)/shard_map/ppermute | solution.py:51
  43.9 1.8 %collective-permute-done.10.refs_3_ = f32[144,128]{1,0:T(8,128)S(1)} collective-permute-done((f32[144,128]{1,0:T(8,128)S(1)}, f32[144,128]{1,0:T(8,128)S(1)}, u32[]{:S(2)}, u32[]{:S(2)}) %collective-permute-start.10) | collective-permute-done | bytes 73760 | tf_op jit(solution)/shard_map/ppermute | solution.py:51
  50.1 5.5 %invert_factor.2.refs_8_ = f32[128,128]{1,0:T(8,128)S(1)} custom-call(f32[64,128]{1,0:T(8,128)S(1)} %get-tuple-element.33.own, f32[64,128]{1,0:T(8,128)S(1)} %collective-permute-done.12.other, s32[40]{0:T(128)S(1)} %pad_add_fusion.order.refs_9_), custom_call_target="tpu_custom_call" | custom-call | flops 2000000000 | bytes 16000000 | tf_op jit(solution)/shard_map/invert_factor/pallas_call | solution.py:295
  57.0 5.0 %collective-permute-done.14.refs_3_ = f32[512,128]{1,0:T(8,128)S(1)} collective-permute-done((f32[512,128]{1,0:T(8,128)S(1)}, f32[512,128]{1,0:T(8,128)S(1)}, u32[]{:S(2)}, u32[]{:S(2)}) %collective-permute-start.14) | collective-permute-done | bytes 262176 | tf_op jit(solution)/shard_map/ppermute | solution.py:51
  63.5 4.2 %project.1 = (bf16[1024,128]{1,0:T(8,128)(2,1)S(1)}, bf16[128,1024]{1,0:T(8,128)(2,1)S(1)}, f32[128,128]{1,0:T(8,128)S(1)}) custom-call(f32[512,128]{1,0:T(8,128)S(1)} %get-tuple-element.32.refs_0_, f32[512,128]{1,0:T(8,128)S(1)} %collective-permute-done.11.refs_1_, f32[512,128]{1,0:T(8,128)S(1)} %collective-permute-done.13.refs_2_, ...), custom_call_target="tpu_custom_call" | custom-call | flops 1073741824 | bytes 8388608 | tf_op jit(solution)/shard_map/project/pallas_call | solution.py:236
  71.2 5.9 %collective-permute-done.22.refs_2_ = f32[576,128]{1,0:T(8,128)S(1)} collective-permute-done((f32[576,128]{1,0:T(8,128)S(1)}, f32[576,128]{1,0:T(8,128)S(1)}, u32[]{:S(2)}, u32[]{:S(2)}) %collective-permute-start.22) | collective-permute-done | bytes 294944 | tf_op jit(solution)/shard_map/ppermute | solution.py:51
  77.2 2.5 %collective-permute-start.23 = (f32[576,128]{1,0:T(8,128)S(1)}, f32[576,128]{1,0:T(8,128)S(1)}, u32[]{:S(2)}, u32[]{:S(2)}) collective-permute-start(f32[576,128]{1,0:T(8,128)S(1)} %combine.20.refs_4_), channel_id=1, source_target_pairs={{0,2},{1,5},{2,0},{3,7},{4,6},{5,1},{6,4},{7,3},{8,10},{9,13},{10,... | collective-permute-start | bytes 884744 | tf_op jit(solution)/shard_map/ppermute | solution.py:51
  80.2 5.9 %collective-permute-done.21.refs_2_ = f32[512,128]{1,0:T(8,128)S(1)} collective-permute-done((f32[512,128]{1,0:T(8,128)S(1)}, f32[512,128]{1,0:T(8,128)S(1)}, u32[]{:S(2)}, u32[]{:S(2)}) %collective-permute-start.21) | collective-permute-done | bytes 262176 | tf_op jit(solution)/shard_map/ppermute | solution.py:51
  88.8 1.8 %collective-permute-start.26 = (f32[144,128]{1,0:T(8,128)S(1)}, f32[144,128]{1,0:T(8,128)S(1)}, u32[]{:S(2)}, u32[]{:S(2)}) collective-permute-start(f32[144,128]{1,0:T(8,128)S(1)} %get-tuple-element.42), channel_id=1, source_target_pairs={{0,24},{1,25},{2,26},{3,27},{4,28},{5,29},{6,30},{7,31},{8,16},{9,... | collective-permute-start | bytes 221192 | tf_op jit(solution)/shard_map/ppermute | solution.py:51
  91.4 2.5 %collective-permute-done.25.refs_2_ = f32[144,128]{1,0:T(8,128)S(1)} collective-permute-done((f32[144,128]{1,0:T(8,128)S(1)}, f32[144,128]{1,0:T(8,128)S(1)}, u32[]{:S(2)}, u32[]{:S(2)}) %collective-permute-start.25) | collective-permute-done | bytes 73760 | tf_op jit(solution)/shard_map/ppermute | solution.py:51
  95.1 1.9 %collective-permute-start.29 = (f32[144,128]{1,0:T(8,128)S(1)}, f32[144,128]{1,0:T(8,128)S(1)}, u32[]{:S(2)}, u32[]{:S(2)}) collective-permute-start(f32[144,128]{1,0:T(8,128)S(1)} %combine.22.refs_0_), channel_id=1, source_target_pairs={{0,24},{1,25},{2,26},{3,27},{4,28},{5,29},{6,30},{7,31},{8,16},{9,... | collective-permute-start | bytes 221192 | tf_op jit(solution)/shard_map/ppermute | solution.py:51
  97.5 2.0 %collective-permute-start.27 = (f32[144,128]{1,0:T(8,128)S(1)}, f32[144,128]{1,0:T(8,128)S(1)}, u32[]{:S(2)}, u32[]{:S(2)}) collective-permute-start(f32[144,128]{1,0:T(8,128)S(1)} %combine.22.refs_0_), channel_id=1, source_target_pairs={{0,8},{1,9},{2,10},{3,11},{4,12},{5,13},{6,14},{7,15},{8,0},{9,1},... | collective-permute-start | bytes 221192 | tf_op jit(solution)/shard_map/ppermute | solution.py:51
  99.6 1.8 %collective-permute-done.29.refs_3_ = f32[144,128]{1,0:T(8,128)S(1)} collective-permute-done((f32[144,128]{1,0:T(8,128)S(1)}, f32[144,128]{1,0:T(8,128)S(1)}, u32[]{:S(2)}, u32[]{:S(2)}) %collective-permute-start.29) | collective-permute-done | bytes 73760 | tf_op jit(solution)/shard_map/ppermute | solution.py:51
  103.0 2.7 %collective-permute-start.31 = (f32[512,128]{1,0:T(8,128)S(1)}, f32[512,128]{1,0:T(8,128)S(1)}, u32[]{:S(2)}, u32[]{:S(2)}) collective-permute-start(f32[512,128]{1,0:T(8,128)S(1)} %get-tuple-element.47.refs_0_), channel_id=1, source_target_pairs={{0,4},{1,5},{2,6},{3,7},{4,0},{5,1},{6,2},{7,3},{8,12},{9,13},{10,... | collective-permute-start | bytes 786440 | tf_op jit(solution)/shard_map/ppermute | solution.py:51
  105.8 5.5 %invert_factor.3.inverse.refs_2_ = f32[128,128]{1,0:T(8,128)S(1)} custom-call(f32[64,128]{1,0:T(8,128)S(1)} %get-tuple-element.46.own, f32[64,128]{1,0:T(8,128)S(1)} %collective-permute-done.30.other, s32[40]{0:T(128)S(1)} %pad_add_fusion.order.refs_9_), custom_call_target="tpu_custom_call" | custom-call | flops 2000000000 | bytes 16000000 | tf_op jit(solution)/shard_map/invert_factor/pallas_call | solution.py:295
  112.6 2.0 %load.1 = f32[1024,128]{1,0:T(8,128)} custom-call(s32[8]{0:T(128)S(1)} %or_xor_fusion.order, f32[512,128]{1,0:T(8,128)S(1)} %get-tuple-element.47.refs_0_, f32[512,128]{1,0:T(8,128)S(1)} %collective-permute-done.31.refs_1_, f32[128,128]{1,0:T(8,128)S(1)} %invert_factor.3.inverse.refs_2_), custom_call_target="tpu_custom_call" | custom-call | flops 100000000 | bytes 1000000 | tf_op jit(solution)/shard_map/load/pallas_call | solution.py:361
  (71 shorter events, 28.9 us)
Async XLA Ops:
  11.4 7.6 %collective-permute-start.3 = (f32[576,128]{1,0:T(8,128)S(1)}, f32[576,128]{1,0:T(8,128)S(1)}, u32[]{:S(2)}, u32[]{:S(2)}) collective-permute-start(f32[576,128]{1,0:T(8,128)S(1)} %combine.13.refs_3_), channel_id=1, source_target_pairs={{0,4},{1,3},{2,6},{3,1},{4,0},{5,7},{6,2},{7,5},{8,12},{9,11},{10,... | collective-permute-start | bytes 884744 | tf_op jit(solution)/shard_map/ppermute | solution.py:51
  19.1 9.6 %collective-permute-start.4 = (f32[576,128]{1,0:T(8,128)S(1)}, f32[576,128]{1,0:T(8,128)S(1)}, u32[]{:S(2)}, u32[]{:S(2)}) collective-permute-start(f32[576,128]{1,0:T(8,128)S(1)} %combine.14.refs_4_), channel_id=1, source_target_pairs={{0,2},{1,5},{2,0},{3,7},{4,6},{5,1},{6,4},{7,3},{8,10},{9,13},{10,... | collective-permute-start | bytes 884744 | tf_op jit(solution)/shard_map/ppermute | solution.py:51
  21.2 6.4 %collective-permute-start.2 = (f32[512,128]{1,0:T(8,128)S(1)}, f32[512,128]{1,0:T(8,128)S(1)}, u32[]{:S(2)}, u32[]{:S(2)}) collective-permute-start(f32[512,128]{1,0:T(8,128)S(1)} %combine.12), channel_id=1, source_target_pairs={{0,4},{1,3},{2,6},{3,1},{4,0},{5,7},{6,2},{7,5},{8,12},{9,11},{10,... | collective-permute-start | bytes 786440 | tf_op jit(solution)/shard_map/ppermute | solution.py:51
  30.5 7.4 %collective-permute-start.6 = (f32[144,128]{1,0:T(8,128)S(1)}, f32[144,128]{1,0:T(8,128)S(1)}, u32[]{:S(2)}, u32[]{:S(2)}) collective-permute-start(f32[144,128]{1,0:T(8,128)S(1)} %get-tuple-element.30), channel_id=1, source_target_pairs={{0,16},{1,17},{2,18},{3,19},{4,20},{5,21},{6,22},{7,23},{8,24},{9,... | collective-permute-start | bytes 221192 | tf_op jit(solution)/shard_map/ppermute | solution.py:51
  33.1 6.3 %collective-permute-start.7 = (f32[144,128]{1,0:T(8,128)S(1)}, f32[144,128]{1,0:T(8,128)S(1)}, u32[]{:S(2)}, u32[]{:S(2)}) collective-permute-start(f32[144,128]{1,0:T(8,128)S(1)} %get-tuple-element.31), channel_id=1, source_target_pairs={{0,24},{1,25},{2,26},{3,27},{4,28},{5,29},{6,30},{7,31},{8,16},{9,... | collective-permute-start | bytes 221192 | tf_op jit(solution)/shard_map/ppermute | solution.py:51
  39.4 6.2 %collective-permute-start.10 = (f32[144,128]{1,0:T(8,128)S(1)}, f32[144,128]{1,0:T(8,128)S(1)}, u32[]{:S(2)}, u32[]{:S(2)}) collective-permute-start(f32[144,128]{1,0:T(8,128)S(1)} %combine.16.refs_0_), channel_id=1, source_target_pairs={{0,24},{1,25},{2,26},{3,27},{4,28},{5,29},{6,30},{7,31},{8,16},{9,... | collective-permute-start | bytes 221192 | tf_op jit(solution)/shard_map/ppermute | solution.py:51
  41.3 5.9 %collective-permute-start.9 = (f32[144,128]{1,0:T(8,128)S(1)}, f32[144,128]{1,0:T(8,128)S(1)}, u32[]{:S(2)}, u32[]{:S(2)}) collective-permute-start(f32[144,128]{1,0:T(8,128)S(1)} %combine.16.refs_0_), channel_id=1, source_target_pairs={{0,16},{1,17},{2,18},{3,19},{4,20},{5,21},{6,22},{7,23},{8,24},{9,... | collective-permute-start | bytes 221192 | tf_op jit(solution)/shard_map/ppermute | solution.py:51
  41.6 5.7 %collective-permute-start.8 = (f32[144,128]{1,0:T(8,128)S(1)}, f32[144,128]{1,0:T(8,128)S(1)}, u32[]{:S(2)}, u32[]{:S(2)}) collective-permute-start(f32[144,128]{1,0:T(8,128)S(1)} %combine.16.refs_0_), channel_id=1, source_target_pairs={{0,8},{1,9},{2,10},{3,11},{4,12},{5,13},{6,14},{7,15},{8,0},{9,1},... | collective-permute-start | bytes 221192 | tf_op jit(solution)/shard_map/ppermute | solution.py:51
  47.3 8.3 %collective-permute-start.11 = (f32[512,128]{1,0:T(8,128)S(1)}, f32[512,128]{1,0:T(8,128)S(1)}, u32[]{:S(2)}, u32[]{:S(2)}) collective-permute-start(f32[512,128]{1,0:T(8,128)S(1)} %get-tuple-element.32.refs_0_), channel_id=1, source_target_pairs={{0,2},{1,5},{2,0},{3,7},{4,6},{5,1},{6,4},{7,3},{8,10},{9,13},{10,... | collective-permute-start | bytes 786440 | tf_op jit(solution)/shard_map/ppermute | solution.py:51
  48.9 8.1 %collective-permute-start.13 = (f32[512,128]{1,0:T(8,128)S(1)}, f32[512,128]{1,0:T(8,128)S(1)}, u32[]{:S(2)}, u32[]{:S(2)}) collective-permute-start(f32[512,128]{1,0:T(8,128)S(1)} %get-tuple-element.32.refs_0_), channel_id=1, source_target_pairs={{0,4},{1,3},{2,6},{3,1},{4,0},{5,7},{6,2},{7,5},{8,12},{9,11},{10,... | collective-permute-start | bytes 786440 | tf_op jit(solution)/shard_map/ppermute | solution.py:51
  55.6 6.4 %collective-permute-start.14 = (f32[512,128]{1,0:T(8,128)S(1)}, f32[512,128]{1,0:T(8,128)S(1)}, u32[]{:S(2)}, u32[]{:S(2)}) collective-permute-start(f32[512,128]{1,0:T(8,128)S(1)} %collective-permute-done.11.refs_1_), channel_id=1, source_target_pairs={{0,4},{1,3},{2,6},{3,1},{4,0},{5,7},{6,2},{7,5},{8,12},{9,11},{10,... | collective-permute-start | bytes 786440 | tf_op jit(solution)/shard_map/ppermute | solution.py:51
  56.4 5.6 %collective-permute-start.15 = (f32[512,128]{1,0:T(8,128)S(1)}, f32[512,128]{1,0:T(8,128)S(1)}, u32[]{:S(2)}, u32[]{:S(2)}) collective-permute-start(f32[512,128]{1,0:T(8,128)S(1)} %get-tuple-element.32.refs_0_), channel_id=1, source_target_pairs={{0,1},{1,0},{2,3},{3,2},{4,5},{5,4},{6,7},{7,6},{8,9},{9,8},{10,11... | collective-permute-start | bytes 786440 | tf_op jit(solution)/shard_map/ppermute | solution.py:51
  56.4 5.6 %collective-permute-start.16 = (f32[512,128]{1,0:T(8,128)S(1)}, f32[512,128]{1,0:T(8,128)S(1)}, u32[]{:S(2)}, u32[]{:S(2)}) collective-permute-start(f32[512,128]{1,0:T(8,128)S(1)} %collective-permute-done.11.refs_1_), channel_id=1, source_target_pairs={{0,1},{1,0},{2,3},{3,2},{4,5},{5,4},{6,7},{7,6},{8,9},{9,8},{10,11... | collective-permute-start | bytes 786440 | tf_op jit(solution)/shard_map/ppermute | solution.py:51
  57.0 5.0 %collective-permute-start.17 = (f32[512,128]{1,0:T(8,128)S(1)}, f32[512,128]{1,0:T(8,128)S(1)}, u32[]{:S(2)}, u32[]{:S(2)}) collective-permute-start(f32[512,128]{1,0:T(8,128)S(1)} %collective-permute-done.13.refs_2_), channel_id=1, source_target_pairs={{0,1},{1,0},{2,3},{3,2},{4,5},{5,4},{6,7},{7,6},{8,9},{9,8},{10,11... | collective-permute-start | bytes 786440 | tf_op jit(solution)/shard_map/ppermute | solution.py:51
  70.4 6.8 %collective-permute-start.22 = (f32[576,128]{1,0:T(8,128)S(1)}, f32[576,128]{1,0:T(8,128)S(1)}, u32[]{:S(2)}, u32[]{:S(2)}) collective-permute-start(f32[576,128]{1,0:T(8,128)S(1)} %combine.19.refs_3_), channel_id=1, source_target_pairs={{0,4},{1,3},{2,6},{3,1},{4,0},{5,7},{6,2},{7,5},{8,12},{9,11},{10,... | collective-permute-start | bytes 884744 | tf_op jit(solution)/shard_map/ppermute | solution.py:51
  77.2 8.9 %collective-permute-start.23 = (f32[576,128]{1,0:T(8,128)S(1)}, f32[576,128]{1,0:T(8,128)S(1)}, u32[]{:S(2)}, u32[]{:S(2)}) collective-permute-start(f32[576,128]{1,0:T(8,128)S(1)} %combine.20.refs_4_), channel_id=1, source_target_pairs={{0,2},{1,5},{2,0},{3,7},{4,6},{5,1},{6,4},{7,3},{8,10},{9,13},{10,... | collective-permute-start | bytes 884744 | tf_op jit(solution)/shard_map/ppermute | solution.py:51
  79.7 6.4 %collective-permute-start.21 = (f32[512,128]{1,0:T(8,128)S(1)}, f32[512,128]{1,0:T(8,128)S(1)}, u32[]{:S(2)}, u32[]{:S(2)}) collective-permute-start(f32[512,128]{1,0:T(8,128)S(1)} %combine.18), channel_id=1, source_target_pairs={{0,4},{1,3},{2,6},{3,1},{4,0},{5,7},{6,2},{7,5},{8,12},{9,11},{10,... | collective-permute-start | bytes 786440 | tf_op jit(solution)/shard_map/ppermute | solution.py:51
  86.2 5.2 %collective-permute-start.24 = (f32[144,128]{1,0:T(8,128)S(1)}, f32[144,128]{1,0:T(8,128)S(1)}, u32[]{:S(2)}, u32[]{:S(2)}) collective-permute-start(f32[144,128]{1,0:T(8,128)S(1)} %get-tuple-element.40), channel_id=1, source_target_pairs={{0,8},{1,9},{2,10},{3,11},{4,12},{5,13},{6,14},{7,15},{8,0},{9,1},... | collective-permute-start | bytes 221192 | tf_op jit(solution)/shard_map/ppermute | solution.py:51
  87.2 6.6 %collective-permute-start.25 = (f32[144,128]{1,0:T(8,128)S(1)}, f32[144,128]{1,0:T(8,128)S(1)}, u32[]{:S(2)}, u32[]{:S(2)}) collective-permute-start(f32[144,128]{1,0:T(8,128)S(1)} %get-tuple-element.41), channel_id=1, source_target_pairs={{0,16},{1,17},{2,18},{3,19},{4,20},{5,21},{6,22},{7,23},{8,24},{9,... | collective-permute-start | bytes 221192 | tf_op jit(solution)/shard_map/ppermute | solution.py:51
  88.8 6.3 %collective-permute-start.26 = (f32[144,128]{1,0:T(8,128)S(1)}, f32[144,128]{1,0:T(8,128)S(1)}, u32[]{:S(2)}, u32[]{:S(2)}) collective-permute-start(f32[144,128]{1,0:T(8,128)S(1)} %get-tuple-element.42), channel_id=1, source_target_pairs={{0,24},{1,25},{2,26},{3,27},{4,28},{5,29},{6,30},{7,31},{8,16},{9,... | collective-permute-start | bytes 221192 | tf_op jit(solution)/shard_map/ppermute | solution.py:51
  95.1 6.2 %collective-permute-start.29 = (f32[144,128]{1,0:T(8,128)S(1)}, f32[144,128]{1,0:T(8,128)S(1)}, u32[]{:S(2)}, u32[]{:S(2)}) collective-permute-start(f32[144,128]{1,0:T(8,128)S(1)} %combine.22.refs_0_), channel_id=1, source_target_pairs={{0,24},{1,25},{2,26},{3,27},{4,28},{5,29},{6,30},{7,31},{8,16},{9,... | collective-permute-start | bytes 221192 | tf_op jit(solution)/shard_map/ppermute | solution.py:51
  97.0 5.9 %collective-permute-start.28 = (f32[144,128]{1,0:T(8,128)S(1)}, f32[144,128]{1,0:T(8,128)S(1)}, u32[]{:S(2)}, u32[]{:S(2)}) collective-permute-start(f32[144,128]{1,0:T(8,128)S(1)} %combine.22.refs_0_), channel_id=1, source_target_pairs={{0,16},{1,17},{2,18},{3,19},{4,20},{5,21},{6,22},{7,23},{8,24},{9,... | collective-permute-start | bytes 221192 | tf_op jit(solution)/shard_map/ppermute | solution.py:51
  97.5 5.4 %collective-permute-start.27 = (f32[144,128]{1,0:T(8,128)S(1)}, f32[144,128]{1,0:T(8,128)S(1)}, u32[]{:S(2)}, u32[]{:S(2)}) collective-permute-start(f32[144,128]{1,0:T(8,128)S(1)} %combine.22.refs_0_), channel_id=1, source_target_pairs={{0,8},{1,9},{2,10},{3,11},{4,12},{5,13},{6,14},{7,15},{8,0},{9,1},... | collective-permute-start | bytes 221192 | tf_op jit(solution)/shard_map/ppermute | solution.py:51
  103.0 9.6 %collective-permute-start.31 = (f32[512,128]{1,0:T(8,128)S(1)}, f32[512,128]{1,0:T(8,128)S(1)}, u32[]{:S(2)}, u32[]{:S(2)}) collective-permute-start(f32[512,128]{1,0:T(8,128)S(1)} %get-tuple-element.47.refs_0_), channel_id=1, source_target_pairs={{0,4},{1,5},{2,6},{3,7},{4,0},{5,1},{6,2},{7,3},{8,12},{9,13},{10,... | collective-permute-start | bytes 786440 | tf_op jit(solution)/shard_map/ppermute | solution.py:51
  (9 other events, 42.0 us)

commit v3 on v2

--- a/solution.py
+++ b/solution.py
@@ -15,12 +15,18 @@
 VMEM = 28 * 1024 * 1024
 SMALL = 16 * 1024 * 1024
 GROUPS = 8
+HALF = TILE // 2
 
 
 def split(value):
     high = value.astype(jnp.bfloat16)
     low = (value - high.astype(jnp.float32)).astype(jnp.bfloat16)
     return high, low
+
+
+def thirds(value):
+    high = value.astype(jnp.bfloat16)
+    return (high,) + split(value - high.astype(jnp.float32))
 
 
 def product(left, right_high, right_low):
@@ -109,15 +115,19 @@
             scale = table[1, pl.ds(block, 1), :]
             value = rows_in[slab, pl.ds(pl.multiple_of(block * TILE, TILE), TILE)].astype(jnp.float32)
             standard[slab, p * TILE : (p + 1) * TILE] = ((value - center) * scale).astype(jnp.bfloat16)
-    project_rows(standard, basis, kept, projected, turned, whole)
+    value = jnp.dot(standard[...], basis[...], preferred_element_type=jnp.float32)
+    finish_rows(value, kept, projected, turned, whole)
+    share_gram(order, whole, gram)
+
+
+def share_gram(order, whole, gram):
     height = TILE // GROUPS
     for place in range(GROUPS):
         start = pl.multiple_of(order[BLOCKS + place] * height, height)
         gram[place * height : (place + 1) * height, :] = whole[pl.ds(start, height), :]
 
 
-def project_rows(standard, basis, kept, projected, turned, gram):
-    value = jnp.dot(standard[...], basis[...], preferred_element_type=jnp.float32)
+def finish_rows(value, kept, projected, turned, gram):
     value = jnp.where(kept[...] > 0.0, value, 0.0)
     low = value.astype(jnp.bfloat16)
     low_turned = value.T.astype(jnp.bfloat16)
@@ -215,54 +225,85 @@
     )(*arrays)
 
 
-def project_kernel(pieces, *refs):
-    parts = refs[:pieces]
-    inverse, order, standard, kept, projected, turned, gram, basis, whole = refs[pieces:]
+def apply_inverse(parts, inverse, basis):
     high, low = split(inverse[...])
     start = 0
     for part in parts:
         size = part.shape[0]
         basis[start : start + size, :] = product(part[...], high, low).astype(jnp.bfloat16)
         start += size
-    project_rows(standard, basis, kept, projected, turned, whole)
-    height = TILE // GROUPS
-    for place in range(GROUPS):
-        start = pl.multiple_of(order[BLOCKS + place] * height, height)
-        gram[place * height : (place + 1) * height, :] = whole[pl.ds(start, height), :]
-
-
-def project(parts, inverse, order, standard, kept):
-    samples, snps = standard.shape
-    return pl.pallas_call(
-        functools.partial(project_kernel, len(parts)),
-        in_specs=[ON_CHIP] * (len(parts) + 1) + [SCALARS, ON_CHIP, ON_CHIP],
+
+
+def add_products(standard, basis, base, value):
+    row = 0
+    for first, count in base:
+        size = count * TILE
+        term = jnp.dot(
+            standard[:, first * TILE : first * TILE + size],
+            basis[row : row + size, :],
+            preferred_element_type=jnp.float32,
+        )
+        value = term if value is None else value + term
+        row += size
+    return value
+
+
+def begin_kernel(pieces, base, *refs):
+    parts = refs[:pieces]
+    inverse, standard, out, basis = refs[pieces:]
+    apply_inverse(parts, inverse, basis)
+    out[...] = add_products(standard, basis, base, None)
+
+
+def begin_project(parts, base, inverse, standard):
+    samples = standard.shape[0]
+    rows = sum(part.shape[0] for part in parts)
+    return pl.pallas_call(
+        functools.partial(begin_kernel, len(parts), base),
+        in_specs=[ON_CHIP] * (len(parts) + 2),
+        out_specs=ON_CHIP,
+        out_shape=jax.ShapeDtypeStruct((samples, TILE), jnp.float32),
+        scratch_shapes=[pltpu.VMEM((rows, TILE), jnp.bfloat16)],
+        compiler_params=pltpu.CompilerParams(vmem_limit_bytes=SMALL),
+        cost_estimate=pl.CostEstimate(flops=2 * samples * rows * TILE, bytes_accessed=2 * samples * rows, transcendentals=0),
+        name="begin_project",
+    )(*parts, inverse, standard)
+
+
+def project_kernel(pieces, base, *refs):
+    parts = refs[:pieces]
+    begun, inverse, order, standard, kept, projected, turned, gram, basis, whole = refs[pieces:]
+    apply_inverse(parts, inverse, basis)
+    value = add_products(standard, basis, base, begun[...])
+    finish_rows(value, kept, projected, turned, whole)
+    share_gram(order, whole, gram)
+
+
+def project(parts, base, begun, inverse, order, standard, kept):
+    samples = standard.shape[0]
+    rows = sum(part.shape[0] for part in parts)
+    return pl.pallas_call(
+        functools.partial(project_kernel, len(parts), base),
+        in_specs=[ON_CHIP] * (len(parts) + 2) + [SCALARS, ON_CHIP, ON_CHIP],
         out_specs=[ON_CHIP] * 3,
         out_shape=[
             jax.ShapeDtypeStruct((samples, TILE), jnp.bfloat16),
             jax.ShapeDtypeStruct((TILE, samples), jnp.bfloat16),
             jax.ShapeDtypeStruct((TILE, TILE), jnp.float32),
         ],
-        scratch_shapes=[pltpu.VMEM((snps, TILE), jnp.bfloat16), pltpu.VMEM((TILE, TILE), jnp.float32)],
-        compiler_params=pltpu.CompilerParams(vmem_limit_bytes=SMALL),
-        cost_estimate=pl.CostEstimate(flops=2 * samples * snps * TILE, bytes_accessed=2 * samples * snps, transcendentals=0),
+        scratch_shapes=[pltpu.VMEM((rows, TILE), jnp.bfloat16), pltpu.VMEM((TILE, TILE), jnp.float32)],
+        compiler_params=pltpu.CompilerParams(vmem_limit_bytes=SMALL),
+        cost_estimate=pl.CostEstimate(flops=2 * samples * rows * TILE, bytes_accessed=2 * samples * rows, transcendentals=0),
         name="project",
-    )(*parts, inverse, order, standard, kept)
+    )(*parts, begun, inverse, order, standard, kept)
 
 
 PANEL = 16
 
 
-def inverse_kernel(own, other, order, out, left, right):
-    height = TILE // GROUPS
-    for half, source in enumerate((own, other)):
-        for row in range(GROUPS // 2):
-            start = pl.multiple_of(order[BLOCKS + half * (GROUPS // 2) + row] * height, height)
-            left[pl.ds(start, height), :] = source[row * height : (row + 1) * height, :]
-    lanes = lax.broadcasted_iota(jnp.int32, (TILE, TILE), 1)
-    subs = lax.broadcasted_iota(jnp.int32, (TILE, TILE), 0)
-    right[...] = jnp.where(lanes == subs, 1.0, 0.0)
+def eliminate(first, last, left, right, out):
     panel_rows = lax.broadcasted_iota(jnp.int32, (PANEL, TILE), 0)
-    for start in range(0, TILE, PANEL):
+    for start in range(first, last, PANEL):
         stop = start + PANEL
         upper = left[start:stop, :]
         done = right[start:stop, :]
@@ -280,28 +321,68 @@
             done = done * factor - below * done[k : k + 1, :]
         out[start:stop, :] = done
         if stop < TILE:
+            left_parts = thirds(upper)
+            right_parts = thirds(jnp.concatenate([upper, done], axis=1))
+            pairs = ((0, 0), (0, 1), (1, 0), (0, 2), (1, 1), (2, 0))
             both = lax.dot_general(
-                upper,
-                jnp.concatenate([upper, done], axis=1),
+                jnp.concatenate([left_parts[i] for i, _ in pairs], axis=0),
+                jnp.concatenate([right_parts[j] for _, j in pairs], axis=0),
                 (((0,), (0,)), ((), ())),
-                precision=lax.Precision.HIGHEST,
                 preferred_element_type=jnp.float32,
             )
             left[stop:, :] -= both[stop:, :TILE]
             right[stop:, :] -= both[stop:, TILE:]
 
 
+def begin_kernel_inverse(last, own, other, order, left, right):
+    height = TILE // GROUPS
+    for half, source in enumerate((own, other)):
+        for row in range(GROUPS // 2):
+            start = pl.multiple_of(order[BLOCKS + half * (GROUPS // 2) + row] * height, height)
+            left[pl.ds(start, height), :] = source[row * height : (row + 1) * height, :]
+    lanes = lax.broadcasted_iota(jnp.int32, (TILE, TILE), 1)
+    subs = lax.broadcasted_iota(jnp.int32, (TILE, TILE), 0)
+    right[...] = jnp.where(lanes == subs, 1.0, 0.0)
+    eliminate(0, last, left, right, right)
+
+
+def end_kernel_inverse(first, left_in, right_in, out, left, right):
+    left[first:, :] = left_in[first:, :]
+    right[first:, :] = right_in[first:, :]
+    out[:first, :] = right_in[:first, :]
+    eliminate(first, TILE, left, right, out)
+
+
+SQUARE = jax.ShapeDtypeStruct((TILE, TILE), jnp.float32)
+
+
+def begin_inverse(last, own, other, order):
+    return pl.pallas_call(
+        functools.partial(begin_kernel_inverse, last),
+        in_specs=[ON_CHIP, ON_CHIP, SCALARS],
+        out_specs=[ON_CHIP, ON_CHIP],
+        out_shape=[SQUARE, SQUARE],
+        compiler_params=pltpu.CompilerParams(vmem_limit_bytes=SMALL),
+        cost_estimate=pl.CostEstimate(flops=1_000_000_000, bytes_accessed=8_000_000, transcendentals=0),
+        name="begin_inverse",
+    )(own, other, order)
+
+
+def end_inverse(first, left, right):
+    return pl.pallas_call(
+        functools.partial(end_kernel_inverse, first),
+        in_specs=[ON_CHIP, ON_CHIP],
+        out_specs=ON_CHIP,
+        out_shape=SQUARE,
+        scratch_shapes=[pltpu.VMEM((TILE, TILE), jnp.float32), pltpu.VMEM((TILE, TILE), jnp.float32)],
+        compiler_params=pltpu.CompilerParams(vmem_limit_bytes=SMALL),
+        cost_estimate=pl.CostEstimate(flops=1_000_000_000, bytes_accessed=8_000_000, transcendentals=0),
+        name="end_inverse",
+    )(left, right)
+
+
 def invert_factor(own, other, order):
-    return pl.pallas_call(
-        inverse_kernel,
-        in_specs=[ON_CHIP, ON_CHIP, SCALARS],
-        out_specs=ON_CHIP,
-        out_shape=jax.ShapeDtypeStruct((TILE, TILE), jnp.float32),
-        scratch_shapes=[pltpu.VMEM((TILE, TILE), jnp.float32), pltpu.VMEM((TILE, TILE), jnp.float32)],
-        compiler_params=pltpu.CompilerParams(vmem_limit_bytes=SMALL),
-        cost_estimate=pl.CostEstimate(flops=2_000_000_000, bytes_accessed=16_000_000, transcendentals=0),
-        name="invert_factor",
-    )(own, other, order)
+    return begin_inverse(TILE, own, other, order)[1]
 
 
 def pick_kernel(keep, projected, chosen):
@@ -348,12 +429,10 @@
     parts = refs[:pieces]
     inverse, loadings = refs[pieces:]
     high, low = split(inverse[...])
-    position = 0
-    for part in parts:
-        for row in range(0, part.shape[0], TILE):
-            start = pl.multiple_of(order[position] * TILE, TILE)
-            loadings[pl.ds(start, TILE), :] = product(part[row : row + TILE, :], high, low)
-            position += 1
+    value = product(jnp.concatenate([part[...] for part in parts], axis=0), high, low)
+    for position in range(value.shape[0] // TILE):
+        start = pl.multiple_of(order[position] * TILE, TILE)
+        loadings[pl.ds(start, TILE), :] = value[position * TILE : (position + 1) * TILE, :]
 
 
 def load(order, parts, inverse):
@@ -377,55 +456,81 @@
     eight = 8 * TILE
     slot = TILE // GROUPS
     half = TILE // 2
+    three = 3 * TILE
     far = exchange(totals(turned, standard, 24, 32, gram), core_mask)
+    upper = totals(turned, standard, 8, 16)
+    send, send_rest = combine(
+        [upper, far, gram],
+        [
+            [span(three, (0, four + TILE), (1, four + TILE)), span(half, (2, 0), (1, eight))],
+            [span(four + TILE, (0, 0), (1, 0))],
+        ],
+    )
+    first = exchange(send, first_mask)
+    rest = exchange(send_rest, first_mask)
     close = exchange(totals(turned, standard, 16, 24), core_mask)
-    own = totals(turned, standard, 0, 16)
-    (send,) = combine(
-        [own, far, gram],
-        [[span(four, (0, eight + four), (1, four)), span(half, (2, 0), (1, eight))]],
-    )
-    first = exchange(send, first_mask)
-    (send_rest,) = combine([own, far], [[span(four, (0, eight), (1, 0))]])
-    rest = exchange(send_rest, first_mask)
+    own = totals(turned, standard, 0, 8)
     (send_next,) = combine(
         [own, close, first, send],
-        [[span(four, (0, four), (1, four), (2, 0)), span(half, (3, four), (2, four))]],
+        [[span(three, (0, four + TILE), (1, four + TILE), (2, 0)), span(half, (3, three), (2, three))]],
     )
     second = exchange(send_next, second_mask)
-    packets = combine(
-        [own, close, rest, second, send_next],
+    (send_last,) = combine([own, close, rest], [[span(TILE, (0, four), (1, four), (2, four))]])
+    last = exchange(send_last, second_mask)
+
+    def share(q):
+        return span(slot, (4, three + q * slot), (3, three + q * slot))
+
+    def packet(q):
+        start = q * TILE
+        return [span(TILE, (0, start), (1, start), (2, start), (3, start - TILE)), share(q)]
+
+    *packets, own_share = combine(
+        [own, close, rest, second, send_next], [packet(q) for q in (3, 2, 1)] + [[share(0)]]
+    )
+    arrived = [exchange(packet, lambda d, q=q: (3 - q) << 3) for q, packet in enumerate(packets)]
+    total, share = combine(
+        [own, close, rest, last, own_share] + arrived,
         [
-            [
-                span(TILE, (0, q * TILE), (1, q * TILE), (2, q * TILE), (3, q * TILE)),
-                span(slot, (4, four + q * slot), (3, four + q * slot)),
-            ]
-            for q in range(4)
+            [span(TILE, *((i, 0) for i in (0, 1, 2, 3, 5, 6, 7)))],
+            [span(slot, (4, 0), (7, TILE), (6, TILE), (5, TILE))],
         ],
     )
-    return packets
+    return across_rest(total), across_rest(share)
+
+
+def across_rest(value):
+    bit = BLOCKS
+    while bit < lax.axis_size(AXES):
+        value = value + exchange(value, lambda d, bit=bit: bit)
+        bit *= 2
+    return value
 
 
 def along_z(value):
     return [exchange(value, lambda d, q=q: q << 3) for q in range(1, 4)]
 
 
-def finish_sum(packets):
-    size = TILE + TILE // GROUPS
-    arrived = [exchange(packets[q], lambda d, q=q: q << 3) for q in range(1, 4)]
-    (total,) = combine([packets[0]] + arrived, [[span(size, *((q, 0) for q in range(4)))]])
-    bit = BLOCKS
-    while bit < lax.axis_size(AXES):
-        total = total + exchange(total, lambda d, bit=bit: bit)
-        bit *= 2
-    return total
-
-
-def gather_near(total):
-    arrived = [total] + along_z(total)
+def gather_near(total, share):
     slot = TILE // GROUPS
+    (packet,) = combine([total, share], [[span(TILE, (0, 0)), span(slot, (1, 0))]])
     return combine(
-        arrived,
+        [packet] + along_z(packet),
         [[span(TILE, (q, 0)) for q in range(4)], [span(slot, (q, TILE)) for q in range(4)]],
+    )
+
+
+def gather_last(total, share, mask):
+    slot = TILE // GROUPS
+    (packet,) = combine([total, share], [[span(TILE, (0, 0)), span(slot, (1, 0))]])
+    arrived = along_z(packet)
+    return combine(
+        [total, share] + arrived + [exchange(total, mask)],
+        [
+            [span(TILE, (i, 0)) for i in (2, 3, 4)],
+            [span(slot, (1, 0))] + [span(slot, (i, TILE)) for i in (2, 3, 4)],
+            [span(TILE, (0, 0)), span(TILE, (5, 0))],
+        ],
     )
 
 
@@ -438,26 +543,32 @@
     keep = keep_rows.reshape(-1, TILE)
     counts = allele_counts.reshape(-1, TILE)
     standard, _, turned, gram, kept = standardize(samples_total, order, dosage, keep, counts, projection)
-    total = finish_sum(scatter_sum(turned, standard, gram))
-    near, own_gram = gather_near(total)
+    total, share = scatter_sum(turned, standard, gram)
+    near, share = gather_near(total, share)
     across = exchange(near, second_mask)
-    along = exchange(near, first_mask)
-    inverse = invert_factor(own_gram, exchange(own_gram, core_mask), order)
-    across, inverse = lax.optimization_barrier((across, inverse))
-    plane = [near, across, along, exchange(across, first_mask)]
-    parts = plane + [exchange(part, core_mask) for part in plane]
-    projected, turned, gram = project(parts, inverse, order, standard, kept)
-    packets = scatter_sum(turned, standard, gram)
-    total = finish_sum(packets)
+    other = exchange(share, core_mask)
+    later, other = lax.optimization_barrier((near, other))
+    along = exchange(later, first_mask)
+    middle = begin_inverse(HALF, share, other, order)
+    across, middle = lax.optimization_barrier((across, middle))
+    corner = exchange(across, first_mask)
+    inverse = end_inverse(HALF, *middle)
+    early = [near, across, along] + [exchange(part, core_mask) for part in (near, across)]
+    begun = begin_project(early, [(0, 4), (4, 4), (8, 4), (16, 4), (20, 4)], inverse, standard)
+    corner, begun = lax.optimization_barrier((corner, begun))
+    late = [exchange(along, core_mask), corner, exchange(corner, core_mask)]
+    ranges = [(24, 4), (12, 4), (28, 4)]
+    projected, turned, gram = project(late, ranges, begun, inverse, order, standard, kept)
+    total, share = scatter_sum(turned, standard, gram)
     chosen = pick_rows(keep, projected)
     total, chosen = lax.optimization_barrier((total, chosen))
-    near, own_gram = gather_near(total)
-    parts = [near, exchange(near, lambda d: 4)]
-    inverse = invert_factor(own_gram, exchange(own_gram, core_mask), order)
+    near, share, corners = gather_last(total, share, lambda d: 4)
+    beside = exchange(near, lambda d: 4)
+    inverse = invert_factor(share, exchange(share, core_mask), order)
     scores = score(math.sqrt(kept_total), chosen, inverse)
-    position = lax.iota(jnp.int32, 8)
+    position = jnp.array([0, 4, 1, 2, 3, 5, 6, 7], jnp.int32)
     place = (lax.axis_index("wide") & 7) ^ (((position & 3) << 1) | (position >> 2))
-    loadings = load(place, parts, inverse)
+    loadings = load(place, [corners, near, beside], inverse)
     return (scores, loadings)
 
 

time: 115 us -> 106 us (0.922)
  waiting for transfers between devices: 46.8 us -> 33.4 us
  starting transfers between devices: 35.8 us -> 41.7 us
  Pallas kernels: 31 us -> 29.5 us
    ppermute x32 -> x35, waiting for transfers between devices: 46.8 us -> 33.4 us  [exchange(): lax.ppermute(value, AXES, [(d, d ^ mask_of(d)) for d in range(count)])]
    ppermute x32 -> x35, starting transfers between devices: 35.8 us -> 41.7 us  [exchange(): lax.ppermute(value, AXES, [(d, d ^ mask_of(d)) for d in range(count)])]
    pallas_call x3 -> x5, Pallas kernels: 15.1 us -> 13.2 us  [the longest x2 6.93 us: begin_inverse(): pl.pallas_call(functools.partial(begin_kernel_inverse, last), in_specs=[O...]
    pallas_call x6 -> x8, Pallas kernels: 3.86 us -> 4.42 us  [totals(): pl.pallas_call(functools.partial(totals_kernel, low, high), in_specs=[ON_...]
  transfers between devices with their start and end apart: 32 -> 35, of which waited for: 18 -> 20; matrix products, arithmetic and copies ran while one was open for 0% -> 0% of each run, Pallas kernels for 14% -> 15%
where the time goes in v3:
time: 106 us
  starting transfers between devices  41.7 us (39%)
  waiting for transfers between devices  33.4 us (32%)
  Pallas kernels  29.5 us (28%)
    ppermute x35, starting transfers between devices, exchange(): lax.ppermute(value, AXES, [(d, d ^ mask_of(d)) for d in range(count)])  41.7 us
    ppermute x35, waiting for transfers between devices, exchange(): lax.ppermute(value, AXES, [(d, d ^ mask_of(d)) for d in range(count)])  33.4 us
    pallas_call x1, Pallas kernels, standardize(): pl.pallas_call(functools.partial(standard_kernel, samples_total), in_spec...  7.92 us
    pallas_call x2, Pallas kernels, begin_inverse(): pl.pallas_call(functools.partial(begin_kernel_inverse, last), in_specs=[O...  6.93 us
    pallas_call x8, Pallas kernels, totals(): pl.pallas_call(functools.partial(totals_kernel, low, high), in_specs=[ON_...  4.42 us
    pallas_call x1, Pallas kernels, project(): pl.pallas_call(functools.partial(project_kernel, len(parts), base), in_sp...  2.44 us
    pallas_call x1, Pallas kernels, begin_project(): pl.pallas_call(functools.partial(begin_kernel, len(parts), base), in_spec...  2.14 us
  transfers between devices with their start and end apart: 35, of which 20 were waited for; matrix products, arithmetic and copies ran while one was open for 0% of the time, Pallas kernels for 15%

profile of v3, /device:TPU:0, one launch (start us, length us, event | category | flops | bytes accessed | tf_op | source)
XLA Modules:
  0.0 105.6 jit_solution(14562425961056460781)
XLA Ops:
  0.7 7.9 %standardize.1 = (bf16[1024,4096]{1,0:T(8,128)(2,1)S(1)}, bf16[1024,128]{1,0:T(8,128)(2,1)}, bf16[128,1024]{1,0:T(8,128)(2,1)S(1)}, f32[128,128]{1,0:T(8,128)S(1)}, f32[1024,128]{1,0:T(8,128)S(1)}) custom-call(s32[40]{0:T(128)S(1)} %pad_add_fusion.order.refs_5_, bf16[1024,4096]{1,0:T(8,128)(2,1)} %dosage.1, s32[7,128]{1,0:T(8,128)} %bitcast.2, ...), custom_call_target="tpu_custom_call" | custom-call | flops 1073741824 | bytes 16777216 | tf_op jit(solution)/shard_map/standardize/pallas_call | solution.py:147
  11.4 2.9 %collective-permute-start.4 = (f32[448,128]{1,0:T(8,128)S(1)}, f32[448,128]{1,0:T(8,128)S(1)}, u32[]{:S(2)}, u32[]{:S(2)}) collective-permute-start(f32[448,128]{1,0:T(8,128)S(1)} %get-tuple-element.46.refs_3_), channel_id=1, source_target_pairs={{0,4},{1,3},{2,6},{3,1},{4,0},{5,7},{6,2},{7,5},{8,12},{9,11},{10,... | collective-permute-start | bytes 688136 | tf_op jit(solution)/shard_map/ppermute | solution.py:57
  15.0 3.4 %collective-permute-done.4.refs_2_ = f32[448,128]{1,0:T(8,128)S(1)} collective-permute-done((f32[448,128]{1,0:T(8,128)S(1)}, f32[448,128]{1,0:T(8,128)S(1)}, u32[]{:S(2)}, u32[]{:S(2)}) %collective-permute-start.4) | collective-permute-done | bytes 229408 | tf_op jit(solution)/shard_map/ppermute | solution.py:57
  18.3 2.1 %collective-permute-start.5 = (f32[448,128]{1,0:T(8,128)S(1)}, f32[448,128]{1,0:T(8,128)S(1)}, u32[]{:S(2)}, u32[]{:S(2)}) collective-permute-start(f32[448,128]{1,0:T(8,128)S(1)} %combine.16.refs_4_), channel_id=1, source_target_pairs={{0,2},{1,5},{2,0},{3,7},{4,6},{5,1},{6,4},{7,3},{8,10},{9,13},{10,... | collective-permute-start | bytes 688136 | tf_op jit(solution)/shard_map/ppermute | solution.py:57
  20.5 2.5 %collective-permute-done.2.refs_2_ = f32[640,128]{1,0:T(8,128)S(1)} collective-permute-done((f32[640,128]{1,0:T(8,128)S(1)}, f32[640,128]{1,0:T(8,128)S(1)}, u32[]{:S(2)}, u32[]{:S(2)}) %collective-permute-start.2) | collective-permute-done | bytes 327712 | tf_op jit(solution)/shard_map/ppermute | solution.py:57
  24.5 4.2 %collective-permute-start.6 = (f32[144,128]{1,0:T(8,128)S(1)}, f32[144,128]{1,0:T(8,128)S(1)}, u32[]{:S(2)}, u32[]{:S(2)}) collective-permute-start(f32[144,128]{1,0:T(8,128)S(1)} %get-tuple-element.48), channel_id=1, source_target_pairs={{0,24},{1,25},{2,26},{3,27},{4,28},{5,29},{6,30},{7,31},{8,16},{9,... | collective-permute-start | bytes 221192 | tf_op jit(solution)/shard_map/ppermute | solution.py:57
  31.1 2.6 %collective-permute-done.3.refs_3_ = f32[128,128]{1,0:T(8,128)S(1)} collective-permute-done((f32[128,128]{1,0:T(8,128)S(1)}, f32[128,128]{1,0:T(8,128)S(1)}, u32[]{:S(2)}, u32[]{:S(2)}) %collective-permute-start.3) | collective-permute-done | bytes 65568 | tf_op jit(solution)/shard_map/ppermute | solution.py:57
  36.3 2.2 %collective-permute-start.11 = (f32[144,128]{1,0:T(8,128)S(1)}, f32[144,128]{1,0:T(8,128)S(1)}, u32[]{:S(2)}, u32[]{:S(2)}) collective-permute-start(f32[144,128]{1,0:T(8,128)S(1)} %combine.19.refs_0_), channel_id=1, source_target_pairs={{0,24},{1,25},{2,26},{3,27},{4,28},{5,29},{6,30},{7,31},{8,16},{9,... | collective-permute-start | bytes 221192 | tf_op jit(solution)/shard_map/ppermute | solution.py:57
  38.6 4.4 %collective-permute-done.10.refs_2_ = f32[144,128]{1,0:T(8,128)S(1)} collective-permute-done((f32[144,128]{1,0:T(8,128)S(1)}, f32[144,128]{1,0:T(8,128)S(1)}, u32[]{:S(2)}, u32[]{:S(2)}) %collective-permute-start.10) | collective-permute-done | bytes 73760 | tf_op jit(solution)/shard_map/ppermute | solution.py:57
  48.0 2.4 %begin_inverse.2 = (f32[128,128]{1,0:T(8,128)S(1)}, f32[128,128]{1,0:T(8,128)S(1)}) custom-call(f32[64,128]{1,0:T(8,128)S(1)} %get-tuple-element.54.own, f32[64,128]{1,0:T(8,128)S(1)} %collective-permute-done.12.other, s32[40]{0:T(128)S(1)} %pad_add_fusion.order.refs_5_), custom_call_target="tpu_custom_call" | custom-call | flops 1000000000 | bytes 8000000 | tf_op jit(solution)/shard_map/begin_inverse/pallas_call | solution.py:360
  55.7 2.1 %begin_project.1.refs_3_ = f32[1024,128]{1,0:T(8,128)S(1)} custom-call(f32[512,128]{1,0:T(8,128)S(1)} %get-tuple-element.55.refs_0_, f32[512,128]{1,0:T(8,128)S(1)} %collective-permute-done.15.refs_1_, f32[512,128]{1,0:T(8,128)S(1)} %collective-permute-done.13.refs_2_, f32[512,128]{1,0:T(8,128)S(1)} %collective-permute-done.17.refs_3_, ...), custom_call_target="tpu_custom_call" | custom-call | flops 671088640 | bytes 5242880 | tf_op jit(solution)/shard_map/begin_project/pallas_call | solution.py:261
  59.5 2.4 %project.1 = (bf16[1024,128]{1,0:T(8,128)(2,1)S(1)}, bf16[128,1024]{1,0:T(8,128)(2,1)S(1)}, f32[128,128]{1,0:T(8,128)S(1)}) custom-call(f32[512,128]{1,0:T(8,128)S(1)} %collective-permute-done.14.refs_0_, f32[512,128]{1,0:T(8,128)S(1)} %collective-permute-done.16.refs_1_, f32[512,128]{1,0:T(8,128)S(1)} %collective-permute-done.19.refs_2_, ...), custom_call_target="tpu_custom_call" | custom-call | flops 402653184 | bytes 3145728 | tf_op jit(solution)/shard_map/project/pallas_call | solution.py:285
  67.3 3.4 %collective-permute-done.24.refs_2_ = f32[448,128]{1,0:T(8,128)S(1)} collective-permute-done((f32[448,128]{1,0:T(8,128)S(1)}, f32[448,128]{1,0:T(8,128)S(1)}, u32[]{:S(2)}, u32[]{:S(2)}) %collective-permute-start.24) | collective-permute-done | bytes 229408 | tf_op jit(solution)/shard_map/ppermute | solution.py:57
  70.7 2.2 %collective-permute-start.25 = (f32[448,128]{1,0:T(8,128)S(1)}, f32[448,128]{1,0:T(8,128)S(1)}, u32[]{:S(2)}, u32[]{:S(2)}) collective-permute-start(f32[448,128]{1,0:T(8,128)S(1)} %combine.23.refs_4_), channel_id=1, source_target_pairs={{0,2},{1,5},{2,0},{3,7},{4,6},{5,1},{6,4},{7,3},{8,10},{9,13},{10,... | collective-permute-start | bytes 688136 | tf_op jit(solution)/shard_map/ppermute | solution.py:57
  72.9 2.3 %collective-permute-done.22.refs_2_ = f32[640,128]{1,0:T(8,128)S(1)} collective-permute-done((f32[640,128]{1,0:T(8,128)S(1)}, f32[640,128]{1,0:T(8,128)S(1)}, u32[]{:S(2)}, u32[]{:S(2)}) %collective-permute-start.22) | collective-permute-done | bytes 327712 | tf_op jit(solution)/shard_map/ppermute | solution.py:57
  77.0 2.1 %collective-permute-start.26 = (f32[144,128]{1,0:T(8,128)S(1)}, f32[144,128]{1,0:T(8,128)S(1)}, u32[]{:S(2)}, u32[]{:S(2)}) collective-permute-start(f32[144,128]{1,0:T(8,128)S(1)} %get-tuple-element.70), channel_id=1, source_target_pairs={{0,24},{1,25},{2,26},{3,27},{4,28},{5,29},{6,30},{7,31},{8,16},{9,... | collective-permute-start | bytes 221192 | tf_op jit(solution)/shard_map/ppermute | solution.py:57
  79.2 2.2 %collective-permute-start.28 = (f32[144,128]{1,0:T(8,128)S(1)}, f32[144,128]{1,0:T(8,128)S(1)}, u32[]{:S(2)}, u32[]{:S(2)}) collective-permute-start(f32[144,128]{1,0:T(8,128)S(1)} %get-tuple-element.72), channel_id=1, source_target_pairs={{0,8},{1,9},{2,10},{3,11},{4,12},{5,13},{6,14},{7,15},{8,0},{9,1},... | collective-permute-start | bytes 221192 | tf_op jit(solution)/shard_map/ppermute | solution.py:57
  81.4 2.1 %collective-permute-start.23 = (f32[128,128]{1,0:T(8,128)S(1)}, f32[128,128]{1,0:T(8,128)S(1)}, u32[]{:S(2)}, u32[]{:S(2)}) collective-permute-start(f32[128,128]{1,0:T(8,128)S(1)} %combine.22), channel_id=1, source_target_pairs={{0,2},{1,5},{2,0},{3,7},{4,6},{5,1},{6,4},{7,3},{8,10},{9,13},{10,... | collective-permute-start | bytes 196616 | tf_op jit(solution)/shard_map/ppermute | solution.py:57
  86.4 2.6 %collective-permute-start.30 = (f32[144,128]{1,0:T(8,128)S(1)}, f32[144,128]{1,0:T(8,128)S(1)}, u32[]{:S(2)}, u32[]{:S(2)}) collective-permute-start(f32[144,128]{1,0:T(8,128)S(1)} %combine.26), channel_id=1, source_target_pairs={{0,16},{1,17},{2,18},{3,19},{4,20},{5,21},{6,22},{7,23},{8,24},{9,... | collective-permute-start | bytes 221192 | tf_op jit(solution)/shard_map/ppermute | solution.py:57
  89.0 1.8 %collective-permute-start.31 = (f32[144,128]{1,0:T(8,128)S(1)}, f32[144,128]{1,0:T(8,128)S(1)}, u32[]{:S(2)}, u32[]{:S(2)}) collective-permute-start(f32[144,128]{1,0:T(8,128)S(1)} %combine.26), channel_id=1, source_target_pairs={{0,24},{1,25},{2,26},{3,27},{4,28},{5,29},{6,30},{7,31},{8,16},{9,... | collective-permute-start | bytes 221192 | tf_op jit(solution)/shard_map/ppermute | solution.py:57
  90.8 1.9 %collective-permute-start.32 = (f32[128,128]{1,0:T(8,128)S(1)}, f32[128,128]{1,0:T(8,128)S(1)}, u32[]{:S(2)}, u32[]{:S(2)}) collective-permute-start(f32[128,128]{1,0:T(8,128)S(1)} %get-tuple-element.76.refs_0_), channel_id=1, source_target_pairs={{0,4},{1,5},{2,6},{3,7},{4,0},{5,1},{6,2},{7,3},{8,12},{9,13},{10,... | collective-permute-start | bytes 196616 | tf_op jit(solution)/shard_map/ppermute | solution.py:57
  92.7 2.4 %collective-permute-done.32.refs_5_ = f32[128,128]{1,0:T(8,128)S(1)} collective-permute-done((f32[128,128]{1,0:T(8,128)S(1)}, f32[128,128]{1,0:T(8,128)S(1)}, u32[]{:S(2)}, u32[]{:S(2)}) %collective-permute-start.32) | collective-permute-done | bytes 65568 | tf_op jit(solution)/shard_map/ppermute | solution.py:57
  98.3 4.5 %begin_inverse.3 = (f32[128,128]{1,0:T(8,128)}, f32[128,128]{1,0:T(8,128)S(1)}) custom-call(f32[64,128]{1,0:T(8,128)S(1)} %get-tuple-element.78.own, f32[64,128]{1,0:T(8,128)S(1)} %collective-permute-done.33.other, s32[40]{0:T(128)S(1)} %pad_add_fusion.order.refs_5_), custom_call_target="tpu_custom_call" | custom-call | flops 1000000000 | bytes 8000000 | tf_op jit(solution)/shard_map/begin_inverse/pallas_call | solution.py:360
  103.9 1.7 %load.1 = f32[1024,128]{1,0:T(8,128)} custom-call(s32[8]{0:T(128)S(1)} %broadcast_xor_fusion.order, f32[256,128]{1,0:T(8,128)S(1)} %get-tuple-element.80.refs_0_, f32[384,128]{1,0:T(8,128)S(1)} %get-tuple-element.81.refs_1_, f32[384,128]{1,0:T(8,128)S(1)} %collective-permute-done.34.refs_2_, f32[128,128]{1,0:T(8,128)S(1)} %get-tuple-element.79.inverse.refs_3_), custom_call_target="tpu_custom_call" | custom-call | flops 100000000 | bytes 1000000 | tf_op jit(solution)/shard_map/load/pallas_call | solution.py:440
  (85 shorter events, 36.2 us)
Async XLA Ops:
  10.3 4.6 %collective-permute-start = (f32[1024,128]{1,0:T(8,128)S(1)}, f32[1024,128]{1,0:T(8,128)S(1)}, u32[]{:S(2)}, u32[]{:S(2)}) collective-permute-start(f32[1024,128]{1,0:T(8,128)S(1)} %totals.9), channel_id=1, source_target_pairs={{0,1},{1,0},{2,3},{3,2},{4,5},{5,4},{6,7},{7,6},{8,9},{9,8},{10,11... | collective-permute-start | bytes 1572872 | tf_op jit(solution)/shard_map/ppermute | solution.py:57
  11.4 6.9 %collective-permute-start.4 = (f32[448,128]{1,0:T(8,128)S(1)}, f32[448,128]{1,0:T(8,128)S(1)}, u32[]{:S(2)}, u32[]{:S(2)}) collective-permute-start(f32[448,128]{1,0:T(8,128)S(1)} %get-tuple-element.46.refs_3_), channel_id=1, source_target_pairs={{0,4},{1,3},{2,6},{3,1},{4,0},{5,7},{6,2},{7,5},{8,12},{9,11},{10,... | collective-permute-start | bytes 688136 | tf_op jit(solution)/shard_map/ppermute | solution.py:57
  14.3 8.7 %collective-permute-start.2 = (f32[640,128]{1,0:T(8,128)S(1)}, f32[640,128]{1,0:T(8,128)S(1)}, u32[]{:S(2)}, u32[]{:S(2)}) collective-permute-start(f32[640,128]{1,0:T(8,128)S(1)} %get-tuple-element.45), channel_id=1, source_target_pairs={{0,4},{1,3},{2,6},{3,1},{4,0},{5,7},{6,2},{7,5},{8,12},{9,11},{10,... | collective-permute-start | bytes 983048 | tf_op jit(solution)/shard_map/ppermute | solution.py:57
  18.3 6.1 %collective-permute-start.5 = (f32[448,128]{1,0:T(8,128)S(1)}, f32[448,128]{1,0:T(8,128)S(1)}, u32[]{:S(2)}, u32[]{:S(2)}) collective-permute-start(f32[448,128]{1,0:T(8,128)S(1)} %combine.16.refs_4_), channel_id=1, source_target_pairs={{0,2},{1,5},{2,0},{3,7},{4,6},{5,1},{6,4},{7,3},{8,10},{9,13},{10,... | collective-permute-start | bytes 688136 | tf_op jit(solution)/shard_map/ppermute | solution.py:57
  24.5 9.2 %collective-permute-start.6 = (f32[144,128]{1,0:T(8,128)S(1)}, f32[144,128]{1,0:T(8,128)S(1)}, u32[]{:S(2)}, u32[]{:S(2)}) collective-permute-start(f32[144,128]{1,0:T(8,128)S(1)} %get-tuple-element.48), channel_id=1, source_target_pairs={{0,24},{1,25},{2,26},{3,27},{4,28},{5,29},{6,30},{7,31},{8,16},{9,... | collective-permute-start | bytes 221192 | tf_op jit(solution)/shard_map/ppermute | solution.py:57
  28.7 6.3 %collective-permute-start.7 = (f32[144,128]{1,0:T(8,128)S(1)}, f32[144,128]{1,0:T(8,128)S(1)}, u32[]{:S(2)}, u32[]{:S(2)}) collective-permute-start(f32[144,128]{1,0:T(8,128)S(1)} %get-tuple-element.49), channel_id=1, source_target_pairs={{0,16},{1,17},{2,18},{3,19},{4,20},{5,21},{6,22},{7,23},{8,24},{9,... | collective-permute-start | bytes 221192 | tf_op jit(solution)/shard_map/ppermute | solution.py:57
  28.7 6.3 %collective-permute-start.8 = (f32[144,128]{1,0:T(8,128)S(1)}, f32[144,128]{1,0:T(8,128)S(1)}, u32[]{:S(2)}, u32[]{:S(2)}) collective-permute-start(f32[144,128]{1,0:T(8,128)S(1)} %get-tuple-element.50), channel_id=1, source_target_pairs={{0,8},{1,9},{2,10},{3,11},{4,12},{5,13},{6,14},{7,15},{8,0},{9,1},... | collective-permute-start | bytes 221192 | tf_op jit(solution)/shard_map/ppermute | solution.py:57
  35.1 8.0 %collective-permute-start.10 = (f32[144,128]{1,0:T(8,128)S(1)}, f32[144,128]{1,0:T(8,128)S(1)}, u32[]{:S(2)}, u32[]{:S(2)}) collective-permute-start(f32[144,128]{1,0:T(8,128)S(1)} %combine.19.refs_0_), channel_id=1, source_target_pairs={{0,16},{1,17},{2,18},{3,19},{4,20},{5,21},{6,22},{7,23},{8,24},{9,... | collective-permute-start | bytes 221192 | tf_op jit(solution)/shard_map/ppermute | solution.py:57
  36.3 6.8 %collective-permute-start.11 = (f32[144,128]{1,0:T(8,128)S(1)}, f32[144,128]{1,0:T(8,128)S(1)}, u32[]{:S(2)}, u32[]{:S(2)}) collective-permute-start(f32[144,128]{1,0:T(8,128)S(1)} %combine.19.refs_0_), channel_id=1, source_target_pairs={{0,24},{1,25},{2,26},{3,27},{4,28},{5,29},{6,30},{7,31},{8,16},{9,... | collective-permute-start | bytes 221192 | tf_op jit(solution)/shard_map/ppermute | solution.py:57
  38.5 5.1 %collective-permute-start.9 = (f32[144,128]{1,0:T(8,128)S(1)}, f32[144,128]{1,0:T(8,128)S(1)}, u32[]{:S(2)}, u32[]{:S(2)}) collective-permute-start(f32[144,128]{1,0:T(8,128)S(1)} %combine.19.refs_0_), channel_id=1, source_target_pairs={{0,8},{1,9},{2,10},{3,11},{4,12},{5,13},{6,14},{7,15},{8,0},{9,1},... | collective-permute-start | bytes 221192 | tf_op jit(solution)/shard_map/ppermute | solution.py:57
  43.6 7.6 %collective-permute-start.15 = (f32[512,128]{1,0:T(8,128)S(1)}, f32[512,128]{1,0:T(8,128)S(1)}, u32[]{:S(2)}, u32[]{:S(2)}) collective-permute-start(f32[512,128]{1,0:T(8,128)S(1)} %get-tuple-element.55.refs_0_), channel_id=1, source_target_pairs={{0,2},{1,5},{2,0},{3,7},{4,6},{5,1},{6,4},{7,3},{8,10},{9,13},{10,... | collective-permute-start | bytes 786440 | tf_op jit(solution)/shard_map/ppermute | solution.py:57
  45.3 10.4 %collective-permute-start.17 = (f32[512,128]{1,0:T(8,128)S(1)}, f32[512,128]{1,0:T(8,128)S(1)}, u32[]{:S(2)}, u32[]{:S(2)}) collective-permute-start(f32[512,128]{1,0:T(8,128)S(1)} %get-tuple-element.55.refs_0_), channel_id=1, source_target_pairs={{0,1},{1,0},{2,3},{3,2},{4,5},{5,4},{6,7},{7,6},{8,9},{9,8},{10,11... | collective-permute-start | bytes 786440 | tf_op jit(solution)/shard_map/ppermute | solution.py:57
  46.5 7.8 %collective-permute-start.13 = (f32[512,128]{1,0:T(8,128)S(1)}, f32[512,128]{1,0:T(8,128)S(1)}, u32[]{:S(2)}, u32[]{:S(2)}) collective-permute-start(f32[512,128]{1,0:T(8,128)S(1)} %get-tuple-element.55.refs_0_), channel_id=1, source_target_pairs={{0,4},{1,3},{2,6},{3,1},{4,0},{5,7},{6,2},{7,5},{8,12},{9,11},{10,... | collective-permute-start | bytes 786440 | tf_op jit(solution)/shard_map/ppermute | solution.py:57
  51.2 6.7 %collective-permute-start.16 = (f32[512,128]{1,0:T(8,128)S(1)}, f32[512,128]{1,0:T(8,128)S(1)}, u32[]{:S(2)}, u32[]{:S(2)}) collective-permute-start(f32[512,128]{1,0:T(8,128)S(1)} %collective-permute-done.15.refs_1_), channel_id=1, source_target_pairs={{0,4},{1,3},{2,6},{3,1},{4,0},{5,7},{6,2},{7,5},{8,12},{9,11},{10,... | collective-permute-start | bytes 786440 | tf_op jit(solution)/shard_map/ppermute | solution.py:57
  64.6 6.1 %collective-permute-start.24 = (f32[448,128]{1,0:T(8,128)S(1)}, f32[448,128]{1,0:T(8,128)S(1)}, u32[]{:S(2)}, u32[]{:S(2)}) collective-permute-start(f32[448,128]{1,0:T(8,128)S(1)} %get-tuple-element.68.refs_3_), channel_id=1, source_target_pairs={{0,4},{1,3},{2,6},{3,1},{4,0},{5,7},{6,2},{7,5},{8,12},{9,11},{10,... | collective-permute-start | bytes 688136 | tf_op jit(solution)/shard_map/ppermute | solution.py:57
  66.0 9.2 %collective-permute-start.22 = (f32[640,128]{1,0:T(8,128)S(1)}, f32[640,128]{1,0:T(8,128)S(1)}, u32[]{:S(2)}, u32[]{:S(2)}) collective-permute-start(f32[640,128]{1,0:T(8,128)S(1)} %get-tuple-element.67), channel_id=1, source_target_pairs={{0,4},{1,3},{2,6},{3,1},{4,0},{5,7},{6,2},{7,5},{8,12},{9,11},{10,... | collective-permute-start | bytes 983048 | tf_op jit(solution)/shard_map/ppermute | solution.py:57
  70.7 6.2 %collective-permute-start.25 = (f32[448,128]{1,0:T(8,128)S(1)}, f32[448,128]{1,0:T(8,128)S(1)}, u32[]{:S(2)}, u32[]{:S(2)}) collective-permute-start(f32[448,128]{1,0:T(8,128)S(1)} %combine.23.refs_4_), channel_id=1, source_target_pairs={{0,2},{1,5},{2,0},{3,7},{4,6},{5,1},{6,4},{7,3},{8,10},{9,13},{10,... | collective-permute-start | bytes 688136 | tf_op jit(solution)/shard_map/ppermute | solution.py:57
  77.0 8.8 %collective-permute-start.26 = (f32[144,128]{1,0:T(8,128)S(1)}, f32[144,128]{1,0:T(8,128)S(1)}, u32[]{:S(2)}, u32[]{:S(2)}) collective-permute-start(f32[144,128]{1,0:T(8,128)S(1)} %get-tuple-element.70), channel_id=1, source_target_pairs={{0,24},{1,25},{2,26},{3,27},{4,28},{5,29},{6,30},{7,31},{8,16},{9,... | collective-permute-start | bytes 221192 | tf_op jit(solution)/shard_map/ppermute | solution.py:57
  79.1 7.2 %collective-permute-start.27 = (f32[144,128]{1,0:T(8,128)S(1)}, f32[144,128]{1,0:T(8,128)S(1)}, u32[]{:S(2)}, u32[]{:S(2)}) collective-permute-start(f32[144,128]{1,0:T(8,128)S(1)} %get-tuple-element.71), channel_id=1, source_target_pairs={{0,16},{1,17},{2,18},{3,19},{4,20},{5,21},{6,22},{7,23},{8,24},{9,... | collective-permute-start | bytes 221192 | tf_op jit(solution)/shard_map/ppermute | solution.py:57
  79.2 7.1 %collective-permute-start.28 = (f32[144,128]{1,0:T(8,128)S(1)}, f32[144,128]{1,0:T(8,128)S(1)}, u32[]{:S(2)}, u32[]{:S(2)}) collective-permute-start(f32[144,128]{1,0:T(8,128)S(1)} %get-tuple-element.72), channel_id=1, source_target_pairs={{0,8},{1,9},{2,10},{3,11},{4,12},{5,13},{6,14},{7,15},{8,0},{9,1},... | collective-permute-start | bytes 221192 | tf_op jit(solution)/shard_map/ppermute | solution.py:57
  86.3 8.7 %collective-permute-start.29 = (f32[144,128]{1,0:T(8,128)S(1)}, f32[144,128]{1,0:T(8,128)S(1)}, u32[]{:S(2)}, u32[]{:S(2)}) collective-permute-start(f32[144,128]{1,0:T(8,128)S(1)} %combine.26), channel_id=1, source_target_pairs={{0,8},{1,9},{2,10},{3,11},{4,12},{5,13},{6,14},{7,15},{8,0},{9,1},... | collective-permute-start | bytes 221192 | tf_op jit(solution)/shard_map/ppermute | solution.py:57
  86.4 9.1 %collective-permute-start.30 = (f32[144,128]{1,0:T(8,128)S(1)}, f32[144,128]{1,0:T(8,128)S(1)}, u32[]{:S(2)}, u32[]{:S(2)}) collective-permute-start(f32[144,128]{1,0:T(8,128)S(1)} %combine.26), channel_id=1, source_target_pairs={{0,16},{1,17},{2,18},{3,19},{4,20},{5,21},{6,22},{7,23},{8,24},{9,... | collective-permute-start | bytes 221192 | tf_op jit(solution)/shard_map/ppermute | solution.py:57
  89.0 6.5 %collective-permute-start.31 = (f32[144,128]{1,0:T(8,128)S(1)}, f32[144,128]{1,0:T(8,128)S(1)}, u32[]{:S(2)}, u32[]{:S(2)}) collective-permute-start(f32[144,128]{1,0:T(8,128)S(1)} %combine.26), channel_id=1, source_target_pairs={{0,24},{1,25},{2,26},{3,27},{4,28},{5,29},{6,30},{7,31},{8,16},{9,... | collective-permute-start | bytes 221192 | tf_op jit(solution)/shard_map/ppermute | solution.py:57
  95.6 8.3 %collective-permute-start.34 = (f32[384,128]{1,0:T(8,128)S(1)}, f32[384,128]{1,0:T(8,128)S(1)}, u32[]{:S(2)}, u32[]{:S(2)}) collective-permute-start(f32[384,128]{1,0:T(8,128)S(1)} %get-tuple-element.81.refs_1_), channel_id=1, source_target_pairs={{0,4},{1,5},{2,6},{3,7},{4,0},{5,1},{6,2},{7,3},{8,12},{9,13},{10,... | collective-permute-start | bytes 589832 | tf_op jit(solution)/shard_map/ppermute | solution.py:57
  (13 other events, 83.6 us)

commit v4 on v3

--- a/solution.py
+++ b/solution.py
@@ -41,15 +41,22 @@
     second = (position >> 2) & 1
     core_bit = (position >> 4) & 1
     target = core ^ core_bit
-    bit_x = jnp.where(target == 0, first, second)
-    bit_y = jnp.where(target == 0, second, first)
+    bit_x = first * (1 - target) + second * target
+    bit_y = second * (1 - target) + first * target
     return core_bit | (bit_y << 1) | (bit_x << 2) | ((position & 3) << 3)
 
 
-def block_order(device):
-    position = lax.iota(jnp.int32, BLOCKS)
+def this_device():
+    return lax.axis_index("wide") * lax.axis_size("narrow") + lax.axis_index("narrow")
+
+
+def block_at(device, position):
     owner = device ^ relative(position, device & 1)
     return (owner & 3) * 8 + ((owner >> 2) & 7)
+
+
+def group_at(device, place):
+    return (((place >> 2) ^ (device & 1)) << 2) | ((place & 3) ^ ((device >> 3) & 3))
 
 
 def exchange(value, mask_of):
@@ -74,9 +81,11 @@
     return (((place >> 2) ^ (device & 1)) << 2) | ((place & 3) ^ ((device >> 3) & 3))
 
 
-def standard_kernel(samples_total, order, dosage, keep, counts, projection, standard, projected, turned, gram, kept, rows_in, sketch_in, keep_in, counts_in, table, basis, whole, sems):
+def standard_kernel(samples_total, dosage, keep, counts, projection, standard, projected, turned, gram, kept, rows_in, sketch_in, keep_in, counts_in, table, basis, whole, sems):
     samples = dosage.shape[0]
     steps = samples // ROWS
+    device = this_device()
+    order = [block_at(device, p) for p in range(BLOCKS)]
     small = [
         pltpu.make_async_copy(source, target, sems.at[i])
         for i, (source, target) in enumerate(((counts, counts_in), (keep, keep_in), (projection, sketch_in)))
@@ -117,13 +126,14 @@
             standard[slab, p * TILE : (p + 1) * TILE] = ((value - center) * scale).astype(jnp.bfloat16)
     value = jnp.dot(standard[...], basis[...], preferred_element_type=jnp.float32)
     finish_rows(value, kept, projected, turned, whole)
-    share_gram(order, whole, gram)
-
-
-def share_gram(order, whole, gram):
+    share_gram(whole, gram)
+
+
+def share_gram(whole, gram):
+    device = this_device()
     height = TILE // GROUPS
     for place in range(GROUPS):
-        start = pl.multiple_of(order[BLOCKS + place] * height, height)
+        start = pl.multiple_of(group_at(device, place) * height, height)
         gram[place * height : (place + 1) * height, :] = whole[pl.ds(start, height), :]
 
 
@@ -137,16 +147,15 @@
 
 
 ON_CHIP = pl.BlockSpec(memory_space=pltpu.VMEM)
-SCALARS = pl.BlockSpec(memory_space=pltpu.SMEM)
 FAR = pl.BlockSpec(memory_space=pltpu.HBM)
 
 
-def standardize(samples_total, order, *arrays):
+def standardize(samples_total, *arrays):
     dosage, keep, counts, projection = [pltpu.with_memory_space_constraint(x, pltpu.HBM) for x in arrays]
     samples, snps = arrays[0].shape
     return pl.pallas_call(
         functools.partial(standard_kernel, samples_total),
-        in_specs=[SCALARS, FAR, FAR, FAR, FAR],
+        in_specs=[FAR, FAR, FAR, FAR],
         out_specs=[ON_CHIP] * 5,
         out_shape=[
             jax.ShapeDtypeStruct((samples, snps), jnp.bfloat16),
@@ -168,7 +177,7 @@
         compiler_params=pltpu.CompilerParams(vmem_limit_bytes=VMEM),
         cost_estimate=pl.CostEstimate(flops=2 * samples * snps * TILE, bytes_accessed=4 * samples * snps, transcendentals=0),
         name="standardize",
-    )(order, dosage, keep, counts, projection)
+    )(dosage, keep, counts, projection)
 
 
 WIDTH = 512
@@ -272,19 +281,19 @@
 
 def project_kernel(pieces, base, *refs):
     parts = refs[:pieces]
-    begun, inverse, order, standard, kept, projected, turned, gram, basis, whole = refs[pieces:]
+    begun, inverse, standard, kept, projected, turned, gram, basis, whole = refs[pieces:]
     apply_inverse(parts, inverse, basis)
     value = add_products(standard, basis, base, begun[...])
     finish_rows(value, kept, projected, turned, whole)
-    share_gram(order, whole, gram)
-
-
-def project(parts, base, begun, inverse, order, standard, kept):
+    share_gram(whole, gram)
+
+
+def project(parts, base, begun, inverse, standard, kept):
     samples = standard.shape[0]
     rows = sum(part.shape[0] for part in parts)
     return pl.pallas_call(
         functools.partial(project_kernel, len(parts), base),
-        in_specs=[ON_CHIP] * (len(parts) + 2) + [SCALARS, ON_CHIP, ON_CHIP],
+        in_specs=[ON_CHIP] * (len(parts) + 4),
         out_specs=[ON_CHIP] * 3,
         out_shape=[
             jax.ShapeDtypeStruct((samples, TILE), jnp.bfloat16),
@@ -295,7 +304,7 @@
         compiler_params=pltpu.CompilerParams(vmem_limit_bytes=SMALL),
         cost_estimate=pl.CostEstimate(flops=2 * samples * rows * TILE, bytes_accessed=2 * samples * rows, transcendentals=0),
         name="project",
-    )(*parts, begun, inverse, order, standard, kept)
+    )(*parts, begun, inverse, standard, kept)
 
 
 PANEL = 16
@@ -334,11 +343,12 @@
             right[stop:, :] -= both[stop:, TILE:]
 
 
-def begin_kernel_inverse(last, own, other, order, left, right):
+def begin_kernel_inverse(last, own, other, left, right):
+    device = this_device()
     height = TILE // GROUPS
     for half, source in enumerate((own, other)):
         for row in range(GROUPS // 2):
-            start = pl.multiple_of(order[BLOCKS + half * (GROUPS // 2) + row] * height, height)
+            start = pl.multiple_of(group_at(device, half * (GROUPS // 2) + row) * height, height)
             left[pl.ds(start, height), :] = source[row * height : (row + 1) * height, :]
     lanes = lax.broadcasted_iota(jnp.int32, (TILE, TILE), 1)
     subs = lax.broadcasted_iota(jnp.int32, (TILE, TILE), 0)
@@ -356,16 +366,16 @@
 SQUARE = jax.ShapeDtypeStruct((TILE, TILE), jnp.float32)
 
 
-def begin_inverse(last, own, other, order):
+def begin_inverse(last, own, other):
     return pl.pallas_call(
         functools.partial(begin_kernel_inverse, last),
-        in_specs=[ON_CHIP, ON_CHIP, SCALARS],
+        in_specs=[ON_CHIP, ON_CHIP],
         out_specs=[ON_CHIP, ON_CHIP],
         out_shape=[SQUARE, SQUARE],
         compiler_params=pltpu.CompilerParams(vmem_limit_bytes=SMALL),
         cost_estimate=pl.CostEstimate(flops=1_000_000_000, bytes_accessed=8_000_000, transcendentals=0),
         name="begin_inverse",
-    )(own, other, order)
+    )(own, other)
 
 
 def end_inverse(first, left, right):
@@ -381,8 +391,8 @@
     )(left, right)
 
 
-def invert_factor(own, other, order):
-    return begin_inverse(TILE, own, other, order)[1]
+def invert_factor(own, other):
+    return begin_inverse(TILE, own, other)[1]
 
 
 def pick_kernel(keep, projected, chosen):
@@ -425,26 +435,28 @@
     )(chosen, inverse)
 
 
-def loadings_kernel(pieces, order, *refs):
+def loadings_kernel(pieces, positions, *refs):
+    wide = lax.axis_index("wide") & 7
     parts = refs[:pieces]
     inverse, loadings = refs[pieces:]
     high, low = split(inverse[...])
     value = product(jnp.concatenate([part[...] for part in parts], axis=0), high, low)
-    for position in range(value.shape[0] // TILE):
-        start = pl.multiple_of(order[position] * TILE, TILE)
-        loadings[pl.ds(start, TILE), :] = value[position * TILE : (position + 1) * TILE, :]
-
-
-def load(order, parts, inverse):
+    for i, position in enumerate(positions):
+        place = wide ^ (((position & 3) << 1) | (position >> 2))
+        start = pl.multiple_of(place * TILE, TILE)
+        loadings[pl.ds(start, TILE), :] = value[i * TILE : (i + 1) * TILE, :]
+
+
+def load(positions, parts, inverse):
     count = sum(part.shape[0] for part in parts)
     return pl.pallas_call(
-        functools.partial(loadings_kernel, len(parts)),
-        in_specs=[pl.BlockSpec(memory_space=pltpu.SMEM)] + [pl.BlockSpec(memory_space=pltpu.VMEM)] * (len(parts) + 1),
+        functools.partial(loadings_kernel, len(parts), positions),
+        in_specs=[ON_CHIP] * (len(parts) + 1),
         out_shape=jax.ShapeDtypeStruct((count, TILE), jnp.float32),
         compiler_params=pltpu.CompilerParams(vmem_limit_bytes=VMEM),
         cost_estimate=pl.CostEstimate(flops=100_000_000, bytes_accessed=1_000_000, transcendentals=0),
         name="load",
-    )(order, *parts, inverse)
+    )(*parts, inverse)
 
 
 def span(rows, *terms):
@@ -489,14 +501,13 @@
         [own, close, rest, second, send_next], [packet(q) for q in (3, 2, 1)] + [[share(0)]]
     )
     arrived = [exchange(packet, lambda d, q=q: (3 - q) << 3) for q, packet in enumerate(packets)]
-    total, share = combine(
-        [own, close, rest, last, own_share] + arrived,
-        [
-            [span(TILE, *((i, 0) for i in (0, 1, 2, 3, 5, 6, 7)))],
-            [span(slot, (4, 0), (7, TILE), (6, TILE), (5, TILE))],
-        ],
-    )
-    return across_rest(total), across_rest(share)
+    block = span(TILE, *((i, 0) for i in (0, 1, 2, 3, 5, 6, 7)))
+    part = span(slot, (4, 0), (7, TILE), (6, TILE), (5, TILE))
+    packet, total = combine([own, close, rest, last, own_share] + arrived, [[block, part], [block]])
+    if lax.axis_size(AXES) == BLOCKS:
+        return packet, total
+    packet = across_rest(packet)
+    return packet, packet[:TILE]
 
 
 def across_rest(value):
@@ -511,25 +522,22 @@
     return [exchange(value, lambda d, q=q: q << 3) for q in range(1, 4)]
 
 
-def gather_near(total, share):
+def gather_near(packet):
     slot = TILE // GROUPS
-    (packet,) = combine([total, share], [[span(TILE, (0, 0)), span(slot, (1, 0))]])
     return combine(
         [packet] + along_z(packet),
         [[span(TILE, (q, 0)) for q in range(4)], [span(slot, (q, TILE)) for q in range(4)]],
     )
 
 
-def gather_last(total, share, mask):
+def gather_last(packet, total, mask):
     slot = TILE // GROUPS
-    (packet,) = combine([total, share], [[span(TILE, (0, 0)), span(slot, (1, 0))]])
-    arrived = along_z(packet)
     return combine(
-        [total, share] + arrived + [exchange(total, mask)],
+        [packet] + along_z(packet) + [exchange(total, mask)],
         [
-            [span(TILE, (i, 0)) for i in (2, 3, 4)],
-            [span(slot, (1, 0))] + [span(slot, (i, TILE)) for i in (2, 3, 4)],
-            [span(TILE, (0, 0)), span(TILE, (5, 0))],
+            [span(TILE, (q, 0)) for q in (1, 2, 3)],
+            [span(slot, (q, TILE)) for q in range(4)],
+            [span(TILE, (0, 0)), span(TILE, (4, 0))],
         ],
     )
 
@@ -538,18 +546,16 @@
     groups = lax.axis_size(AXES)
     samples_total = dosage.shape[0] * groups
     kept_total = keep_rows.shape[0] * groups
-    device = lax.axis_index("wide") * lax.axis_size("narrow") + lax.axis_index("narrow")
-    order = jnp.concatenate([block_order(device), group_order(device)])
     keep = keep_rows.reshape(-1, TILE)
     counts = allele_counts.reshape(-1, TILE)
-    standard, _, turned, gram, kept = standardize(samples_total, order, dosage, keep, counts, projection)
-    total, share = scatter_sum(turned, standard, gram)
-    near, share = gather_near(total, share)
+    standard, _, turned, gram, kept = standardize(samples_total, dosage, keep, counts, projection)
+    packet, _ = scatter_sum(turned, standard, gram)
+    near, share = gather_near(packet)
     across = exchange(near, second_mask)
     other = exchange(share, core_mask)
     later, other = lax.optimization_barrier((near, other))
     along = exchange(later, first_mask)
-    middle = begin_inverse(HALF, share, other, order)
+    middle = begin_inverse(HALF, share, other)
     across, middle = lax.optimization_barrier((across, middle))
     corner = exchange(across, first_mask)
     inverse = end_inverse(HALF, *middle)
@@ -558,17 +564,15 @@
     corner, begun = lax.optimization_barrier((corner, begun))
     late = [exchange(along, core_mask), corner, exchange(corner, core_mask)]
     ranges = [(24, 4), (12, 4), (28, 4)]
-    projected, turned, gram = project(late, ranges, begun, inverse, order, standard, kept)
-    total, share = scatter_sum(turned, standard, gram)
+    projected, turned, gram = project(late, ranges, begun, inverse, standard, kept)
+    packet, total = scatter_sum(turned, standard, gram)
     chosen = pick_rows(keep, projected)
-    total, chosen = lax.optimization_barrier((total, chosen))
-    near, share, corners = gather_last(total, share, lambda d: 4)
+    packet, total, chosen = lax.optimization_barrier((packet, total, chosen))
+    near, share, corners = gather_last(packet, total, lambda d: 4)
     beside = exchange(near, lambda d: 4)
-    inverse = invert_factor(share, exchange(share, core_mask), order)
+    inverse = invert_factor(share, exchange(share, core_mask))
     scores = score(math.sqrt(kept_total), chosen, inverse)
-    position = jnp.array([0, 4, 1, 2, 3, 5, 6, 7], jnp.int32)
-    place = (lax.axis_index("wide") & 7) ^ (((position & 3) << 1) | (position >> 2))
-    loadings = load(place, [corners, near, beside], inverse)
+    loadings = load((0, 4, 1, 2, 3, 5, 6, 7), [corners, near, beside], inverse)
     return (scores, loadings)
 
 

time: 106 us -> 104 us (0.981)
  Pallas kernels: 29.5 us -> 27.3 us
    pallas_call x2, Pallas kernels: 6.93 us -> 5.86 us  [begin_inverse(): pl.pallas_call(functools.partial(begin_kernel_inverse, last), in_specs=[O...]
  transfers between devices with their start and end apart: 35 -> 35, of which waited for: 20 -> 20; matrix products, arithmetic and copies ran while one was open for 0% -> 0% of each run, Pallas kernels for 15% -> 14%
where the time goes in v4:
time: 104 us
  starting transfers between devices  41.6 us (40%)
  waiting for transfers between devices  34.1 us (33%)
  Pallas kernels  27.3 us (26%)
    ppermute x35, starting transfers between devices, exchange(): lax.ppermute(value, AXES, [(d, d ^ mask_of(d)) for d in range(count)])  41.6 us
    ppermute x35, waiting for transfers between devices, exchange(): lax.ppermute(value, AXES, [(d, d ^ mask_of(d)) for d in range(count)])  34.1 us
    pallas_call x1, Pallas kernels, standardize(): pl.pallas_call(functools.partial(standard_kernel, samples_total), in_spec...  7.36 us
    pallas_call x2, Pallas kernels, begin_inverse(): pl.pallas_call(functools.partial(begin_kernel_inverse, last), in_specs=[O...  5.86 us
    pallas_call x8, Pallas kernels, totals(): pl.pallas_call(functools.partial(totals_kernel, low, high), in_specs=[ON_...  4.43 us
    pallas_call x1, Pallas kernels, begin_project(): pl.pallas_call(functools.partial(begin_kernel, len(parts), base), in_spec...  2.14 us
  transfers between devices with their start and end apart: 35, of which 20 were waited for; matrix products, arithmetic and copies ran while one was open for 0% of the time, Pallas kernels for 14%

profile of v4, /device:TPU:0, one launch (start us, length us, event | category | flops | bytes accessed | tf_op | source)
XLA Modules:
  0.0 103.8 jit_solution(17059154434711596756)
XLA Ops:
  0.6 7.4 %standardize.1 = (bf16[1024,4096]{1,0:T(8,128)(2,1)S(1)}, bf16[1024,128]{1,0:T(8,128)(2,1)}, bf16[128,1024]{1,0:T(8,128)(2,1)S(1)}, f32[128,128]{1,0:T(8,128)S(1)}, f32[1024,128]{1,0:T(8,128)S(1)}) custom-call(bf16[1024,4096]{1,0:T(8,128)(2,1)} %dosage.1, s32[7,128]{1,0:T(8,128)} %bitcast.2, s32[32,128]{1,0:T(8,128)} %bitcast.4, bf16[4096,128]{1,0:T(8,128)(2,1)} %projection.1), custom_call_target="tpu_custom_call" | custom-call | flops 1073741824 | bytes 16777216 | tf_op jit(solution)/shard_map/standardize/pallas_call | solution.py:156
  10.7 2.9 %collective-permute-start.4 = (f32[448,128]{1,0:T(8,128)S(1)}, f32[448,128]{1,0:T(8,128)S(1)}, u32[]{:S(2)}, u32[]{:S(2)}) collective-permute-start(f32[448,128]{1,0:T(8,128)S(1)} %get-tuple-element.46.refs_3_), channel_id=1, source_target_pairs={{0,4},{1,3},{2,6},{3,1},{4,0},{5,7},{6,2},{7,5},{8,12},{9,11},{10,... | collective-permute-start | bytes 688136 | tf_op jit(solution)/shard_map/ppermute | solution.py:64
  14.3 3.4 %collective-permute-done.4.refs_2_ = f32[448,128]{1,0:T(8,128)S(1)} collective-permute-done((f32[448,128]{1,0:T(8,128)S(1)}, f32[448,128]{1,0:T(8,128)S(1)}, u32[]{:S(2)}, u32[]{:S(2)}) %collective-permute-start.4) | collective-permute-done | bytes 229408 | tf_op jit(solution)/shard_map/ppermute | solution.py:64
  17.7 2.1 %collective-permute-start.5 = (f32[448,128]{1,0:T(8,128)S(1)}, f32[448,128]{1,0:T(8,128)S(1)}, u32[]{:S(2)}, u32[]{:S(2)}) collective-permute-start(f32[448,128]{1,0:T(8,128)S(1)} %combine.14.refs_4_), channel_id=1, source_target_pairs={{0,2},{1,5},{2,0},{3,7},{4,6},{5,1},{6,4},{7,3},{8,10},{9,13},{10,... | collective-permute-start | bytes 688136 | tf_op jit(solution)/shard_map/ppermute | solution.py:64
  19.8 2.5 %collective-permute-done.2.refs_2_ = f32[640,128]{1,0:T(8,128)S(1)} collective-permute-done((f32[640,128]{1,0:T(8,128)S(1)}, f32[640,128]{1,0:T(8,128)S(1)}, u32[]{:S(2)}, u32[]{:S(2)}) %collective-permute-start.2) | collective-permute-done | bytes 327712 | tf_op jit(solution)/shard_map/ppermute | solution.py:64
  23.8 4.2 %collective-permute-start.6 = (f32[144,128]{1,0:T(8,128)S(1)}, f32[144,128]{1,0:T(8,128)S(1)}, u32[]{:S(2)}, u32[]{:S(2)}) collective-permute-start(f32[144,128]{1,0:T(8,128)S(1)} %get-tuple-element.48), channel_id=1, source_target_pairs={{0,24},{1,25},{2,26},{3,27},{4,28},{5,29},{6,30},{7,31},{8,16},{9,... | collective-permute-start | bytes 221192 | tf_op jit(solution)/shard_map/ppermute | solution.py:64
  30.4 2.6 %collective-permute-done.3.refs_3_ = f32[128,128]{1,0:T(8,128)S(1)} collective-permute-done((f32[128,128]{1,0:T(8,128)S(1)}, f32[128,128]{1,0:T(8,128)S(1)}, u32[]{:S(2)}, u32[]{:S(2)}) %collective-permute-start.3) | collective-permute-done | bytes 65568 | tf_op jit(solution)/shard_map/ppermute | solution.py:64
  36.2 2.2 %collective-permute-start.11 = (f32[144,128]{1,0:T(8,128)S(1)}, f32[144,128]{1,0:T(8,128)S(1)}, u32[]{:S(2)}, u32[]{:S(2)}) collective-permute-start(f32[144,128]{1,0:T(8,128)S(1)} %get-tuple-element.51.refs_0_), channel_id=1, source_target_pairs={{0,24},{1,25},{2,26},{3,27},{4,28},{5,29},{6,30},{7,31},{8,16},{9,... | collective-permute-start | bytes 221192 | tf_op jit(solution)/shard_map/ppermute | solution.py:64
  38.5 4.4 %collective-permute-done.10.refs_2_ = f32[144,128]{1,0:T(8,128)S(1)} collective-permute-done((f32[144,128]{1,0:T(8,128)S(1)}, f32[144,128]{1,0:T(8,128)S(1)}, u32[]{:S(2)}, u32[]{:S(2)}) %collective-permute-start.10) | collective-permute-done | bytes 73760 | tf_op jit(solution)/shard_map/ppermute | solution.py:64
  47.8 1.9 %begin_inverse.2 = (f32[128,128]{1,0:T(8,128)S(1)}, f32[128,128]{1,0:T(8,128)S(1)}) custom-call(f32[64,128]{1,0:T(8,128)S(1)} %get-tuple-element.53.own, f32[64,128]{1,0:T(8,128)S(1)} %collective-permute-done.12.other), custom_call_target="tpu_custom_call" | custom-call | flops 1000000000 | bytes 8000000 | tf_op jit(solution)/shard_map/begin_inverse/pallas_call | solution.py:370
  52.4 1.7 %end_inverse.1.refs_5_.refs_4_ = f32[128,128]{1,0:T(8,128)S(1)} custom-call(f32[128,128]{1,0:T(8,128)S(1)} %get-tuple-element.59.left_in, f32[128,128]{1,0:T(8,128)S(1)} %get-tuple-element.60.right_in), custom_call_target="tpu_custom_call" | custom-call | flops 1000000000 | bytes 8000000 | tf_op jit(solution)/shard_map/end_inverse/pallas_call | solution.py:382
  55.6 2.1 %begin_project.1.refs_3_ = f32[1024,128]{1,0:T(8,128)S(1)} custom-call(f32[512,128]{1,0:T(8,128)S(1)} %get-tuple-element.54.refs_0_, f32[512,128]{1,0:T(8,128)S(1)} %collective-permute-done.15.refs_1_, f32[512,128]{1,0:T(8,128)S(1)} %collective-permute-done.13.refs_2_, f32[512,128]{1,0:T(8,128)S(1)} %collective-permute-done.17.refs_3_, ...), custom_call_target="tpu_custom_call" | custom-call | flops 671088640 | bytes 5242880 | tf_op jit(solution)/shard_map/begin_project/pallas_call | solution.py:270
  59.3 1.9 %project.1 = (bf16[1024,128]{1,0:T(8,128)(2,1)S(1)}, bf16[128,1024]{1,0:T(8,128)(2,1)S(1)}, f32[128,128]{1,0:T(8,128)S(1)}) custom-call(f32[512,128]{1,0:T(8,128)S(1)} %collective-permute-done.14.refs_0_, f32[512,128]{1,0:T(8,128)S(1)} %collective-permute-done.16.refs_1_, f32[512,128]{1,0:T(8,128)S(1)} %collective-permute-done.19.refs_2_, ...), custom_call_target="tpu_custom_call" | custom-call | flops 402653184 | bytes 3145728 | tf_op jit(solution)/shard_map/project/pallas_call | solution.py:294
  66.5 3.4 %collective-permute-done.24.refs_2_ = f32[448,128]{1,0:T(8,128)S(1)} collective-permute-done((f32[448,128]{1,0:T(8,128)S(1)}, f32[448,128]{1,0:T(8,128)S(1)}, u32[]{:S(2)}, u32[]{:S(2)}) %collective-permute-start.24) | collective-permute-done | bytes 229408 | tf_op jit(solution)/shard_map/ppermute | solution.py:64
  70.0 2.2 %collective-permute-start.25 = (f32[448,128]{1,0:T(8,128)S(1)}, f32[448,128]{1,0:T(8,128)S(1)}, u32[]{:S(2)}, u32[]{:S(2)}) collective-permute-start(f32[448,128]{1,0:T(8,128)S(1)} %combine.20.refs_4_), channel_id=1, source_target_pairs={{0,2},{1,5},{2,0},{3,7},{4,6},{5,1},{6,4},{7,3},{8,10},{9,13},{10,... | collective-permute-start | bytes 688136 | tf_op jit(solution)/shard_map/ppermute | solution.py:64
  72.2 2.3 %collective-permute-done.22.refs_2_ = f32[640,128]{1,0:T(8,128)S(1)} collective-permute-done((f32[640,128]{1,0:T(8,128)S(1)}, f32[640,128]{1,0:T(8,128)S(1)}, u32[]{:S(2)}, u32[]{:S(2)}) %collective-permute-start.22) | collective-permute-done | bytes 327712 | tf_op jit(solution)/shard_map/ppermute | solution.py:64
  76.3 2.2 %collective-permute-start.26 = (f32[144,128]{1,0:T(8,128)S(1)}, f32[144,128]{1,0:T(8,128)S(1)}, u32[]{:S(2)}, u32[]{:S(2)}) collective-permute-start(f32[144,128]{1,0:T(8,128)S(1)} %get-tuple-element.69), channel_id=1, source_target_pairs={{0,24},{1,25},{2,26},{3,27},{4,28},{5,29},{6,30},{7,31},{8,16},{9,... | collective-permute-start | bytes 221192 | tf_op jit(solution)/shard_map/ppermute | solution.py:64
  78.5 2.2 %collective-permute-start.28 = (f32[144,128]{1,0:T(8,128)S(1)}, f32[144,128]{1,0:T(8,128)S(1)}, u32[]{:S(2)}, u32[]{:S(2)}) collective-permute-start(f32[144,128]{1,0:T(8,128)S(1)} %get-tuple-element.71), channel_id=1, source_target_pairs={{0,8},{1,9},{2,10},{3,11},{4,12},{5,13},{6,14},{7,15},{8,0},{9,1},... | collective-permute-start | bytes 221192 | tf_op jit(solution)/shard_map/ppermute | solution.py:64
  80.7 2.1 %collective-permute-start.23 = (f32[128,128]{1,0:T(8,128)S(1)}, f32[128,128]{1,0:T(8,128)S(1)}, u32[]{:S(2)}, u32[]{:S(2)}) collective-permute-start(f32[128,128]{1,0:T(8,128)S(1)} %combine.19), channel_id=1, source_target_pairs={{0,2},{1,5},{2,0},{3,7},{4,6},{5,1},{6,4},{7,3},{8,10},{9,13},{10,... | collective-permute-start | bytes 196616 | tf_op jit(solution)/shard_map/ppermute | solution.py:64
  85.7 2.6 %collective-permute-start.30 = (f32[144,128]{1,0:T(8,128)S(1)}, f32[144,128]{1,0:T(8,128)S(1)}, u32[]{:S(2)}, u32[]{:S(2)}) collective-permute-start(f32[144,128]{1,0:T(8,128)S(1)} %get-tuple-element.76.refs_0_), channel_id=1, source_target_pairs={{0,16},{1,17},{2,18},{3,19},{4,20},{5,21},{6,22},{7,23},{8,24},{9,... | collective-permute-start | bytes 221192 | tf_op jit(solution)/shard_map/ppermute | solution.py:64
  88.3 1.8 %collective-permute-start.31 = (f32[144,128]{1,0:T(8,128)S(1)}, f32[144,128]{1,0:T(8,128)S(1)}, u32[]{:S(2)}, u32[]{:S(2)}) collective-permute-start(f32[144,128]{1,0:T(8,128)S(1)} %get-tuple-element.76.refs_0_), channel_id=1, source_target_pairs={{0,24},{1,25},{2,26},{3,27},{4,28},{5,29},{6,30},{7,31},{8,16},{9,... | collective-permute-start | bytes 221192 | tf_op jit(solution)/shard_map/ppermute | solution.py:64
  90.1 1.8 %collective-permute-start.32 = (f32[128,128]{1,0:T(8,128)S(1)}, f32[128,128]{1,0:T(8,128)S(1)}, u32[]{:S(2)}, u32[]{:S(2)}) collective-permute-start(f32[128,128]{1,0:T(8,128)S(1)} %get-tuple-element.77), channel_id=1, source_target_pairs={{0,4},{1,5},{2,6},{3,7},{4,0},{5,1},{6,2},{7,3},{8,12},{9,13},{10,... | collective-permute-start | bytes 196616 | tf_op jit(solution)/shard_map/ppermute | solution.py:64
  91.9 2.4 %collective-permute-done.32.refs_4_ = f32[128,128]{1,0:T(8,128)S(1)} collective-permute-done((f32[128,128]{1,0:T(8,128)S(1)}, f32[128,128]{1,0:T(8,128)S(1)}, u32[]{:S(2)}, u32[]{:S(2)}) %collective-permute-start.32) | collective-permute-done | bytes 65568 | tf_op jit(solution)/shard_map/ppermute | solution.py:64
  97.6 4.0 %begin_inverse.3 = (f32[128,128]{1,0:T(8,128)}, f32[128,128]{1,0:T(8,128)S(1)}) custom-call(f32[64,128]{1,0:T(8,128)S(1)} %get-tuple-element.78.own, f32[64,128]{1,0:T(8,128)S(1)} %collective-permute-done.33.other), custom_call_target="tpu_custom_call" | custom-call | flops 1000000000 | bytes 8000000 | tf_op jit(solution)/shard_map/begin_inverse/pallas_call | solution.py:370
  (77 shorter events, 36.7 us)
Async XLA Ops:
  9.6 4.6 %collective-permute-start = (f32[1024,128]{1,0:T(8,128)S(1)}, f32[1024,128]{1,0:T(8,128)S(1)}, u32[]{:S(2)}, u32[]{:S(2)}) collective-permute-start(f32[1024,128]{1,0:T(8,128)S(1)} %totals.9), channel_id=1, source_target_pairs={{0,1},{1,0},{2,3},{3,2},{4,5},{5,4},{6,7},{7,6},{8,9},{9,8},{10,11... | collective-permute-start | bytes 1572872 | tf_op jit(solution)/shard_map/ppermute | solution.py:64
  10.7 6.9 %collective-permute-start.4 = (f32[448,128]{1,0:T(8,128)S(1)}, f32[448,128]{1,0:T(8,128)S(1)}, u32[]{:S(2)}, u32[]{:S(2)}) collective-permute-start(f32[448,128]{1,0:T(8,128)S(1)} %get-tuple-element.46.refs_3_), channel_id=1, source_target_pairs={{0,4},{1,3},{2,6},{3,1},{4,0},{5,7},{6,2},{7,5},{8,12},{9,11},{10,... | collective-permute-start | bytes 688136 | tf_op jit(solution)/shard_map/ppermute | solution.py:64
  13.6 8.6 %collective-permute-start.2 = (f32[640,128]{1,0:T(8,128)S(1)}, f32[640,128]{1,0:T(8,128)S(1)}, u32[]{:S(2)}, u32[]{:S(2)}) collective-permute-start(f32[640,128]{1,0:T(8,128)S(1)} %get-tuple-element.45), channel_id=1, source_target_pairs={{0,4},{1,3},{2,6},{3,1},{4,0},{5,7},{6,2},{7,5},{8,12},{9,11},{10,... | collective-permute-start | bytes 983048 | tf_op jit(solution)/shard_map/ppermute | solution.py:64
  17.7 6.1 %collective-permute-start.5 = (f32[448,128]{1,0:T(8,128)S(1)}, f32[448,128]{1,0:T(8,128)S(1)}, u32[]{:S(2)}, u32[]{:S(2)}) collective-permute-start(f32[448,128]{1,0:T(8,128)S(1)} %combine.14.refs_4_), channel_id=1, source_target_pairs={{0,2},{1,5},{2,0},{3,7},{4,6},{5,1},{6,4},{7,3},{8,10},{9,13},{10,... | collective-permute-start | bytes 688136 | tf_op jit(solution)/shard_map/ppermute | solution.py:64
  23.8 9.2 %collective-permute-start.6 = (f32[144,128]{1,0:T(8,128)S(1)}, f32[144,128]{1,0:T(8,128)S(1)}, u32[]{:S(2)}, u32[]{:S(2)}) collective-permute-start(f32[144,128]{1,0:T(8,128)S(1)} %get-tuple-element.48), channel_id=1, source_target_pairs={{0,24},{1,25},{2,26},{3,27},{4,28},{5,29},{6,30},{7,31},{8,16},{9,... | collective-permute-start | bytes 221192 | tf_op jit(solution)/shard_map/ppermute | solution.py:64
  28.0 6.3 %collective-permute-start.7 = (f32[144,128]{1,0:T(8,128)S(1)}, f32[144,128]{1,0:T(8,128)S(1)}, u32[]{:S(2)}, u32[]{:S(2)}) collective-permute-start(f32[144,128]{1,0:T(8,128)S(1)} %get-tuple-element.49), channel_id=1, source_target_pairs={{0,16},{1,17},{2,18},{3,19},{4,20},{5,21},{6,22},{7,23},{8,24},{9,... | collective-permute-start | bytes 221192 | tf_op jit(solution)/shard_map/ppermute | solution.py:64
  28.0 6.3 %collective-permute-start.8 = (f32[144,128]{1,0:T(8,128)S(1)}, f32[144,128]{1,0:T(8,128)S(1)}, u32[]{:S(2)}, u32[]{:S(2)}) collective-permute-start(f32[144,128]{1,0:T(8,128)S(1)} %get-tuple-element.50), channel_id=1, source_target_pairs={{0,8},{1,9},{2,10},{3,11},{4,12},{5,13},{6,14},{7,15},{8,0},{9,1},... | collective-permute-start | bytes 221192 | tf_op jit(solution)/shard_map/ppermute | solution.py:64
  35.0 7.9 %collective-permute-start.10 = (f32[144,128]{1,0:T(8,128)S(1)}, f32[144,128]{1,0:T(8,128)S(1)}, u32[]{:S(2)}, u32[]{:S(2)}) collective-permute-start(f32[144,128]{1,0:T(8,128)S(1)} %get-tuple-element.51.refs_0_), channel_id=1, source_target_pairs={{0,16},{1,17},{2,18},{3,19},{4,20},{5,21},{6,22},{7,23},{8,24},{9,... | collective-permute-start | bytes 221192 | tf_op jit(solution)/shard_map/ppermute | solution.py:64
  36.2 6.8 %collective-permute-start.11 = (f32[144,128]{1,0:T(8,128)S(1)}, f32[144,128]{1,0:T(8,128)S(1)}, u32[]{:S(2)}, u32[]{:S(2)}) collective-permute-start(f32[144,128]{1,0:T(8,128)S(1)} %get-tuple-element.51.refs_0_), channel_id=1, source_target_pairs={{0,24},{1,25},{2,26},{3,27},{4,28},{5,29},{6,30},{7,31},{8,16},{9,... | collective-permute-start | bytes 221192 | tf_op jit(solution)/shard_map/ppermute | solution.py:64
  38.4 5.1 %collective-permute-start.9 = (f32[144,128]{1,0:T(8,128)S(1)}, f32[144,128]{1,0:T(8,128)S(1)}, u32[]{:S(2)}, u32[]{:S(2)}) collective-permute-start(f32[144,128]{1,0:T(8,128)S(1)} %get-tuple-element.51.refs_0_), channel_id=1, source_target_pairs={{0,8},{1,9},{2,10},{3,11},{4,12},{5,13},{6,14},{7,15},{8,0},{9,1},... | collective-permute-start | bytes 221192 | tf_op jit(solution)/shard_map/ppermute | solution.py:64
  43.5 7.6 %collective-permute-start.15 = (f32[512,128]{1,0:T(8,128)S(1)}, f32[512,128]{1,0:T(8,128)S(1)}, u32[]{:S(2)}, u32[]{:S(2)}) collective-permute-start(f32[512,128]{1,0:T(8,128)S(1)} %get-tuple-element.54.refs_0_), channel_id=1, source_target_pairs={{0,2},{1,5},{2,0},{3,7},{4,6},{5,1},{6,4},{7,3},{8,10},{9,13},{10,... | collective-permute-start | bytes 786440 | tf_op jit(solution)/shard_map/ppermute | solution.py:64
  45.2 10.4 %collective-permute-start.17 = (f32[512,128]{1,0:T(8,128)S(1)}, f32[512,128]{1,0:T(8,128)S(1)}, u32[]{:S(2)}, u32[]{:S(2)}) collective-permute-start(f32[512,128]{1,0:T(8,128)S(1)} %get-tuple-element.54.refs_0_), channel_id=1, source_target_pairs={{0,1},{1,0},{2,3},{3,2},{4,5},{5,4},{6,7},{7,6},{8,9},{9,8},{10,11... | collective-permute-start | bytes 786440 | tf_op jit(solution)/shard_map/ppermute | solution.py:64
  46.4 7.8 %collective-permute-start.13 = (f32[512,128]{1,0:T(8,128)S(1)}, f32[512,128]{1,0:T(8,128)S(1)}, u32[]{:S(2)}, u32[]{:S(2)}) collective-permute-start(f32[512,128]{1,0:T(8,128)S(1)} %get-tuple-element.54.refs_0_), channel_id=1, source_target_pairs={{0,4},{1,3},{2,6},{3,1},{4,0},{5,7},{6,2},{7,5},{8,12},{9,11},{10,... | collective-permute-start | bytes 786440 | tf_op jit(solution)/shard_map/ppermute | solution.py:64
  51.1 6.6 %collective-permute-start.16 = (f32[512,128]{1,0:T(8,128)S(1)}, f32[512,128]{1,0:T(8,128)S(1)}, u32[]{:S(2)}, u32[]{:S(2)}) collective-permute-start(f32[512,128]{1,0:T(8,128)S(1)} %collective-permute-done.15.refs_1_), channel_id=1, source_target_pairs={{0,4},{1,3},{2,6},{3,1},{4,0},{5,7},{6,2},{7,5},{8,12},{9,11},{10,... | collective-permute-start | bytes 786440 | tf_op jit(solution)/shard_map/ppermute | solution.py:64
  63.9 6.1 %collective-permute-start.24 = (f32[448,128]{1,0:T(8,128)S(1)}, f32[448,128]{1,0:T(8,128)S(1)}, u32[]{:S(2)}, u32[]{:S(2)}) collective-permute-start(f32[448,128]{1,0:T(8,128)S(1)} %get-tuple-element.67.refs_3_), channel_id=1, source_target_pairs={{0,4},{1,3},{2,6},{3,1},{4,0},{5,7},{6,2},{7,5},{8,12},{9,11},{10,... | collective-permute-start | bytes 688136 | tf_op jit(solution)/shard_map/ppermute | solution.py:64
  65.3 9.2 %collective-permute-start.22 = (f32[640,128]{1,0:T(8,128)S(1)}, f32[640,128]{1,0:T(8,128)S(1)}, u32[]{:S(2)}, u32[]{:S(2)}) collective-permute-start(f32[640,128]{1,0:T(8,128)S(1)} %get-tuple-element.66), channel_id=1, source_target_pairs={{0,4},{1,3},{2,6},{3,1},{4,0},{5,7},{6,2},{7,5},{8,12},{9,11},{10,... | collective-permute-start | bytes 983048 | tf_op jit(solution)/shard_map/ppermute | solution.py:64
  70.0 6.2 %collective-permute-start.25 = (f32[448,128]{1,0:T(8,128)S(1)}, f32[448,128]{1,0:T(8,128)S(1)}, u32[]{:S(2)}, u32[]{:S(2)}) collective-permute-start(f32[448,128]{1,0:T(8,128)S(1)} %combine.20.refs_4_), channel_id=1, source_target_pairs={{0,2},{1,5},{2,0},{3,7},{4,6},{5,1},{6,4},{7,3},{8,10},{9,13},{10,... | collective-permute-start | bytes 688136 | tf_op jit(solution)/shard_map/ppermute | solution.py:64
  76.3 8.8 %collective-permute-start.26 = (f32[144,128]{1,0:T(8,128)S(1)}, f32[144,128]{1,0:T(8,128)S(1)}, u32[]{:S(2)}, u32[]{:S(2)}) collective-permute-start(f32[144,128]{1,0:T(8,128)S(1)} %get-tuple-element.69), channel_id=1, source_target_pairs={{0,24},{1,25},{2,26},{3,27},{4,28},{5,29},{6,30},{7,31},{8,16},{9,... | collective-permute-start | bytes 221192 | tf_op jit(solution)/shard_map/ppermute | solution.py:64
  78.4 7.2 %collective-permute-start.27 = (f32[144,128]{1,0:T(8,128)S(1)}, f32[144,128]{1,0:T(8,128)S(1)}, u32[]{:S(2)}, u32[]{:S(2)}) collective-permute-start(f32[144,128]{1,0:T(8,128)S(1)} %get-tuple-element.70), channel_id=1, source_target_pairs={{0,16},{1,17},{2,18},{3,19},{4,20},{5,21},{6,22},{7,23},{8,24},{9,... | collective-permute-start | bytes 221192 | tf_op jit(solution)/shard_map/ppermute | solution.py:64
  78.5 7.1 %collective-permute-start.28 = (f32[144,128]{1,0:T(8,128)S(1)}, f32[144,128]{1,0:T(8,128)S(1)}, u32[]{:S(2)}, u32[]{:S(2)}) collective-permute-start(f32[144,128]{1,0:T(8,128)S(1)} %get-tuple-element.71), channel_id=1, source_target_pairs={{0,8},{1,9},{2,10},{3,11},{4,12},{5,13},{6,14},{7,15},{8,0},{9,1},... | collective-permute-start | bytes 221192 | tf_op jit(solution)/shard_map/ppermute | solution.py:64
  85.6 8.7 %collective-permute-start.29 = (f32[144,128]{1,0:T(8,128)S(1)}, f32[144,128]{1,0:T(8,128)S(1)}, u32[]{:S(2)}, u32[]{:S(2)}) collective-permute-start(f32[144,128]{1,0:T(8,128)S(1)} %get-tuple-element.76.refs_0_), channel_id=1, source_target_pairs={{0,8},{1,9},{2,10},{3,11},{4,12},{5,13},{6,14},{7,15},{8,0},{9,1},... | collective-permute-start | bytes 221192 | tf_op jit(solution)/shard_map/ppermute | solution.py:64
  85.7 9.1 %collective-permute-start.30 = (f32[144,128]{1,0:T(8,128)S(1)}, f32[144,128]{1,0:T(8,128)S(1)}, u32[]{:S(2)}, u32[]{:S(2)}) collective-permute-start(f32[144,128]{1,0:T(8,128)S(1)} %get-tuple-element.76.refs_0_), channel_id=1, source_target_pairs={{0,16},{1,17},{2,18},{3,19},{4,20},{5,21},{6,22},{7,23},{8,24},{9,... | collective-permute-start | bytes 221192 | tf_op jit(solution)/shard_map/ppermute | solution.py:64
  88.3 6.5 %collective-permute-start.31 = (f32[144,128]{1,0:T(8,128)S(1)}, f32[144,128]{1,0:T(8,128)S(1)}, u32[]{:S(2)}, u32[]{:S(2)}) collective-permute-start(f32[144,128]{1,0:T(8,128)S(1)} %get-tuple-element.76.refs_0_), channel_id=1, source_target_pairs={{0,24},{1,25},{2,26},{3,27},{4,28},{5,29},{6,30},{7,31},{8,16},{9,... | collective-permute-start | bytes 221192 | tf_op jit(solution)/shard_map/ppermute | solution.py:64
  94.9 7.8 %collective-permute-start.34 = (f32[384,128]{1,0:T(8,128)S(1)}, f32[384,128]{1,0:T(8,128)S(1)}, u32[]{:S(2)}, u32[]{:S(2)}) collective-permute-start(f32[384,128]{1,0:T(8,128)S(1)} %get-tuple-element.81.refs_1_), channel_id=1, source_target_pairs={{0,4},{1,5},{2,6},{3,7},{4,0},{5,1},{6,2},{7,3},{8,12},{9,13},{10,... | collective-permute-start | bytes 589832 | tf_op jit(solution)/shard_map/ppermute | solution.py:64
  (12 other events, 52.5 us)

commit v5 on v4

--- a/solution.py
+++ b/solution.py
@@ -12,6 +12,8 @@
 TILE = 128
 BLOCKS = 32
 ROWS = 256
+STRIP = 64
+SPLIT = 96
 VMEM = 28 * 1024 * 1024
 SMALL = 16 * 1024 * 1024
 GROUPS = 8
@@ -81,7 +83,7 @@
     return (((place >> 2) ^ (device & 1)) << 2) | ((place & 3) ^ ((device >> 3) & 3))
 
 
-def standard_kernel(samples_total, dosage, keep, counts, projection, standard, projected, turned, gram, kept, rows_in, sketch_in, keep_in, counts_in, table, basis, whole, sems):
+def standard_kernel(samples_total, dosage, keep, counts, projection, standard, projected, turned, gram, kept, far, rows_in, sketch_in, keep_in, counts_in, table, basis, whole, sems):
     samples = dosage.shape[0]
     steps = samples // ROWS
     device = this_device()
@@ -105,6 +107,9 @@
     frequency = counts_in[...].astype(jnp.float32) / (2.0 * samples_total)
     table[0] = 2.0 * frequency
     table[1] = 1.0 / jnp.sqrt(2.0 * frequency * (1.0 - frequency))
+    for p in range(BLOCKS):
+        table[2, p : p + 1, :] = table[0, pl.ds(order[p], 1), :]
+        table[3, p : p + 1, :] = table[1, pl.ds(order[p], 1), :]
     for i in range(samples // TILE):
         rows = lax.broadcasted_iota(jnp.int32, (TILE, TILE), 0) + i * TILE
         found = jnp.zeros((TILE, TILE), jnp.float32)
@@ -118,15 +123,16 @@
             for p in range(BLOCKS):
                 start = pl.multiple_of(order[p] * TILE, TILE)
                 basis[p * TILE : (p + 1) * TILE, :] = sketch_in[pl.ds(start, TILE), :]
-        for p in range(BLOCKS):
-            block = order[p]
-            center = table[0, pl.ds(block, 1), :]
-            scale = table[1, pl.ds(block, 1), :]
-            value = rows_in[slab, pl.ds(pl.multiple_of(block * TILE, TILE), TILE)].astype(jnp.float32)
-            standard[slab, p * TILE : (p + 1) * TILE] = ((value - center) * scale).astype(jnp.bfloat16)
+        for row in range(slab.start, slab.stop, STRIP):
+            strip = slice(row, row + STRIP)
+            for p in range(BLOCKS):
+                value = rows_in[strip, pl.ds(pl.multiple_of(order[p] * TILE, TILE), TILE)].astype(jnp.float32)
+                value = (value - table[2, p : p + 1, :]) * table[3, p : p + 1, :]
+                standard[strip, p * TILE : (p + 1) * TILE] = value.astype(jnp.bfloat16)
     value = jnp.dot(standard[...], basis[...], preferred_element_type=jnp.float32)
     finish_rows(value, kept, projected, turned, whole)
     share_gram(whole, gram)
+    totals_kernel(24, 32, turned, standard, gram, far)
 
 
 def share_gram(whole, gram):
@@ -156,20 +162,21 @@
     return pl.pallas_call(
         functools.partial(standard_kernel, samples_total),
         in_specs=[FAR, FAR, FAR, FAR],
-        out_specs=[ON_CHIP] * 5,
+        out_specs=[ON_CHIP] * 6,
         out_shape=[
             jax.ShapeDtypeStruct((samples, snps), jnp.bfloat16),
             jax.ShapeDtypeStruct((samples, TILE), jnp.bfloat16),
             jax.ShapeDtypeStruct((TILE, samples), jnp.bfloat16),
             jax.ShapeDtypeStruct((TILE, TILE), jnp.float32),
             jax.ShapeDtypeStruct((samples, TILE), jnp.float32),
+            jax.ShapeDtypeStruct((8 * TILE + HALF, TILE), jnp.float32),
         ],
         scratch_shapes=[
             pltpu.VMEM((samples, snps), jnp.bfloat16),
             pltpu.VMEM(arrays[3].shape, jnp.bfloat16),
             pltpu.VMEM(arrays[1].shape, jnp.int32),
             pltpu.VMEM(arrays[2].shape, jnp.int32),
-            pltpu.VMEM((2,) + arrays[2].shape, jnp.float32),
+            pltpu.VMEM((4,) + arrays[2].shape, jnp.float32),
             pltpu.VMEM(arrays[3].shape, jnp.bfloat16),
             pltpu.VMEM((TILE, TILE), jnp.float32),
             pltpu.SemaphoreType.DMA((3 + samples // ROWS,)),
@@ -463,13 +470,13 @@
     return (rows, terms)
 
 
-def scatter_sum(turned, standard, gram):
+def scatter_sum(turned, standard, gram, far):
     four = 4 * TILE
     eight = 8 * TILE
     slot = TILE // GROUPS
     half = TILE // 2
     three = 3 * TILE
-    far = exchange(totals(turned, standard, 24, 32, gram), core_mask)
+    far = exchange(far, core_mask)
     upper = totals(turned, standard, 8, 16)
     send, send_rest = combine(
         [upper, far, gram],
@@ -548,24 +555,24 @@
     kept_total = keep_rows.shape[0] * groups
     keep = keep_rows.reshape(-1, TILE)
     counts = allele_counts.reshape(-1, TILE)
-    standard, _, turned, gram, kept = standardize(samples_total, dosage, keep, counts, projection)
-    packet, _ = scatter_sum(turned, standard, gram)
+    standard, _, turned, gram, kept, far = standardize(samples_total, dosage, keep, counts, projection)
+    packet, _ = scatter_sum(turned, standard, gram, far)
     near, share = gather_near(packet)
     across = exchange(near, second_mask)
     other = exchange(share, core_mask)
     later, other = lax.optimization_barrier((near, other))
     along = exchange(later, first_mask)
-    middle = begin_inverse(HALF, share, other)
+    middle = begin_inverse(SPLIT, share, other)
     across, middle = lax.optimization_barrier((across, middle))
     corner = exchange(across, first_mask)
-    inverse = end_inverse(HALF, *middle)
+    inverse = end_inverse(SPLIT, *middle)
     early = [near, across, along] + [exchange(part, core_mask) for part in (near, across)]
     begun = begin_project(early, [(0, 4), (4, 4), (8, 4), (16, 4), (20, 4)], inverse, standard)
     corner, begun = lax.optimization_barrier((corner, begun))
     late = [exchange(along, core_mask), corner, exchange(corner, core_mask)]
     ranges = [(24, 4), (12, 4), (28, 4)]
     projected, turned, gram = project(late, ranges, begun, inverse, standard, kept)
-    packet, total = scatter_sum(turned, standard, gram)
+    packet, total = scatter_sum(turned, standard, gram, totals(turned, standard, 24, 32, gram))
     chosen = pick_rows(keep, projected)
     packet, total, chosen = lax.optimization_barrier((packet, total, chosen))
     near, share, corners = gather_last(packet, total, lambda d: 4)

time: 104 us -> 103 us (level)
    pallas_call x8 -> x7, Pallas kernels: 4.43 us -> 3.87 us  [totals(): pl.pallas_call(functools.partial(totals_kernel, low, high), in_specs=[ON_...]
  transfers between devices with their start and end apart: 35 -> 35, of which waited for: 20 -> 21; matrix products, arithmetic and copies ran while one was open for 0% -> 0% of each run, Pallas kernels for 14% -> 15%
where the time goes in v5:
time: 103 us
  starting transfers between devices  41.7 us (40%)
  waiting for transfers between devices  33.6 us (33%)
  Pallas kernels  26.9 us (26%)
    ppermute x35, starting transfers between devices, exchange(): lax.ppermute(value, AXES, [(d, d ^ mask_of(d)) for d in range(count)])  41.7 us
    ppermute x35, waiting for transfers between devices, exchange(): lax.ppermute(value, AXES, [(d, d ^ mask_of(d)) for d in range(count)])  33.6 us
    pallas_call x1, Pallas kernels, standardize(): pl.pallas_call(functools.partial(standard_kernel, samples_total), in_spec...  7.5 us
    pallas_call x2, Pallas kernels, begin_inverse(): pl.pallas_call(functools.partial(begin_kernel_inverse, last), in_specs=[O...  6.8 us
    pallas_call x7, Pallas kernels, totals(): pl.pallas_call(functools.partial(totals_kernel, low, high), in_specs=[ON_...  3.87 us
    pallas_call x1, Pallas kernels, begin_project(): pl.pallas_call(functools.partial(begin_kernel, len(parts), base), in_spec...  2.14 us
  transfers between devices with their start and end apart: 35, of which 21 were waited for; matrix products, arithmetic and copies ran while one was open for 0% of the time, Pallas kernels for 15%

profile of v5, /device:TPU:0, one launch (start us, length us, event | category | flops | bytes accessed | tf_op | source)
XLA Modules:
  0.0 103.1 jit_solution(13720453969550897723)
XLA Ops:
  0.6 7.5 %standardize.1 = (bf16[1024,4096]{1,0:T(8,128)(2,1)S(1)}, bf16[1024,128]{1,0:T(8,128)(2,1)}, bf16[128,1024]{1,0:T(8,128)(2,1)S(1)}, f32[128,128]{1,0:T(8,128)S(1...) custom-call(bf16[1024,4096]{1,0:T(8,128)(2,1)} %dosage.1, s32[7,128]{1,0:T(8,128)} %bitcast.2, s32[32,128]{1,0:T(8,128)} %bitcast.4, ...), custom_call_target="tpu_custom_call" | custom-call | flops 1073741824 | bytes 16777216 | tf_op jit(solution)/shard_map/standardize/pallas_call | solution.py:162
  10.3 2.9 %collective-permute-start.4 = (f32[448,128]{1,0:T(8,128)S(1)}, f32[448,128]{1,0:T(8,128)S(1)}, u32[]{:S(2)}, u32[]{:S(2)}) collective-permute-start(f32[448,128]{1,0:T(8,128)S(1)} %get-tuple-element.48.refs_3_), channel_id=1, source_target_pairs={{0,4},{1,3},{2,6},{3,1},{4,0},{5,7},{6,2},{7,5},{8,12},{9,11},{10,... | collective-permute-start | bytes 688136 | tf_op jit(solution)/shard_map/ppermute | solution.py:66
  13.9 3.4 %collective-permute-done.4.refs_2_ = f32[448,128]{1,0:T(8,128)S(1)} collective-permute-done((f32[448,128]{1,0:T(8,128)S(1)}, f32[448,128]{1,0:T(8,128)S(1)}, u32[]{:S(2)}, u32[]{:S(2)}) %collective-permute-start.4) | collective-permute-done | bytes 229408 | tf_op jit(solution)/shard_map/ppermute | solution.py:66
  17.3 2.1 %collective-permute-start.5 = (f32[448,128]{1,0:T(8,128)S(1)}, f32[448,128]{1,0:T(8,128)S(1)}, u32[]{:S(2)}, u32[]{:S(2)}) collective-permute-start(f32[448,128]{1,0:T(8,128)S(1)} %combine.14.refs_4_), channel_id=1, source_target_pairs={{0,2},{1,5},{2,0},{3,7},{4,6},{5,1},{6,4},{7,3},{8,10},{9,13},{10,... | collective-permute-start | bytes 688136 | tf_op jit(solution)/shard_map/ppermute | solution.py:66
  19.4 2.5 %collective-permute-done.2.refs_2_ = f32[640,128]{1,0:T(8,128)S(1)} collective-permute-done((f32[640,128]{1,0:T(8,128)S(1)}, f32[640,128]{1,0:T(8,128)S(1)}, u32[]{:S(2)}, u32[]{:S(2)}) %collective-permute-start.2) | collective-permute-done | bytes 327712 | tf_op jit(solution)/shard_map/ppermute | solution.py:66
  23.4 4.2 %collective-permute-start.6 = (f32[144,128]{1,0:T(8,128)S(1)}, f32[144,128]{1,0:T(8,128)S(1)}, u32[]{:S(2)}, u32[]{:S(2)}) collective-permute-start(f32[144,128]{1,0:T(8,128)S(1)} %get-tuple-element.50), channel_id=1, source_target_pairs={{0,24},{1,25},{2,26},{3,27},{4,28},{5,29},{6,30},{7,31},{8,16},{9,... | collective-permute-start | bytes 221192 | tf_op jit(solution)/shard_map/ppermute | solution.py:66
  28.3 1.7 %collective-permute-start.3 = (f32[128,128]{1,0:T(8,128)S(1)}, f32[128,128]{1,0:T(8,128)S(1)}, u32[]{:S(2)}, u32[]{:S(2)}) collective-permute-start(f32[128,128]{1,0:T(8,128)S(1)} %combine.13), channel_id=1, source_target_pairs={{0,2},{1,5},{2,0},{3,7},{4,6},{5,1},{6,4},{7,3},{8,10},{9,13},{10,... | collective-permute-start | bytes 196616 | tf_op jit(solution)/shard_map/ppermute | solution.py:66
  30.0 2.6 %collective-permute-done.3.refs_3_ = f32[128,128]{1,0:T(8,128)S(1)} collective-permute-done((f32[128,128]{1,0:T(8,128)S(1)}, f32[128,128]{1,0:T(8,128)S(1)}, u32[]{:S(2)}, u32[]{:S(2)}) %collective-permute-start.3) | collective-permute-done | bytes 65568 | tf_op jit(solution)/shard_map/ppermute | solution.py:66
  35.7 2.2 %collective-permute-start.11 = (f32[144,128]{1,0:T(8,128)S(1)}, f32[144,128]{1,0:T(8,128)S(1)}, u32[]{:S(2)}, u32[]{:S(2)}) collective-permute-start(f32[144,128]{1,0:T(8,128)S(1)} %get-tuple-element.53.refs_0_), channel_id=1, source_target_pairs={{0,24},{1,25},{2,26},{3,27},{4,28},{5,29},{6,30},{7,31},{8,16},{9,... | collective-permute-start | bytes 221192 | tf_op jit(solution)/shard_map/ppermute | solution.py:66
  38.1 4.4 %collective-permute-done.10.refs_2_ = f32[144,128]{1,0:T(8,128)S(1)} collective-permute-done((f32[144,128]{1,0:T(8,128)S(1)}, f32[144,128]{1,0:T(8,128)S(1)}, u32[]{:S(2)}, u32[]{:S(2)}) %collective-permute-start.10) | collective-permute-done | bytes 73760 | tf_op jit(solution)/shard_map/ppermute | solution.py:66
  43.1 1.7 %collective-permute-start.15 = (f32[512,128]{1,0:T(8,128)S(1)}, f32[512,128]{1,0:T(8,128)S(1)}, u32[]{:S(2)}, u32[]{:S(2)}) collective-permute-start(f32[512,128]{1,0:T(8,128)S(1)} %get-tuple-element.56.refs_0_), channel_id=1, source_target_pairs={{0,2},{1,5},{2,0},{3,7},{4,6},{5,1},{6,4},{7,3},{8,10},{9,13},{10,... | collective-permute-start | bytes 786440 | tf_op jit(solution)/shard_map/ppermute | solution.py:66
  47.5 2.8 %begin_inverse.2 = (f32[128,128]{1,0:T(8,128)S(1)}, f32[128,128]{1,0:T(8,128)S(1)}) custom-call(f32[64,128]{1,0:T(8,128)S(1)} %get-tuple-element.55.own, f32[64,128]{1,0:T(8,128)S(1)} %collective-permute-done.12.other), custom_call_target="tpu_custom_call" | custom-call | flops 1000000000 | bytes 8000000 | tf_op jit(solution)/shard_map/begin_inverse/pallas_call | solution.py:377
  54.2 2.1 %begin_project.1.refs_3_ = f32[1024,128]{1,0:T(8,128)S(1)} custom-call(f32[512,128]{1,0:T(8,128)S(1)} %get-tuple-element.56.refs_0_, f32[512,128]{1,0:T(8,128)S(1)} %collective-permute-done.15.refs_1_, f32[512,128]{1,0:T(8,128)S(1)} %collective-permute-done.13.refs_2_, f32[512,128]{1,0:T(8,128)S(1)} %collective-permute-done.17.refs_3_, ...), custom_call_target="tpu_custom_call" | custom-call | flops 671088640 | bytes 5242880 | tf_op jit(solution)/shard_map/begin_project/pallas_call | solution.py:277
  58.6 1.9 %project.1 = (bf16[1024,128]{1,0:T(8,128)(2,1)S(1)}, bf16[128,1024]{1,0:T(8,128)(2,1)S(1)}, f32[128,128]{1,0:T(8,128)S(1)}) custom-call(f32[512,128]{1,0:T(8,128)S(1)} %collective-permute-done.14.refs_0_, f32[512,128]{1,0:T(8,128)S(1)} %collective-permute-done.16.refs_1_, f32[512,128]{1,0:T(8,128)S(1)} %collective-permute-done.19.refs_2_, ...), custom_call_target="tpu_custom_call" | custom-call | flops 402653184 | bytes 3145728 | tf_op jit(solution)/shard_map/project/pallas_call | solution.py:301
  65.8 3.4 %collective-permute-done.24.refs_2_ = f32[448,128]{1,0:T(8,128)S(1)} collective-permute-done((f32[448,128]{1,0:T(8,128)S(1)}, f32[448,128]{1,0:T(8,128)S(1)}, u32[]{:S(2)}, u32[]{:S(2)}) %collective-permute-start.24) | collective-permute-done | bytes 229408 | tf_op jit(solution)/shard_map/ppermute | solution.py:66
  69.3 2.5 %collective-permute-start.25 = (f32[448,128]{1,0:T(8,128)S(1)}, f32[448,128]{1,0:T(8,128)S(1)}, u32[]{:S(2)}, u32[]{:S(2)}) collective-permute-start(f32[448,128]{1,0:T(8,128)S(1)} %combine.20.refs_4_), channel_id=1, source_target_pairs={{0,2},{1,5},{2,0},{3,7},{4,6},{5,1},{6,4},{7,3},{8,10},{9,13},{10,... | collective-permute-start | bytes 688136 | tf_op jit(solution)/shard_map/ppermute | solution.py:66
  73.5 2.3 %collective-permute-done.25.refs_3_ = f32[448,128]{1,0:T(8,128)S(1)} collective-permute-done((f32[448,128]{1,0:T(8,128)S(1)}, f32[448,128]{1,0:T(8,128)S(1)}, u32[]{:S(2)}, u32[]{:S(2)}) %collective-permute-start.25) | collective-permute-done | bytes 229408 | tf_op jit(solution)/shard_map/ppermute | solution.py:66
  75.9 2.1 %collective-permute-start.26 = (f32[144,128]{1,0:T(8,128)S(1)}, f32[144,128]{1,0:T(8,128)S(1)}, u32[]{:S(2)}, u32[]{:S(2)}) collective-permute-start(f32[144,128]{1,0:T(8,128)S(1)} %get-tuple-element.71), channel_id=1, source_target_pairs={{0,24},{1,25},{2,26},{3,27},{4,28},{5,29},{6,30},{7,31},{8,16},{9,... | collective-permute-start | bytes 221192 | tf_op jit(solution)/shard_map/ppermute | solution.py:66
  78.1 2.2 %collective-permute-start.28 = (f32[144,128]{1,0:T(8,128)S(1)}, f32[144,128]{1,0:T(8,128)S(1)}, u32[]{:S(2)}, u32[]{:S(2)}) collective-permute-start(f32[144,128]{1,0:T(8,128)S(1)} %get-tuple-element.73), channel_id=1, source_target_pairs={{0,8},{1,9},{2,10},{3,11},{4,12},{5,13},{6,14},{7,15},{8,0},{9,1},... | collective-permute-start | bytes 221192 | tf_op jit(solution)/shard_map/ppermute | solution.py:66
  80.3 2.1 %collective-permute-start.23 = (f32[128,128]{1,0:T(8,128)S(1)}, f32[128,128]{1,0:T(8,128)S(1)}, u32[]{:S(2)}, u32[]{:S(2)}) collective-permute-start(f32[128,128]{1,0:T(8,128)S(1)} %combine.19), channel_id=1, source_target_pairs={{0,2},{1,5},{2,0},{3,7},{4,6},{5,1},{6,4},{7,3},{8,10},{9,13},{10,... | collective-permute-start | bytes 196616 | tf_op jit(solution)/shard_map/ppermute | solution.py:66
  85.3 2.6 %collective-permute-start.30 = (f32[144,128]{1,0:T(8,128)S(1)}, f32[144,128]{1,0:T(8,128)S(1)}, u32[]{:S(2)}, u32[]{:S(2)}) collective-permute-start(f32[144,128]{1,0:T(8,128)S(1)} %get-tuple-element.78.refs_0_), channel_id=1, source_target_pairs={{0,16},{1,17},{2,18},{3,19},{4,20},{5,21},{6,22},{7,23},{8,24},{9,... | collective-permute-start | bytes 221192 | tf_op jit(solution)/shard_map/ppermute | solution.py:66
  87.9 1.8 %collective-permute-start.31 = (f32[144,128]{1,0:T(8,128)S(1)}, f32[144,128]{1,0:T(8,128)S(1)}, u32[]{:S(2)}, u32[]{:S(2)}) collective-permute-start(f32[144,128]{1,0:T(8,128)S(1)} %get-tuple-element.78.refs_0_), channel_id=1, source_target_pairs={{0,24},{1,25},{2,26},{3,27},{4,28},{5,29},{6,30},{7,31},{8,16},{9,... | collective-permute-start | bytes 221192 | tf_op jit(solution)/shard_map/ppermute | solution.py:66
  91.2 2.7 %collective-permute-done.32.refs_4_ = f32[128,128]{1,0:T(8,128)S(1)} collective-permute-done((f32[128,128]{1,0:T(8,128)S(1)}, f32[128,128]{1,0:T(8,128)S(1)}, u32[]{:S(2)}, u32[]{:S(2)}) %collective-permute-start.32) | collective-permute-done | bytes 65568 | tf_op jit(solution)/shard_map/ppermute | solution.py:66
  96.9 4.0 %begin_inverse.3 = (f32[128,128]{1,0:T(8,128)}, f32[128,128]{1,0:T(8,128)S(1)}) custom-call(f32[64,128]{1,0:T(8,128)S(1)} %get-tuple-element.80.own, f32[64,128]{1,0:T(8,128)S(1)} %collective-permute-done.33.other), custom_call_target="tpu_custom_call" | custom-call | flops 1000000000 | bytes 8000000 | tf_op jit(solution)/shard_map/begin_inverse/pallas_call | solution.py:377
  (76 shorter events, 34.3 us)
Async XLA Ops:
  9.2 4.7 %collective-permute-start = (f32[1024,128]{1,0:T(8,128)S(1)}, f32[1024,128]{1,0:T(8,128)S(1)}, u32[]{:S(2)}, u32[]{:S(2)}) collective-permute-start(f32[1024,128]{1,0:T(8,128)S(1)} %totals.8), channel_id=1, source_target_pairs={{0,1},{1,0},{2,3},{3,2},{4,5},{5,4},{6,7},{7,6},{8,9},{9,8},{10,11... | collective-permute-start | bytes 1572872 | tf_op jit(solution)/shard_map/ppermute | solution.py:66
  10.3 6.9 %collective-permute-start.4 = (f32[448,128]{1,0:T(8,128)S(1)}, f32[448,128]{1,0:T(8,128)S(1)}, u32[]{:S(2)}, u32[]{:S(2)}) collective-permute-start(f32[448,128]{1,0:T(8,128)S(1)} %get-tuple-element.48.refs_3_), channel_id=1, source_target_pairs={{0,4},{1,3},{2,6},{3,1},{4,0},{5,7},{6,2},{7,5},{8,12},{9,11},{10,... | collective-permute-start | bytes 688136 | tf_op jit(solution)/shard_map/ppermute | solution.py:66
  13.2 8.7 %collective-permute-start.2 = (f32[640,128]{1,0:T(8,128)S(1)}, f32[640,128]{1,0:T(8,128)S(1)}, u32[]{:S(2)}, u32[]{:S(2)}) collective-permute-start(f32[640,128]{1,0:T(8,128)S(1)} %get-tuple-element.47), channel_id=1, source_target_pairs={{0,4},{1,3},{2,6},{3,1},{4,0},{5,7},{6,2},{7,5},{8,12},{9,11},{10,... | collective-permute-start | bytes 983048 | tf_op jit(solution)/shard_map/ppermute | solution.py:66
  17.3 6.1 %collective-permute-start.5 = (f32[448,128]{1,0:T(8,128)S(1)}, f32[448,128]{1,0:T(8,128)S(1)}, u32[]{:S(2)}, u32[]{:S(2)}) collective-permute-start(f32[448,128]{1,0:T(8,128)S(1)} %combine.14.refs_4_), channel_id=1, source_target_pairs={{0,2},{1,5},{2,0},{3,7},{4,6},{5,1},{6,4},{7,3},{8,10},{9,13},{10,... | collective-permute-start | bytes 688136 | tf_op jit(solution)/shard_map/ppermute | solution.py:66
  23.4 9.2 %collective-permute-start.6 = (f32[144,128]{1,0:T(8,128)S(1)}, f32[144,128]{1,0:T(8,128)S(1)}, u32[]{:S(2)}, u32[]{:S(2)}) collective-permute-start(f32[144,128]{1,0:T(8,128)S(1)} %get-tuple-element.50), channel_id=1, source_target_pairs={{0,24},{1,25},{2,26},{3,27},{4,28},{5,29},{6,30},{7,31},{8,16},{9,... | collective-permute-start | bytes 221192 | tf_op jit(solution)/shard_map/ppermute | solution.py:66
  27.6 6.3 %collective-permute-start.7 = (f32[144,128]{1,0:T(8,128)S(1)}, f32[144,128]{1,0:T(8,128)S(1)}, u32[]{:S(2)}, u32[]{:S(2)}) collective-permute-start(f32[144,128]{1,0:T(8,128)S(1)} %get-tuple-element.51), channel_id=1, source_target_pairs={{0,16},{1,17},{2,18},{3,19},{4,20},{5,21},{6,22},{7,23},{8,24},{9,... | collective-permute-start | bytes 221192 | tf_op jit(solution)/shard_map/ppermute | solution.py:66
  27.6 6.3 %collective-permute-start.8 = (f32[144,128]{1,0:T(8,128)S(1)}, f32[144,128]{1,0:T(8,128)S(1)}, u32[]{:S(2)}, u32[]{:S(2)}) collective-permute-start(f32[144,128]{1,0:T(8,128)S(1)} %get-tuple-element.52), channel_id=1, source_target_pairs={{0,8},{1,9},{2,10},{3,11},{4,12},{5,13},{6,14},{7,15},{8,0},{9,1},... | collective-permute-start | bytes 221192 | tf_op jit(solution)/shard_map/ppermute | solution.py:66
  34.6 7.9 %collective-permute-start.10 = (f32[144,128]{1,0:T(8,128)S(1)}, f32[144,128]{1,0:T(8,128)S(1)}, u32[]{:S(2)}, u32[]{:S(2)}) collective-permute-start(f32[144,128]{1,0:T(8,128)S(1)} %get-tuple-element.53.refs_0_), channel_id=1, source_target_pairs={{0,16},{1,17},{2,18},{3,19},{4,20},{5,21},{6,22},{7,23},{8,24},{9,... | collective-permute-start | bytes 221192 | tf_op jit(solution)/shard_map/ppermute | solution.py:66
  35.7 6.8 %collective-permute-start.11 = (f32[144,128]{1,0:T(8,128)S(1)}, f32[144,128]{1,0:T(8,128)S(1)}, u32[]{:S(2)}, u32[]{:S(2)}) collective-permute-start(f32[144,128]{1,0:T(8,128)S(1)} %get-tuple-element.53.refs_0_), channel_id=1, source_target_pairs={{0,24},{1,25},{2,26},{3,27},{4,28},{5,29},{6,30},{7,31},{8,16},{9,... | collective-permute-start | bytes 221192 | tf_op jit(solution)/shard_map/ppermute | solution.py:66
  38.0 5.1 %collective-permute-start.9 = (f32[144,128]{1,0:T(8,128)S(1)}, f32[144,128]{1,0:T(8,128)S(1)}, u32[]{:S(2)}, u32[]{:S(2)}) collective-permute-start(f32[144,128]{1,0:T(8,128)S(1)} %get-tuple-element.53.refs_0_), channel_id=1, source_target_pairs={{0,8},{1,9},{2,10},{3,11},{4,12},{5,13},{6,14},{7,15},{8,0},{9,1},... | collective-permute-start | bytes 221192 | tf_op jit(solution)/shard_map/ppermute | solution.py:66
  43.1 7.6 %collective-permute-start.15 = (f32[512,128]{1,0:T(8,128)S(1)}, f32[512,128]{1,0:T(8,128)S(1)}, u32[]{:S(2)}, u32[]{:S(2)}) collective-permute-start(f32[512,128]{1,0:T(8,128)S(1)} %get-tuple-element.56.refs_0_), channel_id=1, source_target_pairs={{0,2},{1,5},{2,0},{3,7},{4,6},{5,1},{6,4},{7,3},{8,10},{9,13},{10,... | collective-permute-start | bytes 786440 | tf_op jit(solution)/shard_map/ppermute | solution.py:66
  44.8 9.5 %collective-permute-start.17 = (f32[512,128]{1,0:T(8,128)S(1)}, f32[512,128]{1,0:T(8,128)S(1)}, u32[]{:S(2)}, u32[]{:S(2)}) collective-permute-start(f32[512,128]{1,0:T(8,128)S(1)} %get-tuple-element.56.refs_0_), channel_id=1, source_target_pairs={{0,1},{1,0},{2,3},{3,2},{4,5},{5,4},{6,7},{7,6},{8,9},{9,8},{10,11... | collective-permute-start | bytes 786440 | tf_op jit(solution)/shard_map/ppermute | solution.py:66
  46.0 6.9 %collective-permute-start.13 = (f32[512,128]{1,0:T(8,128)S(1)}, f32[512,128]{1,0:T(8,128)S(1)}, u32[]{:S(2)}, u32[]{:S(2)}) collective-permute-start(f32[512,128]{1,0:T(8,128)S(1)} %get-tuple-element.56.refs_0_), channel_id=1, source_target_pairs={{0,4},{1,3},{2,6},{3,1},{4,0},{5,7},{6,2},{7,5},{8,12},{9,11},{10,... | collective-permute-start | bytes 786440 | tf_op jit(solution)/shard_map/ppermute | solution.py:66
  50.7 6.4 %collective-permute-start.16 = (f32[512,128]{1,0:T(8,128)S(1)}, f32[512,128]{1,0:T(8,128)S(1)}, u32[]{:S(2)}, u32[]{:S(2)}) collective-permute-start(f32[512,128]{1,0:T(8,128)S(1)} %collective-permute-done.15.refs_1_), channel_id=1, source_target_pairs={{0,4},{1,3},{2,6},{3,1},{4,0},{5,7},{6,2},{7,5},{8,12},{9,11},{10,... | collective-permute-start | bytes 786440 | tf_op jit(solution)/shard_map/ppermute | solution.py:66
  63.1 6.1 %collective-permute-start.24 = (f32[448,128]{1,0:T(8,128)S(1)}, f32[448,128]{1,0:T(8,128)S(1)}, u32[]{:S(2)}, u32[]{:S(2)}) collective-permute-start(f32[448,128]{1,0:T(8,128)S(1)} %get-tuple-element.69.refs_3_), channel_id=1, source_target_pairs={{0,4},{1,3},{2,6},{3,1},{4,0},{5,7},{6,2},{7,5},{8,12},{9,11},{10,... | collective-permute-start | bytes 688136 | tf_op jit(solution)/shard_map/ppermute | solution.py:66
  64.6 8.9 %collective-permute-start.22 = (f32[640,128]{1,0:T(8,128)S(1)}, f32[640,128]{1,0:T(8,128)S(1)}, u32[]{:S(2)}, u32[]{:S(2)}) collective-permute-start(f32[640,128]{1,0:T(8,128)S(1)} %get-tuple-element.68), channel_id=1, source_target_pairs={{0,4},{1,3},{2,6},{3,1},{4,0},{5,7},{6,2},{7,5},{8,12},{9,11},{10,... | collective-permute-start | bytes 983048 | tf_op jit(solution)/shard_map/ppermute | solution.py:66
  69.3 6.5 %collective-permute-start.25 = (f32[448,128]{1,0:T(8,128)S(1)}, f32[448,128]{1,0:T(8,128)S(1)}, u32[]{:S(2)}, u32[]{:S(2)}) collective-permute-start(f32[448,128]{1,0:T(8,128)S(1)} %combine.20.refs_4_), channel_id=1, source_target_pairs={{0,2},{1,5},{2,0},{3,7},{4,6},{5,1},{6,4},{7,3},{8,10},{9,13},{10,... | collective-permute-start | bytes 688136 | tf_op jit(solution)/shard_map/ppermute | solution.py:66
  75.9 8.8 %collective-permute-start.26 = (f32[144,128]{1,0:T(8,128)S(1)}, f32[144,128]{1,0:T(8,128)S(1)}, u32[]{:S(2)}, u32[]{:S(2)}) collective-permute-start(f32[144,128]{1,0:T(8,128)S(1)} %get-tuple-element.71), channel_id=1, source_target_pairs={{0,24},{1,25},{2,26},{3,27},{4,28},{5,29},{6,30},{7,31},{8,16},{9,... | collective-permute-start | bytes 221192 | tf_op jit(solution)/shard_map/ppermute | solution.py:66
  78.0 7.2 %collective-permute-start.27 = (f32[144,128]{1,0:T(8,128)S(1)}, f32[144,128]{1,0:T(8,128)S(1)}, u32[]{:S(2)}, u32[]{:S(2)}) collective-permute-start(f32[144,128]{1,0:T(8,128)S(1)} %get-tuple-element.72), channel_id=1, source_target_pairs={{0,16},{1,17},{2,18},{3,19},{4,20},{5,21},{6,22},{7,23},{8,24},{9,... | collective-permute-start | bytes 221192 | tf_op jit(solution)/shard_map/ppermute | solution.py:66
  78.1 7.1 %collective-permute-start.28 = (f32[144,128]{1,0:T(8,128)S(1)}, f32[144,128]{1,0:T(8,128)S(1)}, u32[]{:S(2)}, u32[]{:S(2)}) collective-permute-start(f32[144,128]{1,0:T(8,128)S(1)} %get-tuple-element.73), channel_id=1, source_target_pairs={{0,8},{1,9},{2,10},{3,11},{4,12},{5,13},{6,14},{7,15},{8,0},{9,1},... | collective-permute-start | bytes 221192 | tf_op jit(solution)/shard_map/ppermute | solution.py:66
  85.2 8.7 %collective-permute-start.29 = (f32[144,128]{1,0:T(8,128)S(1)}, f32[144,128]{1,0:T(8,128)S(1)}, u32[]{:S(2)}, u32[]{:S(2)}) collective-permute-start(f32[144,128]{1,0:T(8,128)S(1)} %get-tuple-element.78.refs_0_), channel_id=1, source_target_pairs={{0,8},{1,9},{2,10},{3,11},{4,12},{5,13},{6,14},{7,15},{8,0},{9,1},... | collective-permute-start | bytes 221192 | tf_op jit(solution)/shard_map/ppermute | solution.py:66
  85.3 8.8 %collective-permute-start.30 = (f32[144,128]{1,0:T(8,128)S(1)}, f32[144,128]{1,0:T(8,128)S(1)}, u32[]{:S(2)}, u32[]{:S(2)}) collective-permute-start(f32[144,128]{1,0:T(8,128)S(1)} %get-tuple-element.78.refs_0_), channel_id=1, source_target_pairs={{0,16},{1,17},{2,18},{3,19},{4,20},{5,21},{6,22},{7,23},{8,24},{9,... | collective-permute-start | bytes 221192 | tf_op jit(solution)/shard_map/ppermute | solution.py:66
  87.9 6.2 %collective-permute-start.31 = (f32[144,128]{1,0:T(8,128)S(1)}, f32[144,128]{1,0:T(8,128)S(1)}, u32[]{:S(2)}, u32[]{:S(2)}) collective-permute-start(f32[144,128]{1,0:T(8,128)S(1)} %get-tuple-element.78.refs_0_), channel_id=1, source_target_pairs={{0,24},{1,25},{2,26},{3,27},{4,28},{5,29},{6,30},{7,31},{8,16},{9,... | collective-permute-start | bytes 221192 | tf_op jit(solution)/shard_map/ppermute | solution.py:66
  94.1 7.8 %collective-permute-start.34 = (f32[384,128]{1,0:T(8,128)S(1)}, f32[384,128]{1,0:T(8,128)S(1)}, u32[]{:S(2)}, u32[]{:S(2)}) collective-permute-start(f32[384,128]{1,0:T(8,128)S(1)} %get-tuple-element.83.refs_1_), channel_id=1, source_target_pairs={{0,4},{1,5},{2,6},{3,7},{4,0},{5,1},{6,2},{7,3},{8,12},{9,13},{10,... | collective-permute-start | bytes 589832 | tf_op jit(solution)/shard_map/ppermute | solution.py:66
  (12 other events, 52.5 us)

commit v6 on v5

--- a/solution.py
+++ b/solution.py
@@ -537,15 +537,11 @@
     )
 
 
-def gather_last(packet, total, mask):
+def gather_last(packet):
     slot = TILE // GROUPS
     return combine(
-        [packet] + along_z(packet) + [exchange(total, mask)],
-        [
-            [span(TILE, (q, 0)) for q in (1, 2, 3)],
-            [span(slot, (q, TILE)) for q in range(4)],
-            [span(TILE, (0, 0)), span(TILE, (4, 0))],
-        ],
+        [packet] + along_z(packet),
+        [[span(TILE, (q, 0)) for q in (1, 2, 3)], [span(slot, (q, TILE)) for q in range(4)]],
     )
 
 
@@ -575,11 +571,13 @@
     packet, total = scatter_sum(turned, standard, gram, totals(turned, standard, 24, 32, gram))
     chosen = pick_rows(keep, projected)
     packet, total, chosen = lax.optimization_barrier((packet, total, chosen))
-    near, share, corners = gather_last(packet, total, lambda d: 4)
+    first_beside = exchange(total, lambda d: 4)
+    near, share = gather_last(packet)
     beside = exchange(near, lambda d: 4)
-    inverse = invert_factor(share, exchange(share, core_mask))
+    other, first_beside = lax.optimization_barrier((exchange(share, core_mask), first_beside))
+    inverse = invert_factor(share, other)
     scores = score(math.sqrt(kept_total), chosen, inverse)
-    loadings = load((0, 4, 1, 2, 3, 5, 6, 7), [corners, near, beside], inverse)
+    loadings = load((0, 4, 1, 2, 3, 5, 6, 7), [total, first_beside, near, beside], inverse)
     return (scores, loadings)
 
 

time: 103 us -> 103 us (level)
  transfers between devices with their start and end apart: 35 -> 35, of which waited for: 21 -> 20; matrix products, arithmetic and copies ran while one was open for 0% -> 0% of each run, Pallas kernels for 15% -> 15%
where the time goes in v6:
time: 103 us
  starting transfers between devices  41.7 us (40%)
  waiting for transfers between devices  33.6 us (33%)
  Pallas kernels  26.9 us (26%)
    ppermute x35, starting transfers between devices, exchange(): lax.ppermute(value, AXES, [(d, d ^ mask_of(d)) for d in range(count)])  41.7 us
    ppermute x35, waiting for transfers between devices, exchange(): lax.ppermute(value, AXES, [(d, d ^ mask_of(d)) for d in range(count)])  33.6 us
    pallas_call x1, Pallas kernels, standardize(): pl.pallas_call(functools.partial(standard_kernel, samples_total), in_spec...  7.5 us
    pallas_call x2, Pallas kernels, begin_inverse(): pl.pallas_call(functools.partial(begin_kernel_inverse, last), in_specs=[O...  6.8 us
    pallas_call x7, Pallas kernels, totals(): pl.pallas_call(functools.partial(totals_kernel, low, high), in_specs=[ON_...  3.87 us
    pallas_call x1, Pallas kernels, begin_project(): pl.pallas_call(functools.partial(begin_kernel, len(parts), base), in_spec...  2.14 us
  transfers between devices with their start and end apart: 35, of which 20 were waited for; matrix products, arithmetic and copies ran while one was open for 0% of the time, Pallas kernels for 15%

profile of v6, /device:TPU:0, one launch (start us, length us, event | category | flops | bytes accessed | tf_op | source)
XLA Modules:
  0.0 103.1 jit_solution(7848635773584704273)
XLA Ops:
  0.6 7.5 %standardize.1 = (bf16[1024,4096]{1,0:T(8,128)(2,1)S(1)}, bf16[1024,128]{1,0:T(8,128)(2,1)}, bf16[128,1024]{1,0:T(8,128)(2,1)S(1)}, f32[128,128]{1,0:T(8,128)S(1...) custom-call(bf16[1024,4096]{1,0:T(8,128)(2,1)} %dosage.1, s32[7,128]{1,0:T(8,128)} %bitcast.2, s32[32,128]{1,0:T(8,128)} %bitcast.4, ...), custom_call_target="tpu_custom_call" | custom-call | flops 1073741824 | bytes 16777216 | tf_op jit(solution)/shard_map/standardize/pallas_call | solution.py:162
  10.3 2.9 %collective-permute-start.4 = (f32[448,128]{1,0:T(8,128)S(1)}, f32[448,128]{1,0:T(8,128)S(1)}, u32[]{:S(2)}, u32[]{:S(2)}) collective-permute-start(f32[448,128]{1,0:T(8,128)S(1)} %get-tuple-element.49.refs_3_), channel_id=1, source_target_pairs={{0,4},{1,3},{2,6},{3,1},{4,0},{5,7},{6,2},{7,5},{8,12},{9,11},{10,... | collective-permute-start | bytes 688136 | tf_op jit(solution)/shard_map/ppermute | solution.py:66
  13.9 3.4 %collective-permute-done.4.refs_2_ = f32[448,128]{1,0:T(8,128)S(1)} collective-permute-done((f32[448,128]{1,0:T(8,128)S(1)}, f32[448,128]{1,0:T(8,128)S(1)}, u32[]{:S(2)}, u32[]{:S(2)}) %collective-permute-start.4) | collective-permute-done | bytes 229408 | tf_op jit(solution)/shard_map/ppermute | solution.py:66
  17.3 2.1 %collective-permute-start.5 = (f32[448,128]{1,0:T(8,128)S(1)}, f32[448,128]{1,0:T(8,128)S(1)}, u32[]{:S(2)}, u32[]{:S(2)}) collective-permute-start(f32[448,128]{1,0:T(8,128)S(1)} %combine.14.refs_4_), channel_id=1, source_target_pairs={{0,2},{1,5},{2,0},{3,7},{4,6},{5,1},{6,4},{7,3},{8,10},{9,13},{10,... | collective-permute-start | bytes 688136 | tf_op jit(solution)/shard_map/ppermute | solution.py:66
  19.4 2.5 %collective-permute-done.2.refs_2_ = f32[640,128]{1,0:T(8,128)S(1)} collective-permute-done((f32[640,128]{1,0:T(8,128)S(1)}, f32[640,128]{1,0:T(8,128)S(1)}, u32[]{:S(2)}, u32[]{:S(2)}) %collective-permute-start.2) | collective-permute-done | bytes 327712 | tf_op jit(solution)/shard_map/ppermute | solution.py:66
  23.4 4.2 %collective-permute-start.6 = (f32[144,128]{1,0:T(8,128)S(1)}, f32[144,128]{1,0:T(8,128)S(1)}, u32[]{:S(2)}, u32[]{:S(2)}) collective-permute-start(f32[144,128]{1,0:T(8,128)S(1)} %get-tuple-element.51), channel_id=1, source_target_pairs={{0,24},{1,25},{2,26},{3,27},{4,28},{5,29},{6,30},{7,31},{8,16},{9,... | collective-permute-start | bytes 221192 | tf_op jit(solution)/shard_map/ppermute | solution.py:66
  28.3 1.7 %collective-permute-start.3 = (f32[128,128]{1,0:T(8,128)S(1)}, f32[128,128]{1,0:T(8,128)S(1)}, u32[]{:S(2)}, u32[]{:S(2)}) collective-permute-start(f32[128,128]{1,0:T(8,128)S(1)} %combine.13), channel_id=1, source_target_pairs={{0,2},{1,5},{2,0},{3,7},{4,6},{5,1},{6,4},{7,3},{8,10},{9,13},{10,... | collective-permute-start | bytes 196616 | tf_op jit(solution)/shard_map/ppermute | solution.py:66
  30.0 2.6 %collective-permute-done.3.refs_3_ = f32[128,128]{1,0:T(8,128)S(1)} collective-permute-done((f32[128,128]{1,0:T(8,128)S(1)}, f32[128,128]{1,0:T(8,128)S(1)}, u32[]{:S(2)}, u32[]{:S(2)}) %collective-permute-start.3) | collective-permute-done | bytes 65568 | tf_op jit(solution)/shard_map/ppermute | solution.py:66
  35.7 2.2 %collective-permute-start.11 = (f32[144,128]{1,0:T(8,128)S(1)}, f32[144,128]{1,0:T(8,128)S(1)}, u32[]{:S(2)}, u32[]{:S(2)}) collective-permute-start(f32[144,128]{1,0:T(8,128)S(1)} %get-tuple-element.54.refs_0_), channel_id=1, source_target_pairs={{0,24},{1,25},{2,26},{3,27},{4,28},{5,29},{6,30},{7,31},{8,16},{9,... | collective-permute-start | bytes 221192 | tf_op jit(solution)/shard_map/ppermute | solution.py:66
  38.1 4.4 %collective-permute-done.10.refs_2_ = f32[144,128]{1,0:T(8,128)S(1)} collective-permute-done((f32[144,128]{1,0:T(8,128)S(1)}, f32[144,128]{1,0:T(8,128)S(1)}, u32[]{:S(2)}, u32[]{:S(2)}) %collective-permute-start.10) | collective-permute-done | bytes 73760 | tf_op jit(solution)/shard_map/ppermute | solution.py:66
  43.1 1.7 %collective-permute-start.15 = (f32[512,128]{1,0:T(8,128)S(1)}, f32[512,128]{1,0:T(8,128)S(1)}, u32[]{:S(2)}, u32[]{:S(2)}) collective-permute-start(f32[512,128]{1,0:T(8,128)S(1)} %get-tuple-element.57.refs_0_), channel_id=1, source_target_pairs={{0,2},{1,5},{2,0},{3,7},{4,6},{5,1},{6,4},{7,3},{8,10},{9,13},{10,... | collective-permute-start | bytes 786440 | tf_op jit(solution)/shard_map/ppermute | solution.py:66
  47.5 2.8 %begin_inverse.2 = (f32[128,128]{1,0:T(8,128)S(1)}, f32[128,128]{1,0:T(8,128)S(1)}) custom-call(f32[64,128]{1,0:T(8,128)S(1)} %get-tuple-element.56.own, f32[64,128]{1,0:T(8,128)S(1)} %collective-permute-done.12.other), custom_call_target="tpu_custom_call" | custom-call | flops 1000000000 | bytes 8000000 | tf_op jit(solution)/shard_map/begin_inverse/pallas_call | solution.py:377
  54.2 2.1 %begin_project.1.refs_3_ = f32[1024,128]{1,0:T(8,128)S(1)} custom-call(f32[512,128]{1,0:T(8,128)S(1)} %get-tuple-element.57.refs_0_, f32[512,128]{1,0:T(8,128)S(1)} %collective-permute-done.15.refs_1_, f32[512,128]{1,0:T(8,128)S(1)} %collective-permute-done.13.refs_2_, f32[512,128]{1,0:T(8,128)S(1)} %collective-permute-done.17.refs_3_, ...), custom_call_target="tpu_custom_call" | custom-call | flops 671088640 | bytes 5242880 | tf_op jit(solution)/shard_map/begin_project/pallas_call | solution.py:277
  58.6 1.9 %project.1 = (bf16[1024,128]{1,0:T(8,128)(2,1)S(1)}, bf16[128,1024]{1,0:T(8,128)(2,1)S(1)}, f32[128,128]{1,0:T(8,128)S(1)}) custom-call(f32[512,128]{1,0:T(8,128)S(1)} %collective-permute-done.14.refs_0_, f32[512,128]{1,0:T(8,128)S(1)} %collective-permute-done.16.refs_1_, f32[512,128]{1,0:T(8,128)S(1)} %collective-permute-done.19.refs_2_, ...), custom_call_target="tpu_custom_call" | custom-call | flops 402653184 | bytes 3145728 | tf_op jit(solution)/shard_map/project/pallas_call | solution.py:301
  65.8 3.4 %collective-permute-done.24.refs_2_ = f32[448,128]{1,0:T(8,128)S(1)} collective-permute-done((f32[448,128]{1,0:T(8,128)S(1)}, f32[448,128]{1,0:T(8,128)S(1)}, u32[]{:S(2)}, u32[]{:S(2)}) %collective-permute-start.24) | collective-permute-done | bytes 229408 | tf_op jit(solution)/shard_map/ppermute | solution.py:66
  69.3 2.5 %collective-permute-start.25 = (f32[448,128]{1,0:T(8,128)S(1)}, f32[448,128]{1,0:T(8,128)S(1)}, u32[]{:S(2)}, u32[]{:S(2)}) collective-permute-start(f32[448,128]{1,0:T(8,128)S(1)} %combine.20.refs_4_), channel_id=1, source_target_pairs={{0,2},{1,5},{2,0},{3,7},{4,6},{5,1},{6,4},{7,3},{8,10},{9,13},{10,... | collective-permute-start | bytes 688136 | tf_op jit(solution)/shard_map/ppermute | solution.py:66
  73.5 2.3 %collective-permute-done.25.refs_3_ = f32[448,128]{1,0:T(8,128)S(1)} collective-permute-done((f32[448,128]{1,0:T(8,128)S(1)}, f32[448,128]{1,0:T(8,128)S(1)}, u32[]{:S(2)}, u32[]{:S(2)}) %collective-permute-start.25) | collective-permute-done | bytes 229408 | tf_op jit(solution)/shard_map/ppermute | solution.py:66
  75.9 2.1 %collective-permute-start.26 = (f32[144,128]{1,0:T(8,128)S(1)}, f32[144,128]{1,0:T(8,128)S(1)}, u32[]{:S(2)}, u32[]{:S(2)}) collective-permute-start(f32[144,128]{1,0:T(8,128)S(1)} %get-tuple-element.72), channel_id=1, source_target_pairs={{0,24},{1,25},{2,26},{3,27},{4,28},{5,29},{6,30},{7,31},{8,16},{9,... | collective-permute-start | bytes 221192 | tf_op jit(solution)/shard_map/ppermute | solution.py:66
  78.1 2.2 %collective-permute-start.28 = (f32[144,128]{1,0:T(8,128)S(1)}, f32[144,128]{1,0:T(8,128)S(1)}, u32[]{:S(2)}, u32[]{:S(2)}) collective-permute-start(f32[144,128]{1,0:T(8,128)S(1)} %get-tuple-element.74), channel_id=1, source_target_pairs={{0,8},{1,9},{2,10},{3,11},{4,12},{5,13},{6,14},{7,15},{8,0},{9,1},... | collective-permute-start | bytes 221192 | tf_op jit(solution)/shard_map/ppermute | solution.py:66
  80.3 2.1 %collective-permute-start.23 = (f32[128,128]{1,0:T(8,128)S(1)}, f32[128,128]{1,0:T(8,128)S(1)}, u32[]{:S(2)}, u32[]{:S(2)}) collective-permute-start(f32[128,128]{1,0:T(8,128)S(1)} %combine.19), channel_id=1, source_target_pairs={{0,2},{1,5},{2,0},{3,7},{4,6},{5,1},{6,4},{7,3},{8,10},{9,13},{10,... | collective-permute-start | bytes 196616 | tf_op jit(solution)/shard_map/ppermute | solution.py:66
  85.3 2.6 %collective-permute-start.30 = (f32[144,128]{1,0:T(8,128)S(1)}, f32[144,128]{1,0:T(8,128)S(1)}, u32[]{:S(2)}, u32[]{:S(2)}) collective-permute-start(f32[144,128]{1,0:T(8,128)S(1)} %get-tuple-element.79.refs_0_), channel_id=1, source_target_pairs={{0,16},{1,17},{2,18},{3,19},{4,20},{5,21},{6,22},{7,23},{8,24},{9,... | collective-permute-start | bytes 221192 | tf_op jit(solution)/shard_map/ppermute | solution.py:66
  87.9 1.8 %collective-permute-start.31 = (f32[144,128]{1,0:T(8,128)S(1)}, f32[144,128]{1,0:T(8,128)S(1)}, u32[]{:S(2)}, u32[]{:S(2)}) collective-permute-start(f32[144,128]{1,0:T(8,128)S(1)} %get-tuple-element.79.refs_0_), channel_id=1, source_target_pairs={{0,24},{1,25},{2,26},{3,27},{4,28},{5,29},{6,30},{7,31},{8,16},{9,... | collective-permute-start | bytes 221192 | tf_op jit(solution)/shard_map/ppermute | solution.py:66
  91.2 2.9 %collective-permute-done.30.refs_2_ = f32[144,128]{1,0:T(8,128)S(1)} collective-permute-done((f32[144,128]{1,0:T(8,128)S(1)}, f32[144,128]{1,0:T(8,128)S(1)}, u32[]{:S(2)}, u32[]{:S(2)}) %collective-permute-start.30) | collective-permute-done | bytes 73760 | tf_op jit(solution)/shard_map/ppermute | solution.py:66
  96.9 4.0 %begin_inverse.3 = (f32[128,128]{1,0:T(8,128)}, f32[128,128]{1,0:T(8,128)S(1)}) custom-call(f32[64,128]{1,0:T(8,128)S(1)} %get-tuple-element.80.own, f32[64,128]{1,0:T(8,128)S(1)} %collective-permute-done.32.other), custom_call_target="tpu_custom_call" | custom-call | flops 1000000000 | bytes 8000000 | tf_op jit(solution)/shard_map/begin_inverse/pallas_call | solution.py:377
  (76 shorter events, 34.1 us)
Async XLA Ops:
  10.3 6.9 %collective-permute-start.4 = (f32[448,128]{1,0:T(8,128)S(1)}, f32[448,128]{1,0:T(8,128)S(1)}, u32[]{:S(2)}, u32[]{:S(2)}) collective-permute-start(f32[448,128]{1,0:T(8,128)S(1)} %get-tuple-element.49.refs_3_), channel_id=1, source_target_pairs={{0,4},{1,3},{2,6},{3,1},{4,0},{5,7},{6,2},{7,5},{8,12},{9,11},{10,... | collective-permute-start | bytes 688136 | tf_op jit(solution)/shard_map/ppermute | solution.py:66
  13.2 8.7 %collective-permute-start.2 = (f32[640,128]{1,0:T(8,128)S(1)}, f32[640,128]{1,0:T(8,128)S(1)}, u32[]{:S(2)}, u32[]{:S(2)}) collective-permute-start(f32[640,128]{1,0:T(8,128)S(1)} %get-tuple-element.48), channel_id=1, source_target_pairs={{0,4},{1,3},{2,6},{3,1},{4,0},{5,7},{6,2},{7,5},{8,12},{9,11},{10,... | collective-permute-start | bytes 983048 | tf_op jit(solution)/shard_map/ppermute | solution.py:66
  17.3 6.1 %collective-permute-start.5 = (f32[448,128]{1,0:T(8,128)S(1)}, f32[448,128]{1,0:T(8,128)S(1)}, u32[]{:S(2)}, u32[]{:S(2)}) collective-permute-start(f32[448,128]{1,0:T(8,128)S(1)} %combine.14.refs_4_), channel_id=1, source_target_pairs={{0,2},{1,5},{2,0},{3,7},{4,6},{5,1},{6,4},{7,3},{8,10},{9,13},{10,... | collective-permute-start | bytes 688136 | tf_op jit(solution)/shard_map/ppermute | solution.py:66
  23.4 9.2 %collective-permute-start.6 = (f32[144,128]{1,0:T(8,128)S(1)}, f32[144,128]{1,0:T(8,128)S(1)}, u32[]{:S(2)}, u32[]{:S(2)}) collective-permute-start(f32[144,128]{1,0:T(8,128)S(1)} %get-tuple-element.51), channel_id=1, source_target_pairs={{0,24},{1,25},{2,26},{3,27},{4,28},{5,29},{6,30},{7,31},{8,16},{9,... | collective-permute-start | bytes 221192 | tf_op jit(solution)/shard_map/ppermute | solution.py:66
  27.6 6.3 %collective-permute-start.7 = (f32[144,128]{1,0:T(8,128)S(1)}, f32[144,128]{1,0:T(8,128)S(1)}, u32[]{:S(2)}, u32[]{:S(2)}) collective-permute-start(f32[144,128]{1,0:T(8,128)S(1)} %get-tuple-element.52), channel_id=1, source_target_pairs={{0,16},{1,17},{2,18},{3,19},{4,20},{5,21},{6,22},{7,23},{8,24},{9,... | collective-permute-start | bytes 221192 | tf_op jit(solution)/shard_map/ppermute | solution.py:66
  27.6 6.3 %collective-permute-start.8 = (f32[144,128]{1,0:T(8,128)S(1)}, f32[144,128]{1,0:T(8,128)S(1)}, u32[]{:S(2)}, u32[]{:S(2)}) collective-permute-start(f32[144,128]{1,0:T(8,128)S(1)} %get-tuple-element.53), channel_id=1, source_target_pairs={{0,8},{1,9},{2,10},{3,11},{4,12},{5,13},{6,14},{7,15},{8,0},{9,1},... | collective-permute-start | bytes 221192 | tf_op jit(solution)/shard_map/ppermute | solution.py:66
  34.6 7.9 %collective-permute-start.10 = (f32[144,128]{1,0:T(8,128)S(1)}, f32[144,128]{1,0:T(8,128)S(1)}, u32[]{:S(2)}, u32[]{:S(2)}) collective-permute-start(f32[144,128]{1,0:T(8,128)S(1)} %get-tuple-element.54.refs_0_), channel_id=1, source_target_pairs={{0,16},{1,17},{2,18},{3,19},{4,20},{5,21},{6,22},{7,23},{8,24},{9,... | collective-permute-start | bytes 221192 | tf_op jit(solution)/shard_map/ppermute | solution.py:66
  35.7 6.8 %collective-permute-start.11 = (f32[144,128]{1,0:T(8,128)S(1)}, f32[144,128]{1,0:T(8,128)S(1)}, u32[]{:S(2)}, u32[]{:S(2)}) collective-permute-start(f32[144,128]{1,0:T(8,128)S(1)} %get-tuple-element.54.refs_0_), channel_id=1, source_target_pairs={{0,24},{1,25},{2,26},{3,27},{4,28},{5,29},{6,30},{7,31},{8,16},{9,... | collective-permute-start | bytes 221192 | tf_op jit(solution)/shard_map/ppermute | solution.py:66
  38.0 5.1 %collective-permute-start.9 = (f32[144,128]{1,0:T(8,128)S(1)}, f32[144,128]{1,0:T(8,128)S(1)}, u32[]{:S(2)}, u32[]{:S(2)}) collective-permute-start(f32[144,128]{1,0:T(8,128)S(1)} %get-tuple-element.54.refs_0_), channel_id=1, source_target_pairs={{0,8},{1,9},{2,10},{3,11},{4,12},{5,13},{6,14},{7,15},{8,0},{9,1},... | collective-permute-start | bytes 221192 | tf_op jit(solution)/shard_map/ppermute | solution.py:66
  43.1 7.6 %collective-permute-start.15 = (f32[512,128]{1,0:T(8,128)S(1)}, f32[512,128]{1,0:T(8,128)S(1)}, u32[]{:S(2)}, u32[]{:S(2)}) collective-permute-start(f32[512,128]{1,0:T(8,128)S(1)} %get-tuple-element.57.refs_0_), channel_id=1, source_target_pairs={{0,2},{1,5},{2,0},{3,7},{4,6},{5,1},{6,4},{7,3},{8,10},{9,13},{10,... | collective-permute-start | bytes 786440 | tf_op jit(solution)/shard_map/ppermute | solution.py:66
  44.8 9.5 %collective-permute-start.17 = (f32[512,128]{1,0:T(8,128)S(1)}, f32[512,128]{1,0:T(8,128)S(1)}, u32[]{:S(2)}, u32[]{:S(2)}) collective-permute-start(f32[512,128]{1,0:T(8,128)S(1)} %get-tuple-element.57.refs_0_), channel_id=1, source_target_pairs={{0,1},{1,0},{2,3},{3,2},{4,5},{5,4},{6,7},{7,6},{8,9},{9,8},{10,11... | collective-permute-start | bytes 786440 | tf_op jit(solution)/shard_map/ppermute | solution.py:66
  46.0 6.9 %collective-permute-start.13 = (f32[512,128]{1,0:T(8,128)S(1)}, f32[512,128]{1,0:T(8,128)S(1)}, u32[]{:S(2)}, u32[]{:S(2)}) collective-permute-start(f32[512,128]{1,0:T(8,128)S(1)} %get-tuple-element.57.refs_0_), channel_id=1, source_target_pairs={{0,4},{1,3},{2,6},{3,1},{4,0},{5,7},{6,2},{7,5},{8,12},{9,11},{10,... | collective-permute-start | bytes 786440 | tf_op jit(solution)/shard_map/ppermute | solution.py:66
  50.7 6.4 %collective-permute-start.16 = (f32[512,128]{1,0:T(8,128)S(1)}, f32[512,128]{1,0:T(8,128)S(1)}, u32[]{:S(2)}, u32[]{:S(2)}) collective-permute-start(f32[512,128]{1,0:T(8,128)S(1)} %collective-permute-done.15.refs_1_), channel_id=1, source_target_pairs={{0,4},{1,3},{2,6},{3,1},{4,0},{5,7},{6,2},{7,5},{8,12},{9,11},{10,... | collective-permute-start | bytes 786440 | tf_op jit(solution)/shard_map/ppermute | solution.py:66
  63.1 6.1 %collective-permute-start.24 = (f32[448,128]{1,0:T(8,128)S(1)}, f32[448,128]{1,0:T(8,128)S(1)}, u32[]{:S(2)}, u32[]{:S(2)}) collective-permute-start(f32[448,128]{1,0:T(8,128)S(1)} %get-tuple-element.70.refs_3_), channel_id=1, source_target_pairs={{0,4},{1,3},{2,6},{3,1},{4,0},{5,7},{6,2},{7,5},{8,12},{9,11},{10,... | collective-permute-start | bytes 688136 | tf_op jit(solution)/shard_map/ppermute | solution.py:66
  64.6 8.9 %collective-permute-start.22 = (f32[640,128]{1,0:T(8,128)S(1)}, f32[640,128]{1,0:T(8,128)S(1)}, u32[]{:S(2)}, u32[]{:S(2)}) collective-permute-start(f32[640,128]{1,0:T(8,128)S(1)} %get-tuple-element.69), channel_id=1, source_target_pairs={{0,4},{1,3},{2,6},{3,1},{4,0},{5,7},{6,2},{7,5},{8,12},{9,11},{10,... | collective-permute-start | bytes 983048 | tf_op jit(solution)/shard_map/ppermute | solution.py:66
  69.3 6.5 %collective-permute-start.25 = (f32[448,128]{1,0:T(8,128)S(1)}, f32[448,128]{1,0:T(8,128)S(1)}, u32[]{:S(2)}, u32[]{:S(2)}) collective-permute-start(f32[448,128]{1,0:T(8,128)S(1)} %combine.20.refs_4_), channel_id=1, source_target_pairs={{0,2},{1,5},{2,0},{3,7},{4,6},{5,1},{6,4},{7,3},{8,10},{9,13},{10,... | collective-permute-start | bytes 688136 | tf_op jit(solution)/shard_map/ppermute | solution.py:66
  75.9 8.8 %collective-permute-start.26 = (f32[144,128]{1,0:T(8,128)S(1)}, f32[144,128]{1,0:T(8,128)S(1)}, u32[]{:S(2)}, u32[]{:S(2)}) collective-permute-start(f32[144,128]{1,0:T(8,128)S(1)} %get-tuple-element.72), channel_id=1, source_target_pairs={{0,24},{1,25},{2,26},{3,27},{4,28},{5,29},{6,30},{7,31},{8,16},{9,... | collective-permute-start | bytes 221192 | tf_op jit(solution)/shard_map/ppermute | solution.py:66
  78.0 7.2 %collective-permute-start.27 = (f32[144,128]{1,0:T(8,128)S(1)}, f32[144,128]{1,0:T(8,128)S(1)}, u32[]{:S(2)}, u32[]{:S(2)}) collective-permute-start(f32[144,128]{1,0:T(8,128)S(1)} %get-tuple-element.73), channel_id=1, source_target_pairs={{0,16},{1,17},{2,18},{3,19},{4,20},{5,21},{6,22},{7,23},{8,24},{9,... | collective-permute-start | bytes 221192 | tf_op jit(solution)/shard_map/ppermute | solution.py:66
  78.1 7.1 %collective-permute-start.28 = (f32[144,128]{1,0:T(8,128)S(1)}, f32[144,128]{1,0:T(8,128)S(1)}, u32[]{:S(2)}, u32[]{:S(2)}) collective-permute-start(f32[144,128]{1,0:T(8,128)S(1)} %get-tuple-element.74), channel_id=1, source_target_pairs={{0,8},{1,9},{2,10},{3,11},{4,12},{5,13},{6,14},{7,15},{8,0},{9,1},... | collective-permute-start | bytes 221192 | tf_op jit(solution)/shard_map/ppermute | solution.py:66
  85.2 6.0 %collective-permute-start.29 = (f32[144,128]{1,0:T(8,128)S(1)}, f32[144,128]{1,0:T(8,128)S(1)}, u32[]{:S(2)}, u32[]{:S(2)}) collective-permute-start(f32[144,128]{1,0:T(8,128)S(1)} %get-tuple-element.79.refs_0_), channel_id=1, source_target_pairs={{0,8},{1,9},{2,10},{3,11},{4,12},{5,13},{6,14},{7,15},{8,0},{9,1},... | collective-permute-start | bytes 221192 | tf_op jit(solution)/shard_map/ppermute | solution.py:66
  85.3 8.8 %collective-permute-start.30 = (f32[144,128]{1,0:T(8,128)S(1)}, f32[144,128]{1,0:T(8,128)S(1)}, u32[]{:S(2)}, u32[]{:S(2)}) collective-permute-start(f32[144,128]{1,0:T(8,128)S(1)} %get-tuple-element.79.refs_0_), channel_id=1, source_target_pairs={{0,16},{1,17},{2,18},{3,19},{4,20},{5,21},{6,22},{7,23},{8,24},{9,... | collective-permute-start | bytes 221192 | tf_op jit(solution)/shard_map/ppermute | solution.py:66
  87.9 6.2 %collective-permute-start.31 = (f32[144,128]{1,0:T(8,128)S(1)}, f32[144,128]{1,0:T(8,128)S(1)}, u32[]{:S(2)}, u32[]{:S(2)}) collective-permute-start(f32[144,128]{1,0:T(8,128)S(1)} %get-tuple-element.79.refs_0_), channel_id=1, source_target_pairs={{0,24},{1,25},{2,26},{3,27},{4,28},{5,29},{6,30},{7,31},{8,16},{9,... | collective-permute-start | bytes 221192 | tf_op jit(solution)/shard_map/ppermute | solution.py:66
  89.7 6.0 %collective-permute-start.33 = (f32[128,128]{1,0:T(8,128)S(1)}, f32[128,128]{1,0:T(8,128)S(1)}, u32[]{:S(2)}, u32[]{:S(2)}) collective-permute-start(f32[128,128]{1,0:T(8,128)S(1)} %get-tuple-element.81.refs_0_), channel_id=1, source_target_pairs={{0,4},{1,5},{2,6},{3,7},{4,0},{5,1},{6,2},{7,3},{8,12},{9,13},{10,... | collective-permute-start | bytes 196616 | tf_op jit(solution)/shard_map/ppermute | solution.py:66
  94.1 7.8 %collective-permute-start.34 = (f32[384,128]{1,0:T(8,128)S(1)}, f32[384,128]{1,0:T(8,128)S(1)}, u32[]{:S(2)}, u32[]{:S(2)}) collective-permute-start(f32[384,128]{1,0:T(8,128)S(1)} %get-tuple-element.85.refs_2_), channel_id=1, source_target_pairs={{0,4},{1,5},{2,6},{3,7},{4,0},{5,1},{6,2},{7,3},{8,12},{9,13},{10,... | collective-permute-start | bytes 589832 | tf_op jit(solution)/shard_map/ppermute | solution.py:66
  (12 other events, 52.9 us)
